TPU v7x, 32 devices: a whole 2x2x4 slice. The times are simulated.
32 devices in a mesh: dp: 8 (over z, x), tensor: 4 (over y, core).
Axes of the slice: x: 2, y: 2, z: 4, core: 2. Of those that a mesh axis runs over, the one named last changes fastest.
Arguments:
- tokens: bfloat16 [16384, 1024], P(('dp', 'tensor')), may hold values from -6 to 6
- mix_gain: bfloat16 [1024], P('dp'), may hold values from 0.5 to 1.5
- rnn_weight: bfloat16 [1024, 1536], P('dp', 'tensor'), may hold values from -0.1875 to 0.1875
- gelu_weight: bfloat16 [1024, 1536], P('dp', 'tensor'), may hold values from -0.1875 to 0.1875
- conv_weight: bfloat16 [4, 1536], P(None, ('tensor', 'dp')), may hold values from -3 to 3
- conv_bias: bfloat16 [1536], P(('tensor', 'dp')), may hold values from -1.5 to 1.5
- recur_weight: bfloat16 [12, 128, 128], P('tensor', 'dp'), may hold values from -0.5 to 0.5
- input_weight: bfloat16 [12, 128, 128], P('tensor', 'dp'), may hold values from -0.5 to 0.5
- recur_bias: bfloat16 [1536], P(('tensor', 'dp')), may hold values from -2.5 to 2.5
- input_bias: bfloat16 [1536], P(('tensor', 'dp')), may hold values from -2.5 to 2.5
- decay_param: bfloat16 [1536], P(('tensor', 'dp')), may hold values from -9 to 0
- out_weight: bfloat16 [1536, 1024], P('tensor', 'dp'), may hold values from -0.15625 to 0.15625
- mlp_gain: bfloat16 [1024], P('dp'), may hold values from 0.5 to 1.5
- gate_weight: bfloat16 [1024, 3072], P('dp', 'tensor'), may hold values from -0.1875 to 0.1875
- up_weight: bfloat16 [1024, 3072], P('dp', 'tensor'), may hold values from -0.1875 to 0.1875
- down_weight: bfloat16 [3072, 1024], P('tensor', 'dp'), may hold values from -0.109375 to 0.109375
- cotangent: bfloat16 [16384, 1024], P(('dp', 'tensor')), may hold values from -6 to 6
Outputs:
- block_out: bfloat16 [16384, 1024], P(('dp', 'tensor'))
- grad_tokens: float32 [16384, 1024], P(('dp', 'tensor'))
- grad_mix_gain: float32 [1024], P('dp')
- grad_rnn_weight: float32 [1024, 1536], P('dp', 'tensor')
- grad_gelu_weight: float32 [1024, 1536], P('dp', 'tensor')
- grad_conv_weight: float32 [4, 1536], P(None, ('tensor', 'dp'))
- grad_conv_bias: float32 [1536], P(('tensor', 'dp'))
- grad_recur_weight: float32 [12, 128, 128], P('tensor', 'dp')
- grad_input_weight: float32 [12, 128, 128], P('tensor', 'dp')
- grad_recur_bias: float32 [1536], P(('tensor', 'dp'))
- grad_input_bias: float32 [1536], P(('tensor', 'dp'))
- grad_decay_param: float32 [1536], P(('tensor', 'dp'))
- grad_out_weight: float32 [1536, 1024], P('tensor', 'dp')
- grad_mlp_gain: float32 [1024], P('dp')
- grad_gate_weight: float32 [1024, 3072], P('dp', 'tensor')
- grad_up_weight: float32 [1024, 3072], P('dp', 'tensor')
- grad_down_weight: float32 [3072, 1024], P('tensor', 'dp')
All inputs are finite; a program needn't handle non-finite values.
Results may differ from a plain program's by a relative error of at most 0.012.
Values may be sent and summed in bfloat16 or wider, within the bound.
A program may use at most 192 MiB of HBM per device.

v0:
```python
import jax
import jax.numpy as jnp
from jax import lax
from jax.sharding import PartitionSpec as P

SEQ_LEN = 1024


EPS = 1e-06
GUARD = 0.01
DECAY_SCALE = 8.0


def rms_scale(values, gain):
    return values * lax.rsqrt(jnp.mean(values * values, axis=-1, keepdims=True) + EPS) * gain


def causal_conv(signal, weight, bias):
    width = weight.shape[0]
    length = signal.shape[1]
    padded = jnp.pad(signal, ((0, 0), (width - 1, 0), (0, 0)))
    total = jnp.zeros_like(signal) + bias
    for offset in range(width):
        total = total + weight[offset] * padded[:, width - 1 - offset : width - 1 - offset + length]
    return total


def combine(earlier, later):
    return (earlier[0] * later[0], later[0] * earlier[1] + later[1])


def lru_mix(recur_lin, input_lin, conv_out, branch_lin, decay_param, recur_bias, input_bias):
    recur = jax.nn.sigmoid(recur_lin + recur_bias)
    inward = jax.nn.sigmoid(input_lin + input_bias)
    decay = jnp.exp(-DECAY_SCALE * jax.nn.softplus(decay_param) * recur)
    driven = jnp.sqrt(1.0 - decay * decay + GUARD) * inward * conv_out
    decays_out, state = lax.associative_scan(combine, (decay, driven), axis=1)
    return state * jax.nn.gelu(branch_lin, approximate=True)


def gelu_product(gate_lin, up_lin):
    return jax.nn.gelu(gate_lin, approximate=True) * up_lin


def times_transposed(left, right):
    return lax.dot_general(
        left, right, (((1,), (1,)), ((), ())), preferred_element_type=jnp.float32
    )


def transposed_times(left, right):
    return lax.dot_general(
        left, right, (((0,), (0,)), ((), ())), preferred_element_type=jnp.float32
    )


def body(
    tokens,
    mix_gain,
    rnn_weight,
    gelu_weight,
    conv_weight,
    conv_bias,
    recur_weight,
    input_weight,
    recur_bias,
    input_bias,
    decay_param,
    out_weight,
    mlp_gain,
    gate_weight,
    up_weight,
    down_weight,
    cotangent,
):
    fullw = (
        lax.all_gather(mix_gain, "dp", axis=0, tiled=True),
        lax.all_gather(rnn_weight, "dp", axis=0, tiled=True),
        lax.all_gather(gelu_weight, "dp", axis=0, tiled=True),
        lax.all_gather(conv_weight, "dp", axis=1, tiled=True),
        lax.all_gather(conv_bias, "dp", axis=0, tiled=True),
        lax.all_gather(recur_weight, "dp", axis=1, tiled=True),
        lax.all_gather(input_weight, "dp", axis=1, tiled=True),
        lax.all_gather(recur_bias, "dp", axis=0, tiled=True),
        lax.all_gather(input_bias, "dp", axis=0, tiled=True),
        lax.all_gather(decay_param, "dp", axis=0, tiled=True),
        lax.all_gather(out_weight, "dp", axis=1, tiled=True),
        lax.all_gather(mlp_gain, "dp", axis=0, tiled=True),
        lax.all_gather(gate_weight, "dp", axis=0, tiled=True),
        lax.all_gather(up_weight, "dp", axis=0, tiled=True),
        lax.all_gather(down_weight, "dp", axis=1, tiled=True),
    )
    (
        gain_one,
        rnn_w,
        gelu_w,
        conv_w,
        conv_b,
        recur_w,
        input_w,
        recur_b,
        input_b,
        decay_p,
        out_w,
        gain_two,
        gate_w,
        up_w,
        down_w,
    ) = fullw
    gain_one = gain_one.astype(jnp.float32)
    gain_two = gain_two.astype(jnp.float32)
    conv_wf = conv_w.astype(jnp.float32)
    conv_bf = conv_b.astype(jnp.float32)
    recur_bf = recur_b.astype(jnp.float32)
    input_bf = input_b.astype(jnp.float32)
    decay_pf = decay_p.astype(jnp.float32)
    channels = rnn_w.shape[1]
    heads_local = recur_w.shape[0]
    block = recur_w.shape[2]
    resid = tokens.astype(jnp.float32)
    normed_one = rms_scale(resid, gain_one).astype(jnp.bfloat16)
    rows_one = lax.all_gather(normed_one, "tensor", axis=0, tiled=True)
    group_rows = rows_one.shape[0]
    seqs = group_rows // SEQ_LEN
    rnn_in = jnp.dot(rows_one, rnn_w, preferred_element_type=jnp.float32).reshape(
        seqs, SEQ_LEN, channels
    )
    branch_in = jnp.dot(rows_one, gelu_w, preferred_element_type=jnp.float32).reshape(
        seqs, SEQ_LEN, channels
    )
    conv_low = causal_conv(rnn_in, conv_wf, conv_bf).astype(jnp.bfloat16)
    conv_heads = conv_low.reshape(group_rows, heads_local, block)
    recur_in = jnp.einsum(
        "gkc,kcd->gkd", conv_heads, recur_w, preferred_element_type=jnp.float32
    ).reshape(seqs, SEQ_LEN, channels)
    input_in = jnp.einsum(
        "gkc,kcd->gkd", conv_heads, input_w, preferred_element_type=jnp.float32
    ).reshape(seqs, SEQ_LEN, channels)
    conv_float = conv_low.astype(jnp.float32)
    lru_value, lru_back = jax.vjp(
        lru_mix, recur_in, input_in, conv_float, branch_in, decay_pf, recur_bf, input_bf
    )
    lru_low = lru_value.astype(jnp.bfloat16).reshape(group_rows, channels)
    piece = lru_low
    mixed = resid + lax.psum_scatter(
        jnp.dot(piece, out_w, preferred_element_type=jnp.float32),
        "tensor",
        scatter_dimension=0,
        tiled=True,
    )
    normed_two = rms_scale(mixed, gain_two).astype(jnp.bfloat16)
    rows_two = lax.all_gather(normed_two, "tensor", axis=0, tiled=True)
    gate_in = jnp.dot(rows_two, gate_w, preferred_element_type=jnp.float32)
    up_in = jnp.dot(rows_two, up_w, preferred_element_type=jnp.float32)
    hidden_value, hidden_back = jax.vjp(gelu_product, gate_in, up_in)
    hidden_low = hidden_value.astype(jnp.bfloat16)
    piece = hidden_low
    block_out = (
        mixed
        + lax.psum_scatter(
            jnp.dot(piece, down_w, preferred_element_type=jnp.float32),
            "tensor",
            scatter_dimension=0,
            tiled=True,
        )
    ).astype(jnp.bfloat16)
    backw = (
        lax.all_gather(mix_gain, "dp", axis=0, tiled=True),
        lax.all_gather(rnn_weight, "dp", axis=0, tiled=True),
        lax.all_gather(gelu_weight, "dp", axis=0, tiled=True),
        lax.all_gather(conv_weight, "dp", axis=1, tiled=True),
        lax.all_gather(conv_bias, "dp", axis=0, tiled=True),
        lax.all_gather(recur_weight, "dp", axis=1, tiled=True),
        lax.all_gather(input_weight, "dp", axis=1, tiled=True),
        lax.all_gather(recur_bias, "dp", axis=0, tiled=True),
        lax.all_gather(input_bias, "dp", axis=0, tiled=True),
        lax.all_gather(decay_param, "dp", axis=0, tiled=True),
        lax.all_gather(out_weight, "dp", axis=1, tiled=True),
        lax.all_gather(mlp_gain, "dp", axis=0, tiled=True),
        lax.all_gather(gate_weight, "dp", axis=0, tiled=True),
        lax.all_gather(up_weight, "dp", axis=0, tiled=True),
        lax.all_gather(down_weight, "dp", axis=1, tiled=True),
    )
    rnn_w, gelu_w, conv_w, recur_w, input_w, out_w = (
        backw[1],
        backw[2],
        backw[3],
        backw[5],
        backw[6],
        backw[10],
    )
    gate_w, up_w, down_w = (backw[12], backw[13], backw[14])
    conv_wf = conv_w.astype(jnp.float32)
    cot_rows = lax.all_gather(cotangent, "tensor", axis=0, tiled=True)
    grad_hidden = times_transposed(cot_rows, down_w)
    grad_down = transposed_times(hidden_low, cot_rows)
    grad_gate_f, grad_up_f = hidden_back(grad_hidden)
    grad_gate_low = grad_gate_f.astype(jnp.bfloat16)
    grad_up_low = grad_up_f.astype(jnp.bfloat16)
    grad_gate_w = transposed_times(rows_two, grad_gate_low)
    grad_up_w = transposed_times(rows_two, grad_up_low)
    grad_normed_two = lax.psum_scatter(
        times_transposed(grad_gate_low, gate_w) + times_transposed(grad_up_low, up_w),
        "tensor",
        scatter_dimension=0,
        tiled=True,
    )
    norm_two_value, norm_two_back = jax.vjp(rms_scale, mixed, gain_two)
    grad_mixed_norm, grad_gain_two = norm_two_back(grad_normed_two)
    grad_mixed = cotangent.astype(jnp.float32) + grad_mixed_norm
    grad_branch_rows = lax.all_gather(grad_mixed.astype(jnp.bfloat16), "tensor", axis=0, tiled=True)
    grad_lru = times_transposed(grad_branch_rows, out_w)
    grad_out_w = transposed_times(lru_low, grad_branch_rows)
    (
        grad_recur_f,
        grad_input_f,
        grad_conv_direct,
        grad_branch_f,
        grad_decay_p,
        grad_recur_b,
        grad_input_b,
    ) = lru_back(grad_lru.reshape(seqs, SEQ_LEN, channels))
    grad_recur_low = grad_recur_f.astype(jnp.bfloat16).reshape(group_rows, heads_local, block)
    grad_input_low = grad_input_f.astype(jnp.bfloat16).reshape(group_rows, heads_local, block)
    grad_branch_low = grad_branch_f.astype(jnp.bfloat16).reshape(group_rows, channels)
    grad_recur_w = jnp.einsum(
        "gkc,gkd->kcd", conv_heads, grad_recur_low, preferred_element_type=jnp.float32
    )
    grad_input_w = jnp.einsum(
        "gkc,gkd->kcd", conv_heads, grad_input_low, preferred_element_type=jnp.float32
    )
    grad_conv_out = grad_conv_direct + (
        jnp.einsum("gkd,kcd->gkc", grad_recur_low, recur_w, preferred_element_type=jnp.float32)
        + jnp.einsum("gkd,kcd->gkc", grad_input_low, input_w, preferred_element_type=jnp.float32)
    ).reshape(seqs, SEQ_LEN, channels)
    conv_value, conv_back = jax.vjp(causal_conv, rnn_in, conv_wf, conv_bf)
    grad_rnn_f, grad_conv_w, grad_conv_b = conv_back(grad_conv_out)
    grad_rnn_low = grad_rnn_f.astype(jnp.bfloat16).reshape(group_rows, channels)
    grad_rnn_w = transposed_times(rows_one, grad_rnn_low)
    grad_gelu_w = transposed_times(rows_one, grad_branch_low)
    grad_normed_one = lax.psum_scatter(
        times_transposed(grad_rnn_low, rnn_w) + times_transposed(grad_branch_low, gelu_w),
        "tensor",
        scatter_dimension=0,
        tiled=True,
    )
    norm_one_value, norm_one_back = jax.vjp(rms_scale, resid, gain_one)
    grad_resid_norm, grad_gain_one = norm_one_back(grad_normed_one)
    grad_tokens = grad_mixed + grad_resid_norm
    summed = (
        lax.psum_scatter(grad_gain_one, "dp", scatter_dimension=0, tiled=True),
        lax.psum_scatter(grad_rnn_w, "dp", scatter_dimension=0, tiled=True),
        lax.psum_scatter(grad_gelu_w, "dp", scatter_dimension=0, tiled=True),
        lax.psum_scatter(grad_conv_w, "dp", scatter_dimension=1, tiled=True),
        lax.psum_scatter(grad_conv_b, "dp", scatter_dimension=0, tiled=True),
        lax.psum_scatter(grad_recur_w, "dp", scatter_dimension=1, tiled=True),
        lax.psum_scatter(grad_input_w, "dp", scatter_dimension=1, tiled=True),
        lax.psum_scatter(grad_recur_b, "dp", scatter_dimension=0, tiled=True),
        lax.psum_scatter(grad_input_b, "dp", scatter_dimension=0, tiled=True),
        lax.psum_scatter(grad_decay_p, "dp", scatter_dimension=0, tiled=True),
        lax.psum_scatter(grad_out_w, "dp", scatter_dimension=1, tiled=True),
        lax.psum_scatter(grad_gain_two, "dp", scatter_dimension=0, tiled=True),
        lax.psum_scatter(grad_gate_w, "dp", scatter_dimension=0, tiled=True),
        lax.psum_scatter(grad_up_w, "dp", scatter_dimension=0, tiled=True),
        lax.psum_scatter(grad_down, "dp", scatter_dimension=1, tiled=True),
    )
    gain_one_sum, gain_two_sum = lax.psum((summed[0], summed[11]), "tensor")
    return (
        block_out,
        grad_tokens,
        gain_one_sum,
        summed[1],
        summed[2],
        summed[3],
        summed[4],
        summed[5],
        summed[6],
        summed[7],
        summed[8],
        summed[9],
        summed[10],
        gain_two_sum,
        summed[12],
        summed[13],
        summed[14],
    )


def solution(mesh):
    placed = (
        P(("dp", "tensor"), None),
        P("dp"),
        P("dp", "tensor"),
        P("dp", "tensor"),
        P(None, ("tensor", "dp")),
        P(("tensor", "dp")),
        P("tensor", "dp", None),
        P("tensor", "dp", None),
        P(("tensor", "dp")),
        P(("tensor", "dp")),
        P(("tensor", "dp")),
        P("tensor", "dp"),
        P("dp"),
        P("dp", "tensor"),
        P("dp", "tensor"),
        P("tensor", "dp"),
        P(("dp", "tensor"), None),
    )
    return jax.shard_map(
        body,
        mesh=mesh,
        in_specs=placed,
        out_specs=(
            P(("dp", "tensor"), None),
            P(("dp", "tensor"), None),
            P("dp"),
            P("dp", "tensor"),
            P("dp", "tensor"),
            P(None, ("tensor", "dp")),
            P(("tensor", "dp")),
            P("tensor", "dp", None),
            P("tensor", "dp", None),
            P(("tensor", "dp")),
            P(("tensor", "dp")),
            P(("tensor", "dp")),
            P("tensor", "dp"),
            P("dp"),
            P("dp", "tensor"),
            P("dp", "tensor"),
            P("tensor", "dp"),
        ),
        check_vma=False,
    )
```

profile of v0, /device:TPU:0, one launch (start us, length us, event | category | flops | bytes accessed | tf_op | source)
XLA Modules:
  0.0 1895.5 jit_solution(12186649363546396477)
XLA Ops:
  8.2 22.4 %all-gather.1 = bf16[8,1,128]{2,1,0:T(2,128)(2,1)S(1)} all-gather(bf16[1,1,128]{2,1,0:T(2,128)(2,1)} %bitcast.123), channel_id=1, replica_groups=mesh['dp'=8,'tensor'=4] {'dp'}, dimensions={0}, use_global_device_ids=true | all-gather | bytes 2304 | tf_op jit(solution)/shard_map/all_gather | solution.py:77
  73.8 30.6 %all_gather.72 = bf16[3,128,128]{2,1,0:T(8,128)(2,1)S(1)} all-gather(bf16[3,16,128]{2,1,0:T(8,128)(2,1)S(1)} %copy-done.166), channel_id=1, replica_groups=mesh['dp'=8,'tensor'=4] {'dp'}, dimensions={1}, use_global_device_ids=true | all-gather | bytes 110592 | tf_op jit(solution)/shard_map/all_gather | solution.py:82
  104.3 30.5 %all_gather.74 = bf16[3,128,128]{2,1,0:T(8,128)(2,1)S(1)} all-gather(bf16[3,16,128]{2,1,0:T(8,128)(2,1)S(1)} %copy-done.167), channel_id=1, replica_groups=mesh['dp'=8,'tensor'=4] {'dp'}, dimensions={1}, use_global_device_ids=true | all-gather | bytes 110592 | tf_op jit(solution)/shard_map/all_gather | solution.py:83
  135.0 34.2 %all_gather.71 = bf16[1024,384]{1,0:T(8,128)(2,1)} all-gather(bf16[128,384]{1,0:T(8,128)(2,1)S(1)} %copy-done.115), channel_id=1, replica_groups=mesh['dp'=8,'tensor'=4] {'dp'}, dimensions={0}, use_global_device_ids=true | all-gather | bytes 884736 | tf_op jit(solution)/shard_map/all_gather | solution.py:78
  169.2 34.0 %all_gather.76 = bf16[1024,384]{1,0:T(8,128)(2,1)} all-gather(bf16[128,384]{1,0:T(8,128)(2,1)S(1)} %copy-done.116), channel_id=1, replica_groups=mesh['dp'=8,'tensor'=4] {'dp'}, dimensions={0}, use_global_device_ids=true | all-gather | bytes 884736 | tf_op jit(solution)/shard_map/all_gather | solution.py:79
  203.2 28.7 %all_gather.77 = bf16[384,1024]{1,0:T(8,128)(2,1)} all-gather(bf16[384,128]{1,0:T(8,128)(2,1)S(1)} %copy-done.117), channel_id=1, replica_groups=mesh['dp'=8,'tensor'=4] {'dp'}, dimensions={1}, use_global_device_ids=true | all-gather | bytes 884736 | tf_op jit(solution)/shard_map/all_gather | solution.py:87
  517.4 53.2 %reduce-scatter.16.cloned.1.call-done = f32[512,1024]{1,0:T(8,128)} async-done(((f32[2048,1024]{1,0:T(8,128)}), f32[512,1024]{1,0:T(8,128)}) %reduce-scatter.16.cloned.1.call-update) | async-done | bytes 2097168 | tf_op jit(solution)/shard_map/reduce_scatter | solution.py:145
  576.5 32.3 %all-gather.13.cloned.1.call-done = bf16[2048,1024]{1,0:T(8,128)(2,1)} async-done(((bf16[512,1024]{1,0:T(8,128)(2,1)}), bf16[2048,1024]{1,0:T(8,128)(2,1)}) %all-gather.13.cloned.1.call-update) | async-done | bytes 4194320 | tf_op jit(solution)/shard_map/all_gather | solution.py:152
  617.5 37.8 %all-gather.17.cloned.1.call-done = bf16[1024,768]{1,0:T(8,128)(2,1)} async-done(((bf16[128,768]{1,0:T(8,128)(2,1)}), bf16[1024,768]{1,0:T(8,128)(2,1)}) %all-gather.17.cloned.1.call-update) | async-done | bytes 1572880 | tf_op jit(solution)/shard_map/all_gather | solution.py:90
  664.2 36.3 %all-gather.19.cloned.1.call-done = bf16[768,1024]{1,0:T(8,128)(2,1)} async-done(((bf16[768,128]{1,0:T(8,128)(2,1)}), bf16[768,1024]{1,0:T(8,128)(2,1)}) %all-gather.19.cloned.1.call-update) | async-done | bytes 1572880 | tf_op jit(solution)/shard_map/all_gather | solution.py:91
  700.5 34.2 %all-gather.21.cloned.1.call-done = bf16[2048,1024]{1,0:T(8,128)(2,1)} async-done(((bf16[512,1024]{1,0:T(8,128)(2,1)}), bf16[2048,1024]{1,0:T(8,128)(2,1)}) %all-gather.21.cloned.1.call-update) | async-done | bytes 4194320 | tf_op jit(solution)/shard_map/all_gather | solution.py:194
  758.2 71.7 %reduce-scatter.20.cloned.1.call-done = f32[512,1024]{1,0:T(8,128)} async-done(((f32[2048,1024]{1,0:T(8,128)}), f32[512,1024]{1,0:T(8,128)}) %reduce-scatter.20.cloned.1.call-update) | async-done | bytes 2097168 | tf_op jit(solution)/shard_map/reduce_scatter | solution.py:202
  835.1 34.6 %all-gather.23.cloned.1.call-done = bf16[2048,1024]{1,0:T(8,128)(2,1)} async-done(((bf16[512,1024]{1,0:T(8,128)(2,1)}), bf16[2048,1024]{1,0:T(8,128)(2,1)}) %all-gather.23.cloned.1.call-update) | async-done | bytes 4194320 | tf_op jit(solution)/shard_map/all_gather | solution.py:211
  1185.9 61.4 %reduce-scatter.22.cloned.1.call-done = f32[512,1024]{1,0:T(8,128)} async-done(((f32[2048,1024]{1,0:T(8,128)}), f32[512,1024]{1,0:T(8,128)}) %reduce-scatter.22.cloned.1.call-update) | async-done | bytes 2097168 | tf_op jit(solution)/shard_map/reduce_scatter | solution.py:241
  1249.6 37.1 %all-reduce.114 = (f32[1024]{0:T(1024)S(1)}, f32[384]{0:T(512)S(1)}, f32[384]{0:T(512)S(1)}, f32[384]{0:T(512)S(1)}, f32[384]{0:T(512)S(1)}, /*index=5*/f32[1024]{0:T(1024)S(1)}) all-reduce(f32[1024]{0:T(1024)S(1)} %get-tuple-element.29, f32[384]{0:T(512)S(1)} %get-tuple-element.24, ...), channel_id=6, replica_groups=mesh['dp'=8,'tensor'=4] {'dp'}, use_global_device_ids=true, to_apply=%region_9.10.clone | all-reduce | flops 3584 | bytes 28672
  1295.9 25.8 %reduce-scatter.18.cloned.1.call-done = f32[512,1024]{1,0:T(8,128)} async-done(((f32[2048,1024]{1,0:T(8,128)}), f32[512,1024]{1,0:T(8,128)}) %reduce-scatter.18.cloned.1.call-update) | async-done | bytes 2097168 | tf_op jit(solution)/shard_map/reduce_scatter | solution.py:160
  1326.6 73.3 %reduce-scatter.34.cloned.1.call-done = f32[128,768]{1,0:T(8,128)} async-done(((f32[1024,768]{1,0:T(8,128)}), f32[128,768]{1,0:T(8,128)}) %reduce-scatter.34.cloned.1.call-update) | async-done | bytes 393232 | tf_op jit(solution)/shard_map/reduce_scatter | solution.py:263
  1399.9 77.0 %reduce-scatter.36.cloned.1.call-done = f32[128,768]{1,0:T(8,128)} async-done(((f32[1024,768]{1,0:T(8,128)}), f32[128,768]{1,0:T(8,128)}) %reduce-scatter.36.cloned.1.call-update) | async-done | bytes 393232 | tf_op jit(solution)/shard_map/reduce_scatter | solution.py:264
  1476.8 77.6 %reduce-scatter.38.cloned.1.call-done = f32[768,128]{1,0:T(8,128)} async-done(((f32[768,1024]{1,0:T(8,128)}), f32[768,128]{1,0:T(8,128)}) %reduce-scatter.38.cloned.1.call-update) | async-done | bytes 393232 | tf_op jit(solution)/shard_map/reduce_scatter | solution.py:265
  1554.5 64.1 %reduce-scatter.28.cloned.1.call-done = f32[3,16,128]{2,1,0:T(8,128)} async-done(((f32[3,128,128]{2,1,0:T(8,128)}), f32[3,16,128]{2,1,0:T(8,128)}) %reduce-scatter.28.cloned.1.call-update) | async-done | bytes 24592 | tf_op jit(solution)/shard_map/reduce_scatter | solution.py:256
  1618.6 64.3 %reduce-scatter.30.cloned.1.call-done = f32[3,16,128]{2,1,0:T(8,128)} async-done(((f32[3,128,128]{2,1,0:T(8,128)}), f32[3,16,128]{2,1,0:T(8,128)}) %reduce-scatter.30.cloned.1.call-update) | async-done | bytes 24592 | tf_op jit(solution)/shard_map/reduce_scatter | solution.py:257
  1682.9 68.0 %reduce-scatter.24.cloned.1.call-done = f32[128,384]{1,0:T(8,128)} async-done(((f32[1024,384]{1,0:T(8,128)}), f32[128,384]{1,0:T(8,128)}) %reduce-scatter.24.cloned.1.call-update) | async-done | bytes 196624 | tf_op jit(solution)/shard_map/reduce_scatter | solution.py:252
  1750.9 68.3 %reduce-scatter.26.cloned.1.call-done = f32[128,384]{1,0:T(8,128)} async-done(((f32[1024,384]{1,0:T(8,128)}), f32[128,384]{1,0:T(8,128)}) %reduce-scatter.26.cloned.1.call-update) | async-done | bytes 196624 | tf_op jit(solution)/shard_map/reduce_scatter | solution.py:253
  1819.3 68.5 %reduce-scatter.32.cloned.1.call-done = f32[384,128]{1,0:T(8,128)} async-done(((f32[384,1024]{1,0:T(8,128)}), f32[384,128]{1,0:T(8,128)}) %reduce-scatter.32.cloned.1.call-update) | async-done | bytes 196624 | tf_op jit(solution)/shard_map/reduce_scatter | solution.py:261
  (750 shorter events, 708.4 us)
Async XLA Ops:
  8.1 223.8 %all-gather.11.cloned.1.call-start = ((), (), s32[]{:S(2)}) async-start(), calls=%async_computation.13 | async-start | bytes 5242880 | tf_op jit(solution)/shard_map/all_gather | solution.py:122
  35.9 534.7 %reduce-scatter.16.cloned.1.call-start = ((), (), s32[]{:S(2)}) async-start(), calls=%async_computation.14 | async-start | bytes 10485760 | tf_op jit(solution)/shard_map/reduce_scatter | solution.py:145
  73.7 211.0 %copy-start.133 = (f32[384]{0:T(512)}, f32[384]{0:T(512)S(1)}, u32[]{:S(2)}) copy-start(f32[384]{0:T(512)S(1)} %convert_element_type.74) | copy-start | bytes 4612
  73.7 211.0 %copy-start.145 = (f32[384]{0:T(512)}, f32[384]{0:T(512)S(1)}, u32[]{:S(2)}) copy-start(f32[384]{0:T(512)S(1)} %convert_element_type.79) | copy-start | bytes 4612
  500.6 75.9 %all-gather.15.cloned.1.call-start = ((), (), s32[]{:S(2)}) async-start(), calls=%async_computation.16 | async-start | bytes 1769472 | tf_op jit(solution)/shard_map/all_gather | solution.py:89
  501.2 107.6 %all-gather.13.cloned.1.call-start = ((), (), s32[]{:S(2)}) async-start(), calls=%async_computation.15 | async-start | bytes 5242880 | tf_op jit(solution)/shard_map/all_gather | solution.py:152
  517.4 315.4 %copy-start.113 = (f32[8,1,128]{2,1,0:T(1,128)}, f32[8,1,128]{2,1,0:T(1,128)S(1)}, u32[]{:S(2)}) copy-start(f32[8,1,128]{2,1,0:T(1,128)S(1)} %convert_element_type.96) | copy-start | bytes 12292
  572.6 260.3 %copy-start.5 = (f32[512,1024]{1,0:T(8,128)}, f32[512,1024]{1,0:T(8,128)S(1)}, u32[]{:S(2)}) copy-start(f32[512,1024]{1,0:T(8,128)S(1)} %get-tuple-element.71) | copy-start | bytes 6291460
  574.4 81.0 %all-gather.17.cloned.1.call-start = ((), (), s32[]{:S(2)}) async-start(), calls=%async_computation.17 | async-start | bytes 1769472 | tf_op jit(solution)/shard_map/all_gather | solution.py:90
  575.0 125.6 %all-gather.19.cloned.1.call-start = ((), (), s32[]{:S(2)}) async-start(), calls=%async_computation.18 | async-start | bytes 1769472 | tf_op jit(solution)/shard_map/all_gather | solution.py:91
  575.7 159.0 %all-gather.21.cloned.1.call-start = ((), (), s32[]{:S(2)}) async-start(), calls=%async_computation.20 | async-start | bytes 5242880 | tf_op jit(solution)/shard_map/all_gather | solution.py:194
  576.5 253.5 %reduce-scatter.20.cloned.1.call-start = ((), (), s32[]{:S(2)}) async-start(), calls=%async_computation.21 | async-start | bytes 10485760 | tf_op jit(solution)/shard_map/reduce_scatter | solution.py:202
  758.2 111.5 %all-gather.23.cloned.1.call-start = ((), (), s32[]{:S(2)}) async-start(), calls=%async_computation.22 | async-start | bytes 5242880 | tf_op jit(solution)/shard_map/all_gather | solution.py:211
  835.0 349.4 %reduce-scatter.40.cloned.1.call-start = ((), (), s32[]{:S(2)}) async-start(), calls=%async_computation.32 | async-start | bytes 221184
  1112.8 134.4 %reduce-scatter.22.cloned.1.call-start = ((), (), s32[]{:S(2)}) async-start(), calls=%async_computation.23 | async-start | bytes 10485760 | tf_op jit(solution)/shard_map/reduce_scatter | solution.py:241
  1122.2 199.5 %reduce-scatter.18.cloned.1.call-start = ((), (), s32[]{:S(2)}) async-start(), calls=%async_computation.19 | async-start | bytes 10485760 | tf_op jit(solution)/shard_map/reduce_scatter | solution.py:160
  1131.2 268.7 %reduce-scatter.34.cloned.1.call-start = ((), (), s32[]{:S(2)}) async-start(), calls=%async_computation.29 | async-start | bytes 3538944 | tf_op jit(solution)/shard_map/reduce_scatter | solution.py:263
  1140.4 336.4 %reduce-scatter.36.cloned.1.call-start = ((), (), s32[]{:S(2)}) async-start(), calls=%async_computation.30 | async-start | bytes 3538944 | tf_op jit(solution)/shard_map/reduce_scatter | solution.py:264
  1149.7 404.8 %reduce-scatter.38.cloned.1.call-start = ((), (), s32[]{:S(2)}) async-start(), calls=%async_computation.31 | async-start | bytes 3538944 | tf_op jit(solution)/shard_map/reduce_scatter | solution.py:265
  1158.9 459.7 %reduce-scatter.28.cloned.1.call-start = ((), (), s32[]{:S(2)}) async-start(), calls=%async_computation.26 | async-start | bytes 221184 | tf_op jit(solution)/shard_map/reduce_scatter | solution.py:256
  1162.0 520.9 %reduce-scatter.30.cloned.1.call-start = ((), (), s32[]{:S(2)}) async-start(), calls=%async_computation.27 | async-start | bytes 221184 | tf_op jit(solution)/shard_map/reduce_scatter | solution.py:257
  1164.9 586.0 %reduce-scatter.24.cloned.1.call-start = ((), (), s32[]{:S(2)}) async-start(), calls=%async_computation.24 | async-start | bytes 1769472 | tf_op jit(solution)/shard_map/reduce_scatter | solution.py:252
  1170.9 648.4 %reduce-scatter.26.cloned.1.call-start = ((), (), s32[]{:S(2)}) async-start(), calls=%async_computation.25 | async-start | bytes 1769472 | tf_op jit(solution)/shard_map/reduce_scatter | solution.py:253
  1176.8 711.0 %reduce-scatter.32.cloned.1.call-start = ((), (), s32[]{:S(2)}) async-start(), calls=%async_computation.28 | async-start | bytes 1769472 | tf_op jit(solution)/shard_map/reduce_scatter | solution.py:261
  (183 other events, 4446.9 us)
Sparse Core Ops, SparseCore 0:
  36.0 31.7 all-gather.10
  500.7 69.8 reduce-scatter.15
  835.1 34.4 all-gather.22
Sparse Core Ops, SparseCore 1:
  503.3 42.3 all-gather.14
  574.5 34.3 all-gather.12
  611.1 44.2 all-gather.16
  657.6 42.9 all-gather.18
  702.2 32.5 all-gather.20
  758.2 71.6 reduce-scatter.19
  1112.9 61.2 reduce-scatter.39
  1176.6 70.6 reduce-scatter.21
  1249.9 71.7 reduce-scatter.17
  1325.9 73.9 reduce-scatter.33
  1403.9 72.9 reduce-scatter.35
  1481.0 73.4 reduce-scatter.37
  1558.2 60.4 reduce-scatter.27
  1622.5 60.4 reduce-scatter.29
  1686.9 63.9 reduce-scatter.23
  1755.3 63.9 reduce-scatter.25
  1823.3 64.4 reduce-scatter.31
where the time goes:
time: 1910 us; the launch traced here: 1900 us
  waiting for transfers between devices  951 us (50%)
  local copies, waits for them, and re-layouts  372 us (19%)
  blocking collectives  276 us (14%)
  matrix products  138 us (7%)
  other arithmetic  136 us (7%)
  between operations  21.2 us (1%)
    slice x78, local copies, waits for them, and re-layouts, lru_mix(): decays_out, state = lax.associative_scan(combine, (decay, driven), axis=1)  171 us
    pad x79, local copies, waits for them, and re-layouts, lru_mix(): decays_out, state = lax.associative_scan(combine, (decay, driven), axis=1)  99.1 us
    reduce_scatter x1, waiting for transfers between devices, body(): lax.psum_scatter(grad_down, 'dp', scatter_dimension=1, tiled=True)  77.6 us
    reduce_scatter x1, waiting for transfers between devices, body(): lax.psum_scatter(grad_up_w, 'dp', scatter_dimension=0, tiled=True)  77 us
    reduce_scatter x1, waiting for transfers between devices, body(): lax.psum_scatter(grad_gate_w, 'dp', scatter_dimension=0, tiled=True)  73.3 us
    reduce_scatter x1, waiting for transfers between devices, body(): lax.psum_scatter(times_transposed(grad_gate_low, gate_w) + times_transpos...  71.7 us
    reduce_scatter x1, waiting for transfers between devices, body(): lax.psum_scatter(grad_out_w, 'dp', scatter_dimension=1, tiled=True)  68.5 us
    reduce_scatter x1, waiting for transfers between devices, body(): lax.psum_scatter(grad_gelu_w, 'dp', scatter_dimension=0, tiled=True)  68.3 us
  transfers between devices with their start and end apart: 20, of which 17 were waited for; matrix products, arithmetic and copies ran while one was open for 5% of the time, Pallas kernels for 0%

commit v1 on v0

v1 whole, which is shorter than its diff:
```python
import functools

import jax
import jax.numpy as jnp
from jax import lax
from jax.experimental import pallas as pl
from jax.experimental.pallas import tpu as pltpu
from jax.sharding import PartitionSpec as P

SEQ = 1024
EPS = 1e-06
GUARD = 0.01
DECAY_SCALE = 8.0
GELU_K = 0.7978845608028654
GELU_C = 0.044715
BF = jnp.bfloat16
F32 = jnp.float32
MESH = pl.DeviceIdType.MESH
VMEM_LIMIT = 63 * 1024 * 1024

RNN, GEL, OUT, GA0, UP0, GA1, UP1, DN0, DN1 = range(9)
UNITS = 9
GATE, UP, DOWN = (GA0, GA1), (UP0, UP1), (DN0, DN1)
FLOW = {RNN: "zxy", GEL: "zyx", OUT: "yxz", GA0: "zxy", UP0: "zyx", GA1: "zxy", UP1: "zyx", DN0: "zxy", DN1: "zyx"}
SMALL = 48


def nn(a, b):
    return jnp.dot(a, b, preferred_element_type=F32)


def nt(a, b):
    return lax.dot_general(a, b, (((1,), (1,)), ((), ())), preferred_element_type=F32)


def gelu_parts(v):
    v2 = v * v
    th = jnp.tanh(GELU_K * v * (1.0 + GELU_C * v2))
    half = 0.5 * (1.0 + th)
    return v * half, half + (0.5 * GELU_K) * v * (1.0 - th * th) * (1.0 + (3.0 * GELU_C) * v2)


class Net:
    def __init__(self, z_size, x_size, y_size):
        self.size = {"z": z_size, "x": x_size, "y": y_size, "c": 2}
        dp, t = lax.axis_index("dp"), lax.axis_index("tensor")
        self.at = {"z": dp // x_size, "x": lax.rem(dp, x_size), "y": t // 2, "c": lax.rem(t, 2)}
        self.off = {"z": 0, "x": z_size - 1, "y": z_size + x_size - 2}

    def shifted(self, d, j):
        n = self.size[d]
        return lax.rem(self.at[d] + (j % n), n)

    def device(self, d, j):
        at = dict(self.at)
        at[d] = self.shifted(d, j)
        return (at["z"] * self.size["x"] + at["x"], at["y"] * 2 + at["c"])

    def barrier(self):
        sem = pltpu.get_barrier_semaphore()
        count = 0
        for d in "zxyc":
            for j in range(1, self.size[d]):
                pl.semaphore_signal(sem, inc=1, device_id=self.device(d, j), device_id_type=MESH)
                count += 1
        pl.semaphore_wait(sem, count)


class Gather:
    def __init__(self, net, ref, flows, ss, rs):
        self.net, self.ref, self.flows, self.ss, self.rs = net, ref, flows, ss, rs

    def region(self, u, s, at):
        order = self.flows[u]
        idx = [slice(None) if d in order[:s] else at[d] for d in "yzx"]
        return self.ref.at[(u, *idx)]

    def copy(self, u, s, j, sender):
        d = self.flows[u][s]
        at = dict(self.net.at)
        if sender:
            at[d] = self.net.shifted(d, -j)
        region = self.region(u, s, at)
        k = self.net.off[d] + j - 1
        return pltpu.make_async_remote_copy(
            src_ref=region, dst_ref=region, send_sem=self.ss.at[u, k], recv_sem=self.rs.at[u, k],
            device_id=self.net.device(d, j), device_id_type=MESH)

    def hops(self, u, s):
        return range(1, self.net.size[self.flows[u][s]])

    def start(self, u, s):
        for j in self.hops(u, s):
            self.copy(u, s, j, False).start()

    def wait(self, u, s):
        for j in self.hops(u, s):
            self.copy(u, s, j, True).wait_recv()

    def step(self, u, s):
        self.wait(u, s)
        if s < 2:
            self.start(u, s + 1)

    def drain(self, u):
        for s in range(3):
            for j in self.hops(u, s):
                self.copy(u, s, j, False).wait_send()


def pair_copy(net, src, dst, ss, rs, k):
    return pltpu.make_async_remote_copy(
        src_ref=src, dst_ref=dst, send_sem=ss.at[k], recv_sem=rs.at[k],
        device_id=net.device("c", 1), device_id_type=MESH)


def scan_forward(a, b, carry):
    rows, cols = a.shape
    a = a.reshape(rows // 8, 8, cols)
    b = b.reshape(rows // 8, 8, cols)
    place = lax.broadcasted_iota(jnp.int32, (rows // 8, 8, cols), 1)
    for k in (1, 2, 4):
        keep = place >= k
        b = b + a * jnp.where(keep, pltpu.roll(b, k, 1), 0.0)
        a = a * jnp.where(keep, pltpu.roll(a, k, 1), 1.0)
    out = []
    for g in range(rows // 8):
        s = b[g] + a[g] * carry
        out.append(s)
        carry = s[7:8]
    return jnp.concatenate(out, axis=0), carry


def scan_backward(a, b, carry):
    rows, cols = a.shape
    a = a.reshape(rows // 8, 8, cols)
    b = b.reshape(rows // 8, 8, cols)
    place = lax.broadcasted_iota(jnp.int32, (rows // 8, 8, cols), 1)
    for k in (1, 2, 4):
        keep = place < 8 - k
        b = b + a * jnp.where(keep, pltpu.roll(b, 8 - k, 1), 0.0)
        a = a * jnp.where(keep, pltpu.roll(a, 8 - k, 1), 1.0)
    out = []
    for g in reversed(range(rows // 8)):
        s = b[g] + a[g] * carry
        out.append(s)
        carry = s[0:1]
    return jnp.concatenate(out[::-1], axis=0), carry


def rows_of(i, n):
    return pl.ds(pl.multiple_of(i * n, n), n)


def join_params(gs, prm, gains, sizes):
    y_size = sizes[2]
    for yy in range(y_size):
        prm[yy] = jnp.sum(gs[0, yy, :, :, 32:48, :].astype(F32), axis=(0, 1))
    d = gains.shape[1]
    for n in range(2):
        row = jnp.concatenate([prm[0, 8 + 3 * n + k : 9 + 3 * n + k, :] for k in range(3)], axis=1)
        gains[n : n + 1, :] = row[:, :d]


def head_weight(gs, yy, first, group):
    blocks = gs[0, yy, :, :, first : first + 16, :]
    z, x, r, c = blocks.shape
    if group > 1:
        blocks = jnp.sum(blocks.astype(F32).reshape(z * x // group, group, r, c), axis=1).astype(BF)
    return blocks.reshape(-1, c)


def transpose_into(dst, src, n, step=256):
    @pl.loop(0, n // step)
    def _(i):
        dst[:, rows_of(i, step)] = src[rows_of(i, step), :].T


def forward_kernel(sizes, group,
                   tok, cot, wp, sp,
                   o_w, o_cot, o_cott, o_n1t, o_n2t, o_c6, o_cf, o_a, o_ri, o_lru, o_cv, o_mix, prm, gains, hw,
                   W, gs, T1, SA, SB, N1, RI, A, CV, C6, LRU, PS, PR, MIX,
                   ss, rs, sss, srs, ps, pr, ls, outs):
    net = Net(*sizes)
    y_size = sizes[2]
    c = net.at["c"]
    half = SEQ // 2
    ch = W.shape[-1]
    depth = T1.shape[1]
    own, other = pl.ds(pl.multiple_of(c * half, half), half), pl.ds(pl.multiple_of((1 - c) * half, half), half)
    mine = (net.at["y"], net.at["z"], net.at["x"])

    place = [
        pltpu.make_async_copy(sp, gs.at[(0, *mine)], ls.at[0]),
        pltpu.make_async_copy(wp, W.at[(slice(None), *mine)], ls.at[1]),
        pltpu.make_async_copy(tok, T1.at[own], ls.at[2]),
        pltpu.make_async_copy(cot, SA.at[own], ls.at[3]),
    ]
    for cp in place:
        cp.start()
    net.barrier()

    big = Gather(net, W, FLOW, ss, rs)
    small = Gather(net, gs, {0: "zxy"}, sss, srs)
    tok_copy = pair_copy(net, tok, T1.at[own], ps, pr, 0)
    cot_copy = pair_copy(net, cot, SA.at[own], ps, pr, 1)
    tok_in = pair_copy(net, tok, T1.at[other], ps, pr, 0)
    cot_in = pair_copy(net, cot, SA.at[other], ps, pr, 1)

    place[0].wait()
    small.start(0, 0)
    tok_copy.start()
    cot_copy.start()
    place[1].wait()
    big.start(RNN, 0)
    big.start(GEL, 0)
    big.start(OUT, 0)
    place[2].wait()
    place[3].wait()
    small.step(0, 0)
    small.step(0, 1)
    tok_in.wait_recv()
    cot_in.wait_recv()
    out_copies = []

    def send_out(src, dst):
        cp = pltpu.make_async_copy(src, dst, outs.at[len(out_copies)])
        cp.start()
        out_copies.append([cp, True])
        return len(out_copies) - 1

    def sent(k):
        if out_copies[k][1]:
            out_copies[k][0].wait()
            out_copies[k][1] = False

    k_cot = send_out(SA, o_cot)
    transpose_into(SB, SA, SEQ)
    k_cott = send_out(SB, o_cott)
    big.step(RNN, 0)
    small.wait(0, 2)
    join_params(gs, prm, gains, sizes)
    for yy in range(y_size):
        for n in range(2):
            hw[n, :, yy * ch : (yy + 1) * ch] = head_weight(gs, yy, 16 * n, group)
    big.start(GA0, 0)
    big.step(GEL, 0)

    @pl.loop(0, SEQ // 128)
    def _(i):
        v = T1[rows_of(i, 128), :].astype(F32)
        s = lax.rsqrt(jnp.mean(v * v, axis=1, keepdims=True) + EPS)
        N1[rows_of(i, 128), :] = (v * s * gains[0:1, :]).astype(BF)

    sent(k_cott)
    transpose_into(SB, N1, SEQ)
    k_n1t = send_out(SB, o_n1t)
    RI[0:8, :] = jnp.zeros((8, y_size * ch), F32)
    big.start(UP0, 0)
    big.step(RNN, 1)
    big.step(GEL, 1)
    big.step(OUT, 0)
    big.step(GA0, 0)
    big.wait(RNN, 2)

    def full(u):
        return jnp.concatenate([W[u, yy].reshape(depth, ch) for yy in range(y_size)], axis=1)

    w_out = {}

    def unit_out(u):
        w_out[u] = send_out(W.at[u], o_w.at[u])

    unit_out(RNN)

    @pl.loop(0, SEQ // 512)
    def _(i):
        RI[pl.ds(pl.multiple_of(i * 512 + 8, 8), 512), :] = nn(N1[rows_of(i, 512), :], full(RNN))

    send_out(RI, o_ri)
    big.start(GA1, 0)
    big.step(OUT, 1)
    big.step(UP0, 0)
    big.wait(GEL, 2)
    unit_out(GEL)

    T = 128

    def branch_tile(i, carries):
        hooks = {
            1: [lambda: big.step(GA0, 1)],
            2: [lambda: big.start(UP1, 0)],
            3: [lambda: big.step(UP0, 1), lambda: big.step(GA1, 0)],
            5: [lambda: big.wait(OUT, 2), lambda: big.start(DN0, 0)],
            6: [lambda: big.step(UP1, 0)],
        }
        for tile, fns in hooks.items():
            @pl.when(i == tile)
            def _():
                for fn in fns:
                    fn()
        rows = rows_of(i, T)
        br = nn(N1[rows, :], full(GEL))
        new = []
        for yy in range(y_size):
            cols = slice(yy * ch, (yy + 1) * ch)
            p = prm[yy]
            x = RI[pl.ds(pl.multiple_of(i * T, T), T + 8), cols]
            cv = p[4:5] + p[0:1] * x[8:]
            for k in range(1, 4):
                cv = cv + p[k : k + 1] * pltpu.roll(x, k, 0)[8:]
            cv_low = cv.astype(BF)
            CV[rows, cols] = cv_low
            cv = cv_low.astype(F32)
            rec, inp = [], []
            for h in range(ch // 128):
                hc = slice(yy * ch + h * 128, yy * ch + (h + 1) * 128)
                both = nn(cv_low[:, h * 128 : (h + 1) * 128], jnp.concatenate([hw[0, :, hc], hw[1, :, hc]], axis=1))
                rec.append(both[:, :128])
                inp.append(both[:, 128:])
            r = jax.nn.sigmoid(jnp.concatenate(rec, axis=1) + p[5:6])
            w = jax.nn.sigmoid(jnp.concatenate(inp, axis=1) + p[6:7])
            soft = jnp.log1p(jnp.exp(-jnp.abs(p[7:8]))) + jnp.maximum(p[7:8], 0.0)
            a = jnp.exp((-DECAY_SCALE * soft) * r)
            u = 1.0 - a * a + GUARD
            inv = lax.rsqrt(u)
            root = u * inv
            wc = w * cv
            state, last = scan_forward(a, root * wc, carries[yy])
            first = lax.broadcasted_iota(jnp.int32, (T, ch), 0) == 0
            prev = jnp.where(first, carries[yy], pltpu.roll(state, 1, 0))
            new.append(last)
            g, gp = gelu_parts(br[:, cols])
            LRU[rows, cols] = (state * g).astype(BF)
            cp = (prev - a * wc * inv) * a * r * (-DECAY_SCALE)
            A[rows, cols] = a
            C6[0, rows, cols] = g.astype(BF)
            C6[1, rows, cols] = (state * gp).astype(BF)
            C6[2, rows, cols] = cp.astype(BF)
            C6[3, rows, cols] = (cp * soft * (1.0 - r)).astype(BF)
            C6[4, rows, cols] = (root * wc * (1.0 - w)).astype(BF)
            C6[5, rows, cols] = (root * w).astype(BF)
        return tuple(new)

    lax.fori_loop(0, SEQ // T, branch_tile, tuple(jnp.zeros((1, ch), F32) for _ in range(y_size)))
    unit_out(OUT)
    k_cf = send_out(C6, o_cf)
    send_out(A, o_a)
    send_out(LRU, o_lru)
    send_out(CV, o_cv)

    def out_rows(rows):
        return nt(LRU[rows, :], full(OUT))

    PS[...] = out_rows(other)
    sent(k_cot)
    sent(k_n1t)
    mix_copy = pair_copy(net, PS, PR, ps, pr, 2)
    mix_copy.start()
    MIX[...] = out_rows(own)
    big.wait(GA0, 2)
    unit_out(GA0)
    big.start(DN1, 0)
    big.step(GA1, 1)
    mix_copy.wait_recv()

    @pl.loop(0, half // 128)
    def _(i):
        rows = rows_of(i, 128)
        v = tok[rows, :].astype(F32) + MIX[rows, :] + PR[rows, :]
        MIX[rows, :] = v
        s = lax.rsqrt(jnp.mean(v * v, axis=1, keepdims=True) + EPS)
        SA[pl.ds(pl.multiple_of(c * half + i * 128, 128), 128), :] = (v * s * gains[1:2, :]).astype(BF)

    n2_copy = pair_copy(net, SA.at[own], SA.at[own], ps, pr, 3)
    n2_in = pair_copy(net, SA.at[other], SA.at[other], ps, pr, 3)
    n2_copy.start()
    send_out(MIX, o_mix)
    big.step(DN0, 0)
    big.wait(UP0, 2)
    unit_out(UP0)
    n2_in.wait_recv()
    transpose_into(SB, SA, SEQ)
    send_out(SB, o_n2t)
    sent(k_cf)
    F = 256

    def ff(j):
        @pl.loop(0, SEQ // F)
        def _(i):
            rows = rows_of(i, F)
            up = nn(SA[rows, :], full(UP[j]))
            g, gp = gelu_parts(nn(SA[rows, :], full(GATE[j])))
            C6[j, rows, :] = (g * up).astype(BF)
            C6[2 + j, rows, :] = (gp * up).astype(BF)
            C6[4 + j, rows, :] = g.astype(BF)

    ff(0)
    big.step(UP1, 1)
    big.step(DN1, 0)
    big.wait(GA1, 2)
    unit_out(GA1)
    big.step(DN0, 1)
    big.wait(UP1, 2)
    unit_out(UP1)
    big.step(DN1, 1)
    ff(1)
    send_out(C6, o_c6)
    big.wait(DN0, 2)
    unit_out(DN0)
    big.wait(DN1, 2)
    unit_out(DN1)
    for u in range(UNITS):
        big.drain(u)
    small.drain(0)
    for cp in (tok_copy, cot_copy, mix_copy, n2_copy):
        cp.wait_send()
    for k in range(len(out_copies)):
        sent(k)


class Scatter:
    def __init__(self, net, ref, slots, flows, bufs, index, ss, rs, credit):
        self.net, self.ref, self.slots, self.flows = net, ref, slots, flows
        self.bufs, self.index, self.ss, self.rs, self.credit = bufs, index, ss, rs, credit

    def lands(self, u, s, j):
        buf = self.bufs[self.flows[u], s]
        return buf.at[self.index[u] % buf.shape[0], j - 1]

    def copy(self, u, s, j):
        order = self.flows[u]
        d = order[s]
        at = dict(self.net.at)
        at[d] = self.net.shifted(d, j)
        idx = [at[e] if e in order[: s + 1] else slice(None) for e in "yzx"]
        k = self.net.off[d] + j - 1
        return pltpu.make_async_remote_copy(
            src_ref=self.ref.at[(self.slots[u], *idx)], dst_ref=self.lands(u, s, j),
            send_sem=self.ss.at[u, k], recv_sem=self.rs.at[u, k],
            device_id=self.net.device(d, j), device_id_type=MESH)

    def hops(self, u, s):
        return range(1, self.net.size[self.flows[u][s]])

    def start(self, u, s):
        ring = self.bufs[self.flows[u], s].shape[0]
        if self.index[u] >= ring:
            pl.semaphore_wait(self.credit[self.flows[u]].at[self.index[u] - ring, s], self.net.size[self.flows[u][s]] - 1)
        for j in self.hops(u, s):
            self.copy(u, s, j).start()

    def add(self, u, s, out=None):
        order = self.flows[u]
        d = order[s]
        for j in self.hops(u, s):
            self.copy(u, s, j).wait_recv()
        rest = [e for e in "yzx" if e not in order[: s + 1]]
        buf = self.bufs[order, s]
        b = self.index[u] % buf.shape[0]

        def block(place):
            idx = [place[e] if e in place else self.net.at[e] for e in "yzx"]
            total = self.ref[(self.slots[u], *idx)].astype(F32)
            for j in self.hops(u, s):
                total = total + buf[(b, j - 1, *[place[e] for e in rest])].astype(F32)
            if out is None:
                self.ref[(self.slots[u], *idx)] = total.astype(BF)
            else:
                out[u] = total

        def over(names, place):
            if not names:
                block(place)
            elif names[0] == "z":
                @pl.loop(0, self.net.size["z"])
                def _(z):
                    over(names[1:], {**place, "z": z})
            else:
                for n in range(self.net.size[names[0]]):
                    over(names[1:], {**place, names[0]: n})

        over(rest, {})
        ring = buf.shape[0]
        if (self.flows[u], self.index[u] + ring) in [(self.flows[v], self.index[v]) for v in self.flows]:
            for j in self.hops(u, s):
                pl.semaphore_signal(self.credit[order].at[self.index[u], s], inc=1,
                                    device_id=self.net.device(d, -j), device_id_type=MESH)

    def step(self, u, s, out=None):
        self.add(u, s, out if s == 2 else None)
        if s < 2:
            self.start(u, s + 1)

    def drain(self, u):
        for s in range(3):
            for j in self.hops(u, s):
                self.copy(u, s, j).wait_send()


BACK = {DN0: "yxz", GA0: "yxz", UP0: "yxz", RNN: "yxz", DN1: "xyz", GA1: "xyz", UP1: "xyz", GEL: "xyz", OUT: "zxy"}
SLOT = {DN0: 9, DN1: 10, GA0: DN0, GA1: DN1, UP0: GA0, UP1: GA1, OUT: UP0, GEL: UP1, RNN: OUT}
INDEX = {DN0: 0, DN1: 0, GA0: 1, GA1: 1, UP0: 2, UP1: 2, RNN: 3, GEL: 3, OUT: 0}


def backward_kernel(sizes, group,
                    w_h, cot_h, cott_h, n1t_h, n2t_h, c6_h, cf_h, a_h, ri_h, lru_h, cv_h, mix_h, tok_h, prm, gains, hw,
                    o_block, o_gtok, o_gw, o_gs,
                    W, C6, COT, TT, NT, GM, PS, PR, LRU, AS, RS, acc, GS, pgain,
                    a0, a1, a2, b0, b1, b2, e0, e1, e2, s0, s1, s2,
                    ss, rs, sss, srs, ca, cb, ps, pr, ls, ast, rst):
    net = Net(*sizes)
    z_size, x_size, y_size = sizes
    c = net.at["c"]
    half = SEQ // 2
    ch = W.shape[-1]
    depth = COT.shape[1]
    own, other = pl.ds(pl.multiple_of(c * half, half), half), pl.ds(pl.multiple_of((1 - c) * half, half), half)
    loads = {}

    def load(name, src, dst):
        loads[name] = pltpu.make_async_copy(src, dst, ls.at[len(loads)])
        loads[name].start()

    def loaded(*names):
        for name in names:
            loads[name].wait()

    load("cott", cott_h, TT)
    load("h", c6_h.at[0:2], C6.at[0:2])
    load("cot", cot_h, COT)
    load("w_dn", w_h.at[DN0:], W.at[DN0:9])
    load("ab", c6_h.at[2:6], C6.at[2:6])
    load("w_ff", w_h.at[GA0:DN0], W.at[GA0:DN0])
    load("n2t", n2t_h, NT)
    load("mix", mix_h, GM)
    load("w_rnn", w_h.at[0:GA0], W.at[0:GA0])
    load("lru", lru_h, LRU)
    load("tok", tok_h, PS.at[1])
    net.barrier()
    bufs = {("yxz", 0): a0, ("yxz", 1): a1, ("yxz", 2): a2, ("xyz", 0): b0, ("xyz", 1): b1, ("xyz", 2): b2,
            ("zxy", 0): e0, ("zxy", 1): e1, ("zxy", 2): e2}
    big = Scatter(net, W, SLOT, BACK, bufs, INDEX, ss, rs, {"yxz": ca, "xyz": cb, "zxy": None})
    small = Scatter(net, GS, {0: 0}, {0: "yxz"}, {("yxz", 0): s0, ("yxz", 1): s1, ("yxz", 2): s2}, {0: 0}, sss, srs, None)

    def step(u, s):
        big.step(u, s, o_gw)

    def full(u):
        return jnp.concatenate([W[u, yy].reshape(depth, ch) for yy in range(y_size)], axis=1)

    zh = z_size // 2

    def weight_grad(u, left, right):
        @pl.loop(0, 2)
        def _(i):
            val = nn(left[rows_of(i, depth // 2), :], right[...]).astype(BF)
            for yy in range(y_size):
                W[SLOT[u], yy, pl.ds(i * zh, zh)] = val[:, yy * ch : (yy + 1) * ch].reshape(
                    zh, x_size, depth // (z_size * x_size), ch)

    loaded("cott", "h")
    weight_grad(DN0, TT, C6.at[0])
    big.start(DN0, 0)
    weight_grad(DN1, TT, C6.at[1])
    big.start(DN1, 0)
    loaded("cot", "w_dn", "ab")
    F = 256
    for j in range(2):
        @pl.loop(0, SEQ // F)
        def _(i):
            rows = rows_of(i, F)
            gh = nn(COT[rows, :], full(DOWN[j]))
            C6[2 + j, rows, :] = (gh * C6[2 + j, rows, :].astype(F32)).astype(BF)
            C6[4 + j, rows, :] = (gh * C6[4 + j, rows, :].astype(F32)).astype(BF)

    loaded("w_ff")

    def mlp_back(base, i):
        rows = pl.ds(pl.multiple_of(base + i * F, F), F)
        return (nt(C6[2, rows, :], full(GA0)) + nt(C6[3, rows, :], full(GA1))
                + nt(C6[4, rows, :], full(UP0)) + nt(C6[5, rows, :], full(UP1)))

    def mlp_out(base, i):
        rows = pl.ds(pl.multiple_of(base + i * F, F), F)
        return nt(C6[0, rows, :], full(DN0)) + nt(C6[1, rows, :], full(DN1))

    def partial_rows(fn, base, dst):
        @pl.loop(0, half // F)
        def _(i):
            dst[rows_of(i, F), :] = fn(base, i).astype(dst.dtype)

    base_own, base_other = c * half, (1 - c) * half
    partial_rows(mlp_back, base_other, PS.at[0])
    back_copy = pair_copy(net, PS.at[0], PR.at[0], ps, pr, 0)
    back_copy.start()
    partial_rows(mlp_back, base_own, o_gtok)
    loaded("mix", "n2t", "tok")
    acc[...] = jnp.zeros_like(acc)
    pgain[...] = jnp.zeros_like(pgain)
    step(DN0, 0)
    step(DN1, 0)
    back_copy.wait_recv()
    T = 128

    @pl.loop(0, half // T)
    def _(i):
        rows = rows_of(i, T)
        at = pl.ds(pl.multiple_of(base_own + i * T, T), T)
        v = GM[rows, :]
        gn = o_gtok[rows, :] + PR[0, rows, :].astype(F32)
        s = lax.rsqrt(jnp.mean(v * v, axis=1, keepdims=True) + EPS)
        q = gn * gains[1:2, :]
        pgain[1:2, :] += jnp.sum(gn * v * s, axis=0, keepdims=True)
        gm = COT[at, :].astype(F32) + s * q - (s * s * s) * v * jnp.mean(q * v, axis=1, keepdims=True)
        o_gtok[rows, :] = gm
        COT[at, :] = gm.astype(BF)

    row_copy = pair_copy(net, COT.at[own], COT.at[own], ps, pr, 1)
    row_in = pair_copy(net, COT.at[other], COT.at[other], ps, pr, 1)
    row_copy.start()
    back_copy.wait_send()
    partial_rows(mlp_out, base_other, PS.at[0])
    out_copy = pair_copy(net, PS.at[0], PR.at[1], ps, pr, 2)
    out_copy.start()
    @pl.loop(0, half // F)
    def _(i):
        GM[rows_of(i, F), :] += mlp_out(base_own, i)

    weight_grad(GA0, NT, C6.at[2])
    big.start(GA0, 0)
    weight_grad(GA1, NT, C6.at[3])
    big.start(GA1, 0)
    step(DN0, 1)
    step(DN1, 1)
    row_in.wait_recv()
    loaded("w_rnn", "lru")
    weight_grad(UP0, NT, C6.at[4])
    weight_grad(UP1, NT, C6.at[5])
    load("n1t", n1t_h, NT)
    load("cf", cf_h, C6)
    transpose_into(TT, COT, SEQ)
    weight_grad(OUT, TT, LRU)
    big.start(OUT, 0)
    load("cv", cv_h, LRU)
    out_copy.wait_recv()

    @pl.loop(0, half // F)
    def _(i):
        rows = rows_of(i, F)
        PR[1, rows, :] = (GM[rows, :] + PR[1, rows, :].astype(F32)).astype(BF)

    block_copy = pltpu.make_async_copy(PR.at[1], o_block, ls.at[15])
    block_copy.start()
    tiles = SEQ // T

    def fetch(n, slot):
        at = (tiles - 1 - n) * T
        return (
            pltpu.make_async_copy(a_h.at[pl.ds(pl.multiple_of(at, T), T)], AS.at[slot], ast.at[slot]),
            pltpu.make_async_copy(ri_h.at[pl.ds(pl.multiple_of(at, T), T + 8)], RS.at[slot], rst.at[slot]),
        )

    for cp in fetch(0, 0):
        cp.start()
    loaded("cf")

    def back_tile(n, carries):
        hooks = {
            0: [lambda: step(DN0, 2), lambda: step(DN1, 2)],
            1: [lambda: step(GA0, 0), lambda: big.start(UP0, 0)],
            2: [lambda: step(GA1, 0), lambda: big.start(UP1, 0)],
            4: [lambda: step(GA0, 1)],
            5: [lambda: step(GA1, 1)],
            6: [lambda: step(OUT, 0)],
            7: [lambda: step(GA0, 2), lambda: step(GA1, 2), lambda: step(OUT, 1)],
        }
        for tile, fns in hooks.items():
            @pl.when(n == tile)
            def _():
                for fn in fns:
                    fn()
        slot = lax.rem(n, 2)
        for cp in fetch(n, slot):
            cp.wait()

        @pl.when(n + 1 < tiles)
        def _():
            for cp in fetch(n + 1, 1 - slot):
                cp.start()

        i = tiles - 1 - n
        rows = rows_of(i, T)
        gl_all = nn(COT[rows, :], full(OUT))
        new = []
        for yy in range(y_size):
            adj_next, a_next, gco_next = carries[yy]
            cols = slice(yy * ch, (yy + 1) * ch)
            p = prm[yy]
            gl = gl_all[:, cols]
            at = AS[slot, :, cols]
            last = lax.broadcasted_iota(jnp.int32, (T, ch), 0) == T - 1
            shifted = jnp.where(last, a_next, pltpu.roll(at, T - 1, 0))
            adj, adj_first = scan_backward(shifted, gl * C6[0, rows, cols].astype(F32), adj_next)
            C6[1, rows, cols] = (gl * C6[1, rows, cols].astype(F32)).astype(BF)
            grp = adj * C6[3, rows, cols].astype(F32)
            gip = adj * C6[4, rows, cols].astype(F32)
            gr_low, gi_low = grp.astype(BF), gip.astype(BF)
            gcd = adj * C6[5, rows, cols].astype(F32)
            acc[yy, 5:6] += jnp.sum(grp, axis=0, keepdims=True)
            acc[yy, 6:7] += jnp.sum(gip, axis=0, keepdims=True)
            acc[yy, 7:8] += jnp.sum(adj * C6[2, rows, cols].astype(F32), axis=0, keepdims=True)
            C6[3, rows, cols] = gr_low
            C6[4, rows, cols] = gi_low
            parts = []
            for h in range(ch // 128):
                hs = slice(h * 128, (h + 1) * 128)
                hc = slice(yy * ch + h * 128, yy * ch + (h + 1) * 128)
                parts.append(nt(jnp.concatenate([gr_low[:, hs], gi_low[:, hs]], axis=1),
                                jnp.concatenate([hw[0, :, hc], hw[1, :, hc]], axis=1)))
            gco = gcd + jnp.concatenate(parts, axis=1)
            ext = jnp.concatenate([gco, gco_next], axis=0)
            x = RS[slot, :, cols]
            grn = p[0:1] * gco
            acc[yy, 0:1] += jnp.sum(gco * x[8:], axis=0, keepdims=True)
            acc[yy, 4:5] += jnp.sum(gco, axis=0, keepdims=True)
            for k in range(1, 4):
                grn = grn + p[k : k + 1] * pltpu.roll(ext, T + 8 - k, 0)[:T]
                acc[yy, k : k + 1] += jnp.sum(gco * pltpu.roll(x, k, 0)[8:], axis=0, keepdims=True)
            C6[5, rows, cols] = grn.astype(BF)
            new.append((adj_first, at[0:1], gco[0:8]))
        return tuple(new)

    zero = (jnp.zeros((1, ch), F32), jnp.zeros((1, ch), F32), jnp.zeros((8, ch), F32))
    lax.fori_loop(0, tiles, back_tile, (zero,) * y_size)
    loaded("n1t")
    step(UP0, 0)
    weight_grad(RNN, NT, C6.at[5])
    big.start(RNN, 0)
    step(UP1, 0)
    weight_grad(GEL, NT, C6.at[1])
    big.start(GEL, 0)

    def rnn_back(base, i):
        rows = pl.ds(pl.multiple_of(base + i * F, F), F)
        return nt(C6[5, rows, :], full(RNN)) + nt(C6[1, rows, :], full(GEL))

    out_copy.wait_send()
    partial_rows(rnn_back, base_other, PS.at[0])
    rnn_copy = pair_copy(net, PS.at[0], PR.at[0], ps, pr, 3)
    rnn_copy.start()
    partial_rows(rnn_back, base_own, GM)
    step(UP0, 1)
    step(UP1, 1)
    loaded("cv")
    for yy in range(y_size):
        acc[yy, 7:8] = acc[yy, 7:8] * jax.nn.sigmoid(prm[yy, 7:8])
        for h in range(ch // 128):
            hs = slice(h * 128, (h + 1) * 128)
            hc = slice(yy * ch + h * 128, yy * ch + (h + 1) * 128)
            both = lax.dot_general(LRU[:, hc], jnp.concatenate([C6[3, :, hc], C6[4, :, hc]], axis=1),
                                   (((0,), (0,)), ((), ())), preferred_element_type=F32)
            for n in range(2):
                val = both[:, n * 128 : (n + 1) * 128].astype(BF)
                if group > 1:
                    val = jnp.broadcast_to(val.reshape(-1, 1, 16, 128), (z_size * x_size // group, group, 16, 128))
                GS[0, yy, :, :, 16 * n : 16 * n + 16, hs] = val.reshape(z_size, x_size, 16, 128)
    rnn_copy.wait_recv()

    @pl.loop(0, half // T)
    def _(i):
        rows = rows_of(i, T)
        v = PS[1, rows, :].astype(F32)
        gn = GM[rows, :] + PR[0, rows, :].astype(F32)
        s = lax.rsqrt(jnp.mean(v * v, axis=1, keepdims=True) + EPS)
        q = gn * gains[0:1, :]
        pgain[0:1, :] += jnp.sum(gn * v * s, axis=0, keepdims=True)
        o_gtok[rows, :] += s * q - (s * s * s) * v * jnp.mean(q * v, axis=1, keepdims=True)

    gain_copy = pair_copy(net, pgain.at[0:8], pgain.at[8:16], ps, pr, 4)
    gain_copy.start()
    step(OUT, 2)
    gain_copy.wait_recv()
    for n in range(2):
        row = pgain[n : n + 1, :] + pgain[8 + n : 9 + n, :]
        row = jnp.concatenate([row, jnp.zeros((1, 3 * ch - depth), F32)], axis=1)
        for k in range(3):
            for yy in range(y_size):
                acc[yy, 8 + 3 * n + k : 9 + 3 * n + k, :] = row[:, k * ch : (k + 1) * ch]

    @pl.loop(0, z_size)
    def _(z):
        for yy in range(y_size):
            for xx in range(x_size):
                GS[0, yy, z, xx, 32:48, :] = acc[yy].astype(BF)

    small.start(0, 0)
    step(UP0, 2)
    step(UP1, 2)
    small.step(0, 0)
    step(RNN, 0)
    step(GEL, 0)
    small.step(0, 1)
    step(RNN, 1)
    step(GEL, 1)
    small.step(0, 2, o_gs)
    step(RNN, 2)
    step(GEL, 2)
    for u in range(UNITS):
        big.drain(u)
    small.drain(0)
    for cp in (row_copy, rnn_copy, gain_copy):
        cp.wait_send()
    block_copy.wait()


def params_block(args, dp_index, dp, ch, depth):
    (mix_gain, conv_weight, conv_bias, recur_weight, input_weight, recur_bias, input_bias, decay_param, mlp_gain) = args
    rows8 = jnp.concatenate([conv_weight, conv_bias[None], recur_bias[None], input_bias[None], decay_param[None]], axis=0)
    rows8 = lax.dynamic_update_slice(jnp.zeros((8, ch), BF), rows8, (0, dp_index * rows8.shape[1]))
    gains = jnp.stack([mix_gain, mlp_gain])
    gains = lax.dynamic_update_slice(jnp.zeros((2, 3 * ch), BF), gains, (0, dp_index * gains.shape[1]))
    heads = []
    for w in (recur_weight, input_weight):
        w = jnp.transpose(w, (1, 0, 2)).reshape(w.shape[1], ch)
        if w.shape[0] < 16:
            w = lax.dynamic_update_slice(jnp.zeros((16, ch), BF), w, (lax.rem(dp_index * w.shape[0], 16), 0))
        heads.append(w)
    return jnp.concatenate([*heads, rows8, gains.reshape(6, ch), jnp.zeros((2, ch), BF)], axis=0)


def any_spec():
    return pl.BlockSpec(memory_space=pl.ANY)


def vmem_spec():
    return pl.BlockSpec(memory_space=pltpu.VMEM)


def body(sizes, tokens, mix_gain, rnn_weight, gelu_weight, conv_weight, conv_bias, recur_weight, input_weight,
         recur_bias, input_bias, decay_param, out_weight, mlp_gain, gate_weight, up_weight, down_weight, cotangent):
    z_size, x_size, y_size = sizes
    dp = z_size * x_size
    dp_index = lax.axis_index("dp")
    rows, depth = tokens.shape
    part, ch = rnn_weight.shape
    head_rows = recur_weight.shape[1]
    group = max(1, 16 // head_rows)
    wide = y_size * ch
    wp = jnp.stack([rnn_weight, gelu_weight, out_weight.T, gate_weight[:, :ch], up_weight[:, :ch],
                    gate_weight[:, ch:], up_weight[:, ch:], down_weight[:ch].T, down_weight[ch:].T])
    sp = params_block((mix_gain, conv_weight, conv_bias, recur_weight, input_weight, recur_bias, input_bias,
                       decay_param, mlp_gain), dp_index, dp, ch, depth)
    shape = jax.ShapeDtypeStruct
    grid = (y_size, z_size, x_size)
    hops = z_size + x_size + y_size - 3
    f_out = [
        shape((UNITS, *grid, part, ch), BF), shape((SEQ, depth), BF), shape((depth, SEQ), BF),
        shape((depth, SEQ), BF), shape((depth, SEQ), BF), shape((6, SEQ, wide), BF), shape((6, SEQ, wide), BF),
        shape((SEQ, wide), F32), shape((SEQ + 8, wide), F32), shape((SEQ, wide), BF), shape((SEQ, wide), BF),
        shape((rows, depth), F32), shape((y_size, 16, ch), F32), shape((8, depth), F32), shape((2, 128, wide), BF),
    ]
    dma, sem = pltpu.SemaphoreType.DMA, pltpu.SemaphoreType.REGULAR
    kept = pl.pallas_call(
        functools.partial(forward_kernel, sizes, group),
        out_shape=f_out,
        in_specs=[vmem_spec(), any_spec(), any_spec(), any_spec()],
        out_specs=[any_spec()] * 12 + [vmem_spec()] * 3,
        scratch_shapes=[
            pltpu.VMEM((UNITS, *grid, part, ch), BF), pltpu.VMEM((1, *grid, SMALL, ch), BF),
            pltpu.VMEM((SEQ, depth), BF), pltpu.VMEM((SEQ, depth), BF), pltpu.VMEM((depth, SEQ), BF),
            pltpu.VMEM((SEQ, depth), BF), pltpu.VMEM((SEQ + 8, wide), F32), pltpu.VMEM((SEQ, wide), F32),
            pltpu.VMEM((SEQ, wide), BF), pltpu.VMEM((6, SEQ, wide), BF), pltpu.VMEM((SEQ, wide), BF),
            pltpu.VMEM((rows, depth), F32), pltpu.VMEM((rows, depth), F32), pltpu.VMEM((rows, depth), F32),
            dma((UNITS, hops)), dma((UNITS, hops)), dma((1, hops)), dma((1, hops)), dma((4,)), dma((4,)), dma((4,)),
            dma((24,)),
        ],
        compiler_params=pltpu.CompilerParams(collective_id=0, has_side_effects=True, vmem_limit_bytes=VMEM_LIMIT),
        name="gather_forward",
    )(tokens, cotangent, wp, sp)
    small_shape = (SMALL, ch)
    block_out, grad_tokens, gw, gs = pl.pallas_call(
        functools.partial(backward_kernel, sizes, group),
        out_shape=[shape((rows, depth), BF), shape((rows, depth), F32), shape((UNITS, part, ch), F32),
                   shape((1, SMALL, ch), F32)],
        in_specs=[any_spec()] * 13 + [vmem_spec()] * 3,
        out_specs=[any_spec()] + [vmem_spec()] * 3,
        scratch_shapes=[
            pltpu.VMEM((UNITS + 2, *grid, part, ch), BF), pltpu.VMEM((6, SEQ, wide), BF), pltpu.VMEM((SEQ, depth), BF),
            pltpu.VMEM((depth, SEQ), BF), pltpu.VMEM((depth, SEQ), BF), pltpu.VMEM((rows, depth), F32),
            pltpu.VMEM((2, rows, depth), BF), pltpu.VMEM((2, rows, depth), BF), pltpu.VMEM((SEQ, wide), BF),
            pltpu.VMEM((2, 128, wide), F32), pltpu.VMEM((2, 136, wide), F32), pltpu.VMEM((y_size, 16, ch), F32),
            pltpu.VMEM((1, *grid, SMALL, ch), BF), pltpu.VMEM((16, depth), F32),
            pltpu.VMEM((2, y_size - 1, z_size, x_size, part, ch), BF),
            pltpu.VMEM((2, x_size - 1, z_size, part, ch), BF),
            pltpu.VMEM((4, z_size - 1, part, ch), BF),
            pltpu.VMEM((2, x_size - 1, y_size, z_size, part, ch), BF),
            pltpu.VMEM((2, y_size - 1, z_size, part, ch), BF),
            pltpu.VMEM((4, z_size - 1, part, ch), BF),
            pltpu.VMEM((1, z_size - 1, y_size, x_size, part, ch), BF),
            pltpu.VMEM((1, x_size - 1, y_size, part, ch), BF),
            pltpu.VMEM((1, y_size - 1, part, ch), BF),
            pltpu.VMEM((1, y_size - 1, z_size, x_size, *small_shape), BF),
            pltpu.VMEM((1, x_size - 1, z_size, *small_shape), BF),
            pltpu.VMEM((1, z_size - 1, *small_shape), BF),
            dma((UNITS, hops)), dma((UNITS, hops)), dma((1, hops)), dma((1, hops)),
            sem((2, 2)), sem((2, 2)), dma((5,)), dma((5,)), dma((16,)), dma((2,)), dma((2,)),
        ],
        compiler_params=pltpu.CompilerParams(collective_id=1, has_side_effects=True, vmem_limit_bytes=VMEM_LIMIT),
        name="backward_scatter",
    )(*kept[:12], tokens, *kept[12:])
    gs = gs[0]
    heads = []
    for n in range(2):
        g = gs[16 * n : 16 * n + 16]
        if head_rows < 16:
            g = lax.dynamic_slice(g, (lax.rem(dp_index * head_rows, 16), 0), (head_rows, ch))
        heads.append(jnp.transpose(g.reshape(head_rows, ch // 128, 128), (1, 0, 2)))
    own = ch // dp
    par = lax.dynamic_slice(gs[32:40], (0, dp_index * own), (8, own))
    gains = lax.dynamic_slice(gs[40:46].reshape(2, 3 * ch), (0, dp_index * part), (2, part))
    return (
        block_out, grad_tokens, gains[0], gw[RNN], gw[GEL], par[0:4], par[4], heads[0], heads[1],
        par[5], par[6], par[7], gw[OUT].T, gains[1],
        jnp.concatenate([gw[GA0], gw[GA1]], axis=1), jnp.concatenate([gw[UP0], gw[UP1]], axis=1),
        jnp.concatenate([gw[DN0], gw[DN1]], axis=1).T,
    )


def solution(mesh):
    dp, tensor = mesh.shape["dp"], mesh.shape["tensor"]
    x_size = 2
    sizes = (dp // x_size, x_size, tensor // 2)
    rows, split, vec = P(("dp", "tensor"), None), P("dp", "tensor"), P(("tensor", "dp"))
    head, flip, taps = P("tensor", "dp", None), P("tensor", "dp"), P(None, ("tensor", "dp"))
    return jax.shard_map(
        functools.partial(body, sizes),
        mesh=mesh,
        in_specs=(rows, P("dp"), split, split, taps, vec, head, head, vec, vec, vec, flip, P("dp"), split, split, flip,
                  rows),
        out_specs=(rows, rows, P("dp"), split, split, taps, vec, head, head, vec, vec, vec, flip, P("dp"), split, split,
                   flip),
        check_vma=False,
    )
```

time: 1910 us -> 377 us (0.20)
  waiting for transfers between devices: 951 us -> 0 us
  local copies, waits for them, and re-layouts: 372 us -> 22.7 us
  Pallas kernels: 0 us -> 348 us
  blocking collectives: 276 us -> 0 us
  matrix products: 138 us -> 0 us
  other arithmetic: 136 us -> 4.21 us
  between operations: 21.2 us -> 0.83 us
    reduce_scatter x12 -> x0, waiting for transfers between devices: 773 us -> none  [the longest x1 77.6 us: body(): lax.psum_scatter(grad_down, 'dp', scatter_dimension=1, tiled=True)]
    pallas_call x0 -> x2, Pallas kernels: none -> 348 us  [the longest x1 185 us: body(): pl.pallas_call(functools.partial(backward_kernel, sizes, group), out_shap...]
    all_gather x8 -> x0, blocking collectives: 213 us -> none  [the longest x1 34.2 us: body(): lax.all_gather(rnn_weight, 'dp', axis=0, tiled=True)]
    all_gather x7 -> x0, waiting for transfers between devices: 175 us -> none  [the longest x1 37.8 us: body(): lax.all_gather(up_weight, 'dp', axis=0, tiled=True)]
    slice x79 -> x5, local copies, waits for them, and re-layouts: 171 us -> 3.72 us  [the longest x1 0.96 us: body(): down_weight[ch:]]
    dot_general x24 -> x0, matrix products: 138 us -> none  [the longest x6 43 us: times_transposed(): lax.dot_general(left, right, (((1,), (1,)), ((), ())), preferred_element_...]
    pad x79 -> x0, local copies, waits for them, and re-layouts: 99.1 us -> none  [lru_mix(): decays_out, state = lax.associative_scan(combine, (decay, driven), axis=1)]
    reshape x9 -> x5, local copies, waits for them, and re-layouts: 60.1 us -> 0.77 us  [the longest x1 0.71 us: params_block(): w = jnp.transpose(w, (1, 0, 2)).reshape(w.shape[1], ch)]
  transfers between devices with their start and end apart: 20 -> 0, of which waited for: 17 -> 0; matrix products, arithmetic and copies ran while one was open for 5% -> 0% of each run, Pallas kernels for 0% -> 0%
where the time goes in v1:
time: 377 us; the launch traced here: 376 us
  Pallas kernels  348 us (92%)
  local copies, waits for them, and re-layouts  22.7 us (6%)
  other arithmetic  4.21 us (1%)
    pallas_call x1, Pallas kernels, body(): pl.pallas_call(functools.partial(backward_kernel, sizes, group), out_shap...  185 us
    pallas_call x1, Pallas kernels, body(): pl.pallas_call(functools.partial(forward_kernel, sizes, group), out_shape...  163 us
    unnamed x31, local copies, waits for them, and re-layouts  11.2 us

profile of v1, /device:TPU:0, one launch (start us, length us, event | category | flops | bytes accessed | tf_op | source)
XLA Modules:
  0.0 376.0 jit_solution(3944794998156857748)
XLA Ops:
  0.7 0.8 concatenate.15
  1.5 0.7 constant_dynamic-update-slice_fusion
  2.4 0.7 copy_bitcast_fusion
  3.1 2.4 concatenate.16.sp
  5.6 1.0 copy.43
  6.6 1.0 fusion
  7.8 0.9 bitcast_dynamic-update-slice_fusion.8
  8.7 0.9 bitcast_dynamic-update-slice_fusion.7
  9.7 0.9 bitcast_dynamic-update-slice_fusion.6
  10.6 0.9 bitcast_dynamic-update-slice_fusion.5
  11.6 0.9 copy-done.3
  12.5 162.9 %gather_forward.1 = (bf16[9,2,4,2,128,384]{5,4,3,2,1,0:T(8,128)(2,1)}, bf16[1024,1024]{1,0:T(8,128)(2,1)}, bf16[1024,1024]{1,0:T(8,128)(2,1)}, bf16[1024,1024]{1...) custom-call(bf16[512,1024]{1,0:T(8,128)(2,1)} %tok_h.1, ...), custom_call_target="tpu_custom_call" | custom-call | tf_op jit(solution)/shard_map/gather_forward/pallas_call | solution.py:864
  175.4 185.4 %backward_scatter.1 = (bf16[512,1024]{1,0:T(8,128)(2,1)}, f32[512,1024]{1,0:T(8,128)}, f32[9,128,384]{2,1,0:T(8,128)}, f32[1,48,384]{2,1,0:T(8,128)}) custom-call(bf16[9,2,4,2,128,384]{5,4,3,2,1,0:T(8,128)(2,1)} %get-tuple-element.36.w_h, bf16[1024,1024]{1,0:T(8,128)(2,1)} %get-tuple-element.37.cot_h, bf16[1024,1024]{1,0:T(8,128)(2,1)} %get-tuple-element.38.cott_h, ...), custom_call_target="tpu_custom_call" | custom-call | tf_op jit(solution)/shard_map/backward_scatter/pallas_call | solution.py:882
  360.8 0.7 slice.99
  362.7 0.7 slice.95
  363.4 0.8 fusion.1
  364.7 0.6 copy.49
  366.0 2.5 slice_bitcast_fusion.1
  368.5 0.9 copy.51
  369.4 0.8 copy.50
  370.2 1.8 pad_maximum_fusion.1
  372.0 1.7 pad_maximum_fusion
  373.7 1.0 copy.70
  374.7 1.3 copy.71
  (35 shorter events, 3.0 us)
Async XLA Ops:
  0.7 1.8 copy-start
  0.7 10.8 %copy-start.6 = (bf16[128,768]{1,0:T(8,128)(2,1)S(1)}, bf16[128,768]{1,0:T(8,128)(2,1)}, u32[]{:S(2)}) copy-start(bf16[128,768]{1,0:T(8,128)(2,1)} %param.31) | copy-start | bytes 589828
  0.7 10.8 %copy-start.5 = (bf16[128,768]{1,0:T(8,128)(2,1)S(1)}, bf16[128,768]{1,0:T(8,128)(2,1)}, u32[]{:S(2)}) copy-start(bf16[128,768]{1,0:T(8,128)(2,1)} %param.30) | copy-start | bytes 589828
  11.6 0.9 copy-start.3
  368.4 5.3 %copy-start.4 = (bf16[512,1024]{1,0:T(8,128)(2,1)S(1)}, bf16[512,1024]{1,0:T(8,128)(2,1)}, u32[]{:S(2)}) copy-start(bf16[512,1024]{1,0:T(8,128)(2,1)} %get-tuple-element.127) | copy-start | bytes 3145732
  369.4 5.3 %copy-start.2 = (f32[512,1024]{1,0:T(8,128)S(1)}, f32[512,1024]{1,0:T(8,128)}, u32[]{:S(2)}) copy-start(f32[512,1024]{1,0:T(8,128)} %get-tuple-element.128) | copy-start | bytes 6291460
  373.7 2.3 copy-start.1

commit v2 on v1

v2 whole, which is shorter than its diff:
```python
import functools

import jax
import jax.numpy as jnp
from jax import lax
from jax.experimental import pallas as pl
from jax.experimental.pallas import tpu as pltpu
from jax.sharding import PartitionSpec as P

SEQ = 1024
EPS = 1e-06
GUARD = 0.01
DECAY_SCALE = 8.0
GELU_K = 0.7978845608028654
GELU_C = 0.044715
BF = jnp.bfloat16
F32 = jnp.float32
MESH = pl.DeviceIdType.MESH
VMEM_LIMIT = 63 * 1024 * 1024

RNN, GEL, OUT, GA0, UP0, GA1, UP1, DN0, DN1 = range(9)
UNITS = 9
GATE, UP, DOWN = (GA0, GA1), (UP0, UP1), (DN0, DN1)
CHUNKS = 2 * UNITS
SMALL = 48
F_FLOW = (
    "zyx", "zxy", "zyx", "zyx", "zxy", "zyx", "xzy", "zyx", "zyx", "zyx", "xzy", "xzy", "zyx", "zxy", "yzx", "xyz",
    "xzy", "zyx",
)
F_PLAN = (
    0, 4, 8, "pre1", 1, "pre2", 12, 5, "pre3", 16, 2, 9, 20, 6, 13, 24, 10, 17, 28, 3, 25, 32, 21, 36, 7, "rnn", 29,
    40, 14, 11, 22, 18, 26, 41, 44, 30, 33, 48, 37, 52, 15, "br", 19, "br", "br", 42, 23, 45, 56, 27, "br", 49, 60,
    34, "br", 53, 64, 31, "br", 61, 68, 38, "br", 46, "br", 35, 43, 57, 69, "out", 54, "mix", 65, 50, 62, "n2", 58,
    39, "ffa", 47, "ffa", "ffa", 70, 66, "ffa", 51, 55, "ffb", 59, "ffb", "ffb", "ffb", 67, 63, 71,
)
B_FLOW = (
    "yxz", "xyz", "yzx", "xyz", "yxz", "yxz", "yzx", "xyz", "xzy", "xzy", "xyz", "yxz", "yxz", "xyz", "xzy", "yxz",
    "yzx", "xyz",
)
B_PLAN = (
    "d0", 56, 60, "d1", 64, 68, "gh", "gh", "gh", "gh", "gh", "gh", "gh", 57, 61, "gh", "bo", "bw", "ga0", 69, 65,
    24, 28, "ga1", 58, 62, 40, 44, "gno", 70, "gno", "gnw", 66, 29, "gnw", 25, 63, 59, "norm", "up0", 71, 41, 67, 32,
    36, "up1", 45, 48, 52, "outg", 26, 30, 16, 20, "t", 42, 33, "t", 31, "t", 49, 43, 37, "t", "t", 46, "t", 17, 34,
    "t", 53, "t", 27, 21, 38, 35, 50, "gel", 8, 47, 54, 12, 18, 39, "rnn", 51, 0, 4, 22, "gn1o", "gn1w", 55, 9,
    "heads", 19, 13, "fin", 23, "s0", 1, 5, 14, "s1", 10, 2, 11, 6, "s2", 15, 3, "s3", 7,
)


def run_plan(plan, blocks, event):
    i = 0
    while i < len(plan):
        name = plan[i]
        i += 1
        if isinstance(name, int):
            event(name // 4, name % 4)
            continue
        turns, fn = blocks[name]
        if turns == 1:
            fn()
            continue
        hooks = {}
        for turn in range(1, turns):
            hooks[turn] = []
            while isinstance(plan[i], int):
                hooks[turn].append(plan[i])
                i += 1
            i += 1

        def hook(n, hooks=hooks):
            for turn, steps in hooks.items():
                if steps:
                    @pl.when(n == turn)
                    def _(steps=steps):
                        for step in steps:
                            event(step // 4, step % 4)

        fn(hook)


def nn(a, b):
    return jnp.dot(a, b, preferred_element_type=F32)


def nt(a, b):
    return lax.dot_general(a, b, (((1,), (1,)), ((), ())), preferred_element_type=F32)


def gelu_parts(v):
    v2 = v * v
    th = jnp.tanh(GELU_K * v * (1.0 + GELU_C * v2))
    half = 0.5 * (1.0 + th)
    return v * half, half + (0.5 * GELU_K) * v * (1.0 - th * th) * (1.0 + (3.0 * GELU_C) * v2)


class Net:
    def __init__(self, z_size, x_size, y_size):
        self.size = {"z": z_size, "x": x_size, "y": y_size, "c": 2}
        dp, t = lax.axis_index("dp"), lax.axis_index("tensor")
        self.at = {"z": dp // x_size, "x": lax.rem(dp, x_size), "y": t // 2, "c": lax.rem(t, 2)}
        self.off = {"z": 0, "x": z_size - 1, "y": z_size + x_size - 2}

    def shifted(self, d, j):
        n = self.size[d]
        return lax.rem(self.at[d] + (j % n), n)

    def device(self, d, j):
        at = dict(self.at)
        at[d] = self.shifted(d, j)
        return (at["z"] * self.size["x"] + at["x"], at["y"] * 2 + at["c"])

    def barrier(self):
        sem = pltpu.get_barrier_semaphore()
        count = 0
        for d in "zxyc":
            for j in range(1, self.size[d]):
                pl.semaphore_signal(sem, inc=1, device_id=self.device(d, j), device_id_type=MESH)
                count += 1
        pl.semaphore_wait(sem, count)


def chunk_rows(c, part):
    if part % 32:
        return slice(None) if c % 2 == 0 else None
    return slice(c % 2 * (part // 2), (c % 2 + 1) * (part // 2))


class Gather:
    def __init__(self, net, ref, flows, ss, rs, halves):
        self.net, self.ref, self.flows, self.ss, self.rs, self.halves = net, ref, flows, ss, rs, halves

    def region(self, c, s, at):
        order = self.flows[c]
        idx = [slice(None) if d in order[:s] else at[d] for d in "yzx"]
        if not self.halves:
            return self.ref.at[(c, *idx)]
        return self.ref.at[(c // 2, *idx, chunk_rows(c, self.ref.shape[4]))]

    def copy(self, c, s, j, sender):
        d = self.flows[c][s]
        at = dict(self.net.at)
        if sender:
            at[d] = self.net.shifted(d, -j)
        region = self.region(c, s, at)
        k = self.net.off[d] + j - 1
        return pltpu.make_async_remote_copy(
            src_ref=region, dst_ref=region, send_sem=self.ss.at[c, k], recv_sem=self.rs.at[c, k],
            device_id=self.net.device(d, j), device_id_type=MESH)

    def hops(self, c, s):
        return range(1, self.net.size[self.flows[c][s]])

    def event(self, c, k):
        if self.halves and chunk_rows(c, self.ref.shape[4]) is None:
            return
        if k:
            for j in self.hops(c, k - 1):
                self.copy(c, k - 1, j, True).wait_recv()
        if k < 3:
            for j in self.hops(c, k):
                self.copy(c, k, j, False).start()

    def drain(self, c):
        if self.halves and chunk_rows(c, self.ref.shape[4]) is None:
            return
        for s in range(3):
            for j in self.hops(c, s):
                self.copy(c, s, j, False).wait_send()


def pair_copy(net, src, dst, ss, rs, k):
    return pltpu.make_async_remote_copy(
        src_ref=src, dst_ref=dst, send_sem=ss.at[k], recv_sem=rs.at[k],
        device_id=net.device("c", 1), device_id_type=MESH)


def scan_forward(a, b, carry):
    rows, cols = a.shape
    a = a.reshape(rows // 8, 8, cols)
    b = b.reshape(rows // 8, 8, cols)
    place = lax.broadcasted_iota(jnp.int32, (rows // 8, 8, cols), 1)
    for k in (1, 2, 4):
        keep = place >= k
        b = b + a * jnp.where(keep, pltpu.roll(b, k, 1), 0.0)
        a = a * jnp.where(keep, pltpu.roll(a, k, 1), 1.0)
    out = []
    for g in range(rows // 8):
        s = b[g] + a[g] * carry
        out.append(s)
        carry = s[7:8]
    return jnp.concatenate(out, axis=0), carry


def scan_backward(a, b, carry):
    rows, cols = a.shape
    a = a.reshape(rows // 8, 8, cols)
    b = b.reshape(rows // 8, 8, cols)
    place = lax.broadcasted_iota(jnp.int32, (rows // 8, 8, cols), 1)
    for k in (1, 2, 4):
        keep = place < 8 - k
        b = b + a * jnp.where(keep, pltpu.roll(b, 8 - k, 1), 0.0)
        a = a * jnp.where(keep, pltpu.roll(a, 8 - k, 1), 1.0)
    out = []
    for g in reversed(range(rows // 8)):
        s = b[g] + a[g] * carry
        out.append(s)
        carry = s[0:1]
    return jnp.concatenate(out[::-1], axis=0), carry


def rows_of(i, n):
    return pl.ds(pl.multiple_of(i * n, n), n)


def join_params(gs, prm, gains, sizes):
    y_size = sizes[2]
    for yy in range(y_size):
        prm[yy] = jnp.sum(gs[0, yy, :, :, 32:48, :].astype(F32), axis=(0, 1))
    d = gains.shape[1]
    for n in range(2):
        row = jnp.concatenate([prm[0, 8 + 3 * n + k : 9 + 3 * n + k, :] for k in range(3)], axis=1)
        gains[n : n + 1, :] = row[:, :d]


def head_weight(gs, yy, first, group):
    blocks = gs[0, yy, :, :, first : first + 16, :]
    z, x, r, c = blocks.shape
    if group > 1:
        blocks = jnp.sum(blocks.astype(F32).reshape(z * x // group, group, r, c), axis=1).astype(BF)
    return blocks.reshape(-1, c)


def transpose_into(dst, src, n, step=256):
    @pl.loop(0, n // step)
    def _(i):
        dst[:, rows_of(i, step)] = src[rows_of(i, step), :].T


def forward_kernel(sizes, group,
                   tok, cot, w_rnn, w_gel, w_out, w_gate, w_up, w_down, small_in, rec_in, inp_in,
                   o_w, o_cot, o_cott, o_n1t, o_n2t, o_c6, o_cf, o_a, o_ri, o_lru, o_cv, o_mix, prm, gains, hw,
                   W, gs, T1, SA, SB, N1, RI, A, CV, C6, LRU, PS, PR, MIX, pack,
                   ss, rs, sss, srs, ps, pr, ls, outs):
    net = Net(*sizes)
    z_size, x_size, y_size = sizes
    c = net.at["c"]
    half = SEQ // 2
    ch = W.shape[-1]
    part = W.shape[4]
    depth = T1.shape[1]
    own, other = pl.ds(pl.multiple_of(c * half, half), half), pl.ds(pl.multiple_of((1 - c) * half, half), half)
    mine = (net.at["y"], net.at["z"], net.at["x"])
    dp_index = lax.axis_index("dp")

    sources = {RNN: w_rnn, GEL: w_gel, GA0: w_gate.at[:, 0:ch], GA1: w_gate.at[:, ch : 2 * ch], UP0: w_up.at[:, 0:ch],
               UP1: w_up.at[:, ch : 2 * ch]}
    place = {u: pltpu.make_async_copy(src, W.at[(u, *mine)], ls.at[u]) for u, src in sources.items()}
    place["tok"] = pltpu.make_async_copy(tok, T1.at[own], ls.at[OUT])
    place["cot"] = pltpu.make_async_copy(cot, SA.at[own], ls.at[DN0])
    for cp in place.values():
        cp.start()

    lanes = small_in[...].astype(F32)
    lanes = jnp.concatenate([lanes, jnp.zeros((16, 3 * ch - 128), F32)], axis=1)
    pack[...] = jnp.zeros_like(pack)
    pack[0:8, :] = pltpu.roll(lanes, dp_index * (ch // (z_size * x_size)), 1)[0:8, 0:ch]
    spread = pltpu.roll(lanes, dp_index * part, 1)
    for n in range(2):
        for k in range(3):
            pack[8 + 3 * n + k : 9 + 3 * n + k, :] = spread[8 + n : 9 + n, k * ch : (k + 1) * ch]
    gs[(0, *mine, slice(32, 48))] = pack[...].astype(BF)
    for n, src in enumerate((rec_in, inp_in)):
        for h in range(ch // 128):
            gs[(0, *mine, slice(16 * n, 16 * n + 16), slice(h * 128, (h + 1) * 128))] = src[h]
    if part % 128:
        W[(OUT, *mine)] = w_out[...]
        W[(DN0, *mine)] = w_down[:, :ch]
        W[(DN1, *mine)] = w_down[:, ch:]
    else:
        W[(OUT, *mine)] = w_out[...].T
        W[(DN0, *mine)] = w_down[:ch, :].T
        W[(DN1, *mine)] = w_down[ch:, :].T
    net.barrier()

    big = Gather(net, W, F_FLOW, ss, rs, True)
    small = Gather(net, gs, ("zxy",), sss, srs, False)
    tok_copy = pair_copy(net, tok, T1.at[own], ps, pr, 0)
    cot_copy = pair_copy(net, cot, SA.at[own], ps, pr, 1)
    tok_in = pair_copy(net, tok, T1.at[other], ps, pr, 0)
    cot_in = pair_copy(net, cot, SA.at[other], ps, pr, 1)
    mix_copy = pair_copy(net, PS, PR, ps, pr, 2)
    n2_copy = pair_copy(net, SA.at[own], SA.at[own], ps, pr, 3)
    n2_in = pair_copy(net, SA.at[other], SA.at[other], ps, pr, 3)
    out_copies = {}

    def send_out(name, src, dst):
        out_copies[name] = pltpu.make_async_copy(src, dst, outs.at[len(out_copies)])
        out_copies[name].start()

    waited = set()

    def sent(name):
        if name not in waited:
            waited.add(name)
            out_copies[name].wait()

    small.event(0, 0)
    tok_copy.start()
    cot_copy.start()
    for u in sources:
        place[u].wait()

    def pre1():
        place["tok"].wait()
        place["cot"].wait()
        cot_in.wait_recv()
        send_out("cot", SA, o_cot)
        transpose_into(SB, SA, SEQ)
        send_out("cott", SB, o_cott)
        small.event(0, 1)

    def pre2():
        RI[0:8, :] = jnp.zeros((8, y_size * ch), F32)
        tok_in.wait_recv()
        small.event(0, 2)

    def pre3():
        small.event(0, 3)
        join_params(gs, prm, gains, sizes)
        for yy in range(y_size):
            for n in range(2):
                hw[n, :, yy * ch : (yy + 1) * ch] = head_weight(gs, yy, 16 * n, group)

        @pl.loop(0, SEQ // 128)
        def _(i):
            v = T1[rows_of(i, 128), :].astype(F32)
            s = lax.rsqrt(jnp.mean(v * v, axis=1, keepdims=True) + EPS)
            N1[rows_of(i, 128), :] = (v * s * gains[0:1, :]).astype(BF)

        sent("cott")
        transpose_into(SB, N1, SEQ)
        send_out("n1t", SB, o_n1t)

    def full(u):
        return jnp.concatenate([W[u, yy].reshape(depth, ch) for yy in range(y_size)], axis=1)

    def unit_out(*units):
        for u in units:
            send_out(("w", u), W.at[u], o_w.at[u])

    def rnn():
        @pl.loop(0, SEQ // 512)
        def _(i):
            RI[pl.ds(pl.multiple_of(i * 512 + 8, 8), 512), :] = nn(N1[rows_of(i, 512), :], full(RNN))

        unit_out(RNN)
        send_out("ri", RI, o_ri)

    T = 128

    def branch(hook):
        def branch_tile(i, carries):
            hook(i)
            rows = rows_of(i, T)
            br = nn(N1[rows, :], full(GEL))
            new = []
            for yy in range(y_size):
                cols = slice(yy * ch, (yy + 1) * ch)
                p = prm[yy]
                x = RI[pl.ds(pl.multiple_of(i * T, T), T + 8), cols]
                cv = p[4:5] + p[0:1] * x[8:]
                for k in range(1, 4):
                    cv = cv + p[k : k + 1] * pltpu.roll(x, k, 0)[8:]
                cv_low = cv.astype(BF)
                CV[rows, cols] = cv_low
                cv = cv_low.astype(F32)
                rec, inp = [], []
                for h in range(ch // 128):
                    hc = slice(yy * ch + h * 128, yy * ch + (h + 1) * 128)
                    both = nn(cv_low[:, h * 128 : (h + 1) * 128], jnp.concatenate([hw[0, :, hc], hw[1, :, hc]], axis=1))
                    rec.append(both[:, :128])
                    inp.append(both[:, 128:])
                r = jax.nn.sigmoid(jnp.concatenate(rec, axis=1) + p[5:6])
                w = jax.nn.sigmoid(jnp.concatenate(inp, axis=1) + p[6:7])
                soft = jnp.log1p(jnp.exp(-jnp.abs(p[7:8]))) + jnp.maximum(p[7:8], 0.0)
                a = jnp.exp((-DECAY_SCALE * soft) * r)
                u = 1.0 - a * a + GUARD
                inv = lax.rsqrt(u)
                root = u * inv
                wc = w * cv
                state, last = scan_forward(a, root * wc, carries[yy])
                first = lax.broadcasted_iota(jnp.int32, (T, ch), 0) == 0
                prev = jnp.where(first, carries[yy], pltpu.roll(state, 1, 0))
                new.append(last)
                g, gp = gelu_parts(br[:, cols])
                LRU[rows, cols] = (state * g).astype(BF)
                cp = (prev - a * wc * inv) * a * r * (-DECAY_SCALE)
                A[rows, cols] = a
                C6[0, rows, cols] = g.astype(BF)
                C6[1, rows, cols] = (state * gp).astype(BF)
                C6[2, rows, cols] = cp.astype(BF)
                C6[3, rows, cols] = (cp * soft * (1.0 - r)).astype(BF)
                C6[4, rows, cols] = (root * wc * (1.0 - w)).astype(BF)
                C6[5, rows, cols] = (root * w).astype(BF)
            return tuple(new)

        lax.fori_loop(0, SEQ // T, branch_tile, tuple(jnp.zeros((1, ch), F32) for _ in range(y_size)))
        unit_out(GEL)
        send_out("cf", C6, o_cf)
        send_out("a", A, o_a)
        send_out("lru", LRU, o_lru)
        send_out("cv", CV, o_cv)

    def out_rows(rows):
        return nt(LRU[rows, :], full(OUT))

    def out():
        PS[...] = out_rows(other)
        sent("cot")
        sent("n1t")
        mix_copy.start()
        MIX[...] = out_rows(own)
        unit_out(OUT)

    def mix():
        mix_copy.wait_recv()

        @pl.loop(0, half // 128)
        def _(i):
            rows = rows_of(i, 128)
            v = tok[rows, :].astype(F32) + MIX[rows, :] + PR[rows, :]
            MIX[rows, :] = v
            s = lax.rsqrt(jnp.mean(v * v, axis=1, keepdims=True) + EPS)
            SA[pl.ds(pl.multiple_of(c * half + i * 128, 128), 128), :] = (v * s * gains[1:2, :]).astype(BF)

        n2_copy.start()
        send_out("mix", MIX, o_mix)

    def n2():
        n2_in.wait_recv()
        transpose_into(SB, SA, SEQ)
        send_out("n2t", SB, o_n2t)
        sent("cf")

    F = 256

    def ff(j):
        def loop(hook):
            @pl.loop(0, SEQ // F)
            def _(i):
                hook(i)
                rows = rows_of(i, F)
                up = nn(SA[rows, :], full(UP[j]))
                g, gp = gelu_parts(nn(SA[rows, :], full(GATE[j])))
                C6[j, rows, :] = (g * up).astype(BF)
                C6[2 + j, rows, :] = (gp * up).astype(BF)
                C6[4 + j, rows, :] = g.astype(BF)

            unit_out(GATE[j], UP[j])
        return loop

    run_plan(F_PLAN, {"pre1": (1, pre1), "pre2": (1, pre2), "pre3": (1, pre3), "rnn": (1, rnn), "br": (SEQ // T, branch),
                      "out": (1, out), "mix": (1, mix), "n2": (1, n2), "ffa": (SEQ // F, ff(0)), "ffb": (SEQ // F, ff(1))},
             big.event)
    send_out("c6", C6, o_c6)
    unit_out(DN0, DN1)
    for chunk in range(CHUNKS):
        big.drain(chunk)
    small.drain(0)
    for cp in (tok_copy, cot_copy, mix_copy, n2_copy):
        cp.wait_send()
    for name in out_copies:
        sent(name)


class Scatter:
    def __init__(self, net, ref, flows, bufs, ss, rs, halves):
        self.net, self.ref, self.flows, self.bufs, self.ss, self.rs, self.halves = net, ref, flows, bufs, ss, rs, halves

    def rows(self, c):
        return chunk_rows(c, self.ref.shape[4]) if self.halves else slice(None)

    def slot(self, c):
        return SLOT[c // 2] if self.halves else c

    def copy(self, c, s, j):
        order = self.flows[c]
        d = order[s]
        at = dict(self.net.at)
        at[d] = self.net.shifted(d, j)
        idx = [at[e] if e in order[: s + 1] else slice(None) for e in "yzx"]
        k = self.net.off[d] + j - 1
        return pltpu.make_async_remote_copy(
            src_ref=self.ref.at[(self.slot(c), *idx, self.rows(c))], dst_ref=self.bufs[c, s].at[j - 1],
            send_sem=self.ss.at[c, k], recv_sem=self.rs.at[c, k],
            device_id=self.net.device(d, j), device_id_type=MESH)

    def hops(self, c, s):
        return range(1, self.net.size[self.flows[c][s]])

    def add(self, c, s, out):
        order = self.flows[c]
        for j in self.hops(c, s):
            self.copy(c, s, j).wait_recv()
        rest = [e for e in "zyx" if e not in order[: s + 1]]
        buf = self.bufs[c, s]
        rows = self.rows(c)

        def block(place):
            idx = (self.slot(c), *[place[e] if e in place else self.net.at[e] for e in "yzx"], rows)
            total = self.ref[idx].astype(F32)
            for j in self.hops(c, s):
                total = total + buf[(j - 1, *[place[e] for e in "yzx" if e in place])].astype(F32)
            if s < 2:
                self.ref[idx] = total.astype(BF)
            elif self.halves:
                out[c // 2, rows] = total
            else:
                out[c] = total

        def over(names, place):
            if not names:
                block(place)
            elif names[0] == "z":
                @pl.loop(0, self.net.size["z"])
                def _(z):
                    over(names[1:], {**place, "z": z})
            else:
                for n in range(self.net.size[names[0]]):
                    over(names[1:], {**place, names[0]: n})

        over(rest, {})

    def event(self, c, k, out):
        if self.rows(c) is None:
            return
        if k:
            self.add(c, k - 1, out)
        if k < 3:
            for j in self.hops(c, k):
                self.copy(c, k, j).start()

    def drain(self, c):
        if self.rows(c) is None:
            return
        for s in range(3):
            for j in self.hops(c, s):
                self.copy(c, s, j).wait_send()


def landing(flows, sizes, rows, ch):
    size = dict(zip("zxy", sizes))
    shapes = {}
    for c, order in enumerate(flows):
        n = rows(c)
        for s in range(3):
            if n:
                rest = [size[e] for e in "yzx" if e not in order[: s + 1]]
                shapes[c, s] = (size[order[s]] - 1, *rest, n, ch)
    return shapes


SLOT = {DN0: 9, DN1: 10, GA0: DN0, GA1: DN1, UP0: GA0, UP1: GA1, OUT: UP0, GEL: UP1, RNN: OUT}


def big_landing(sizes, part, ch):
    def rows(c):
        cut = chunk_rows(c, part)
        return 0 if cut is None else len(range(part)[cut])

    return landing(B_FLOW, sizes, rows, ch)


def small_landing(sizes, ch):
    return landing(("yxz",), sizes, lambda c: SMALL, ch)


def backward_kernel(sizes, group,
                    w_h, cot_h, cott_h, n1t_h, n2t_h, c6_h, cf_h, a_h, ri_h, lru_h, cv_h, mix_h, tok_h, prm, gains, hw,
                    o_block, o_gtok, o_gw, o_gs,
                    W, C6, COT, TT, NT, GM, PS, PR, LRU, AS, RS, acc, GS, pgain,
                    ss, rs, sss, srs, ps, pr, ls, ast, rst, *landed):
    net = Net(*sizes)
    z_size, x_size, y_size = sizes
    c = net.at["c"]
    half = SEQ // 2
    ch = W.shape[-1]
    depth = COT.shape[1]
    own, other = pl.ds(pl.multiple_of(c * half, half), half), pl.ds(pl.multiple_of((1 - c) * half, half), half)
    loads = {}

    def load(name, src, dst):
        loads[name] = pltpu.make_async_copy(src, dst, ls.at[len(loads)])
        loads[name].start()

    def loaded(*names):
        for name in names:
            loads[name].wait()

    load("cott", cott_h, TT)
    load("h", c6_h.at[0:2], C6.at[0:2])
    load("cot", cot_h, COT)
    load("w_dn", w_h.at[DN0:], W.at[DN0:9])
    load("ab", c6_h.at[2:6], C6.at[2:6])
    load("mix", mix_h, GM)
    load("n2t", n2t_h, NT)
    load("w_ff", w_h.at[GA0:DN0], W.at[GA0:DN0])
    load("w_rnn", w_h.at[0:GA0], W.at[0:GA0])
    load("lru", lru_h, LRU)
    load("tok", tok_h, PS.at[1])
    net.barrier()
    shapes = big_landing(sizes, W.shape[4], ch)
    big = Scatter(net, W, B_FLOW, dict(zip(shapes, landed)), ss, rs, True)
    small = None
    if group == 1:
        tail = landed[len(shapes):]
        small = Scatter(net, GS, ("yxz",), dict(zip(small_landing(sizes, ch), tail)), sss, srs, False)

    def full(u):
        return jnp.concatenate([W[u, yy].reshape(depth, ch) for yy in range(y_size)], axis=1)

    zh = z_size // 2

    def weight_grad(u, left, right):
        @pl.loop(0, 2)
        def _(i):
            val = nn(left[rows_of(i, depth // 2), :], right[...]).astype(BF)
            for yy in range(y_size):
                W[SLOT[u], yy, pl.ds(i * zh, zh)] = val[:, yy * ch : (yy + 1) * ch].reshape(
                    zh, x_size, depth // (z_size * x_size), ch)

    F = 256
    base_own, base_other = c * half, (1 - c) * half
    back_copy = pair_copy(net, PS.at[0], PR.at[0], ps, pr, 0)
    row_copy = pair_copy(net, COT.at[own], COT.at[own], ps, pr, 1)
    row_in = pair_copy(net, COT.at[other], COT.at[other], ps, pr, 1)
    out_copy = pair_copy(net, PS.at[0], PR.at[1], ps, pr, 2)
    rnn_copy = pair_copy(net, PS.at[0], PR.at[0], ps, pr, 3)
    gain_copy = pair_copy(net, pgain.at[0:8], pgain.at[8:16], ps, pr, 4)
    block_copy = pltpu.make_async_copy(PR.at[1], o_block, ls.at[15])

    def d0():
        loaded("cott", "h")
        weight_grad(DN0, TT, C6.at[0])

    def d1():
        weight_grad(DN1, TT, C6.at[1])

    def gh(hook):
        loaded("cot", "w_dn", "ab")

        @pl.loop(0, 2 * (SEQ // F))
        def _(n):
            hook(n)
            j, i = n // (SEQ // F), lax.rem(n, SEQ // F)
            rows = rows_of(i, F)
            g = nn(COT[rows, :], full(DN0 + j))
            C6[2 + j, rows, :] = (g * C6[2 + j, rows, :].astype(F32)).astype(BF)
            C6[4 + j, rows, :] = (g * C6[4 + j, rows, :].astype(F32)).astype(BF)

    def span(base, i):
        return pl.ds(pl.multiple_of(base + i * F, F), F)

    def mlp_back(rows):
        return (nt(C6[2, rows, :], full(GA0)) + nt(C6[3, rows, :], full(GA1))
                + nt(C6[4, rows, :], full(UP0)) + nt(C6[5, rows, :], full(UP1)))

    def mlp_out(rows):
        return nt(C6[0, rows, :], full(DN0)) + nt(C6[1, rows, :], full(DN1))

    def rnn_back(rows):
        return nt(C6[5, rows, :], full(RNN)) + nt(C6[1, rows, :], full(GEL))

    def partial_rows(fn, base, dst, hook=None):
        @pl.loop(0, half // F)
        def _(i):
            if hook is not None:
                hook(i)
            dst[rows_of(i, F), :] = fn(span(base, i)).astype(dst.dtype)

    def bo():
        partial_rows(mlp_out, base_other, PS.at[0])
        out_copy.start()

    def bw():
        partial_rows(mlp_out, base_own, o_gtok)

    def gno(hook):
        loaded("w_ff", "mix")
        out_copy.wait_recv()

        @pl.loop(0, half // F)
        def _(i):
            rows = rows_of(i, F)
            PR[1, rows, :] = (GM[rows, :] + o_gtok[rows, :] + PR[1, rows, :].astype(F32)).astype(BF)

        block_copy.start()
        out_copy.wait_send()
        partial_rows(mlp_back, base_other, PS.at[0], hook)
        back_copy.start()

    def gnw(hook):
        partial_rows(mlp_back, base_own, o_gtok, hook)

    T = 128

    def norm():
        acc[...] = jnp.zeros_like(acc)
        pgain[...] = jnp.zeros_like(pgain)
        back_copy.wait_recv()

        @pl.loop(0, half // T)
        def _(i):
            rows = rows_of(i, T)
            at = pl.ds(pl.multiple_of(base_own + i * T, T), T)
            v = GM[rows, :]
            gn = o_gtok[rows, :] + PR[0, rows, :].astype(F32)
            s = lax.rsqrt(jnp.mean(v * v, axis=1, keepdims=True) + EPS)
            q = gn * gains[1:2, :]
            pgain[1:2, :] += jnp.sum(gn * v * s, axis=0, keepdims=True)
            gm = COT[at, :].astype(F32) + s * q - (s * s * s) * v * jnp.mean(q * v, axis=1, keepdims=True)
            o_gtok[rows, :] = gm
            COT[at, :] = gm.astype(BF)

        row_copy.start()

    def ga0():
        loaded("n2t")
        weight_grad(GA0, NT, C6.at[2])

    def ga1():
        weight_grad(GA1, NT, C6.at[3])

    def up0():
        weight_grad(UP0, NT, C6.at[4])

    def up1():
        weight_grad(UP1, NT, C6.at[5])
        load("n1t", n1t_h, NT)
        load("cf", cf_h, C6)

    tiles = SEQ // T

    def fetch(n, slot):
        at = (tiles - 1 - n) * T
        return (
            pltpu.make_async_copy(a_h.at[pl.ds(pl.multiple_of(at, T), T)], AS.at[slot], ast.at[slot]),
            pltpu.make_async_copy(ri_h.at[pl.ds(pl.multiple_of(at, T), T + 8)], RS.at[slot], rst.at[slot]),
        )

    def outg():
        row_in.wait_recv()
        loaded("w_rnn", "lru")
        transpose_into(TT, COT, SEQ)
        weight_grad(OUT, TT, LRU)
        load("cv", cv_h, LRU)
        for cp in fetch(0, 0):
            cp.start()
        loaded("cf")

    def back(hook):
        def back_tile(n, carries):
            hook(n)
            slot = lax.rem(n, 2)
            for cp in fetch(n, slot):
                cp.wait()

            @pl.when(n + 1 < tiles)
            def _():
                for cp in fetch(n + 1, 1 - slot):
                    cp.start()

            i = tiles - 1 - n
            rows = rows_of(i, T)
            gl_all = nn(COT[rows, :], full(OUT))
            new = []
            for yy in range(y_size):
                adj_next, a_next, gco_next = carries[yy]
                cols = slice(yy * ch, (yy + 1) * ch)
                p = prm[yy]
                gl = gl_all[:, cols]
                at = AS[slot, :, cols]
                last = lax.broadcasted_iota(jnp.int32, (T, ch), 0) == T - 1
                shifted = jnp.where(last, a_next, pltpu.roll(at, T - 1, 0))
                adj, adj_first = scan_backward(shifted, gl * C6[0, rows, cols].astype(F32), adj_next)
                C6[1, rows, cols] = (gl * C6[1, rows, cols].astype(F32)).astype(BF)
                grp = adj * C6[3, rows, cols].astype(F32)
                gip = adj * C6[4, rows, cols].astype(F32)
                gr_low, gi_low = grp.astype(BF), gip.astype(BF)
                gcd = adj * C6[5, rows, cols].astype(F32)
                acc[yy, 5:6] += jnp.sum(grp, axis=0, keepdims=True)
                acc[yy, 6:7] += jnp.sum(gip, axis=0, keepdims=True)
                acc[yy, 7:8] += jnp.sum(adj * C6[2, rows, cols].astype(F32), axis=0, keepdims=True)
                C6[3, rows, cols] = gr_low
                C6[4, rows, cols] = gi_low
                parts = []
                for h in range(ch // 128):
                    hs = slice(h * 128, (h + 1) * 128)
                    hc = slice(yy * ch + h * 128, yy * ch + (h + 1) * 128)
                    parts.append(nt(jnp.concatenate([gr_low[:, hs], gi_low[:, hs]], axis=1),
                                    jnp.concatenate([hw[0, :, hc], hw[1, :, hc]], axis=1)))
                gco = gcd + jnp.concatenate(parts, axis=1)
                ext = jnp.concatenate([gco, gco_next], axis=0)
                x = RS[slot, :, cols]
                grn = p[0:1] * gco
                acc[yy, 0:1] += jnp.sum(gco * x[8:], axis=0, keepdims=True)
                acc[yy, 4:5] += jnp.sum(gco, axis=0, keepdims=True)
                for k in range(1, 4):
                    grn = grn + p[k : k + 1] * pltpu.roll(ext, T + 8 - k, 0)[:T]
                    acc[yy, k : k + 1] += jnp.sum(gco * pltpu.roll(x, k, 0)[8:], axis=0, keepdims=True)
                C6[5, rows, cols] = grn.astype(BF)
                new.append((adj_first, at[0:1], gco[0:8]))
            return tuple(new)

        zero = (jnp.zeros((1, ch), F32), jnp.zeros((1, ch), F32), jnp.zeros((8, ch), F32))
        lax.fori_loop(0, tiles, back_tile, (zero,) * y_size)
        loaded("n1t")

    def gel():
        weight_grad(GEL, NT, C6.at[1])

    def rnn():
        weight_grad(RNN, NT, C6.at[5])

    def gn1o():
        loaded("tok")
        back_copy.wait_send()
        partial_rows(rnn_back, base_other, PS.at[0])
        rnn_copy.start()

    def gn1w():
        partial_rows(rnn_back, base_own, GM)

    def heads():
        loaded("cv")
        for yy in range(y_size):
            acc[yy, 7:8] = acc[yy, 7:8] * jax.nn.sigmoid(prm[yy, 7:8])
            for h in range(ch // 128):
                hs = slice(h * 128, (h + 1) * 128)
                hc = slice(yy * ch + h * 128, yy * ch + (h + 1) * 128)
                both = lax.dot_general(LRU[:, hc], jnp.concatenate([C6[3, :, hc], C6[4, :, hc]], axis=1),
                                       (((0,), (0,)), ((), ())), preferred_element_type=F32)
                for n in range(2):
                    val = both[:, n * 128 : (n + 1) * 128]
                    if group > 1:
                        o_gs[yy, 128 * n : 128 * n + 128, hs] = val
                    else:
                        GS[0, yy, :, :, 16 * n : 16 * n + 16, hs] = val.astype(BF).reshape(z_size, x_size, 16, 128)

    def fin():
        rnn_copy.wait_recv()

        @pl.loop(0, half // T)
        def _(i):
            rows = rows_of(i, T)
            v = PS[1, rows, :].astype(F32)
            gn = GM[rows, :] + PR[0, rows, :].astype(F32)
            s = lax.rsqrt(jnp.mean(v * v, axis=1, keepdims=True) + EPS)
            q = gn * gains[0:1, :]
            pgain[0:1, :] += jnp.sum(gn * v * s, axis=0, keepdims=True)
            o_gtok[rows, :] += s * q - (s * s * s) * v * jnp.mean(q * v, axis=1, keepdims=True)

        gain_copy.start()

    def small_step(k):
        def fn():
            if k == 0:
                gain_copy.wait_recv()
                for n in range(2):
                    row = pgain[n : n + 1, :] + pgain[8 + n : 9 + n, :]
                    row = jnp.concatenate([row, jnp.zeros((1, 3 * ch - depth), F32)], axis=1)
                    for m in range(3):
                        for yy in range(y_size):
                            acc[yy, 8 + 3 * n + m : 9 + 3 * n + m, :] = row[:, m * ch : (m + 1) * ch]
                if group > 1:
                    for yy in range(y_size):
                        o_gs[yy, 256:272, :] = acc[yy]
                    return

                @pl.loop(0, z_size)
                def _(z):
                    for yy in range(y_size):
                        for xx in range(x_size):
                            GS[0, yy, z, xx, 32:48, :] = acc[yy].astype(BF)

            if group == 1:
                small.event(0, k, o_gs)
        return fn

    blocks = dict(d0=d0, d1=d1, bo=bo, bw=bw, ga0=ga0, ga1=ga1, norm=norm, up0=up0, up1=up1, outg=outg, gel=gel, rnn=rnn,
                  gn1o=gn1o, gn1w=gn1w, heads=heads, fin=fin)
    blocks = {name: (1, fn) for name, fn in blocks.items()}
    for k in range(4):
        blocks["s" + str(k)] = (1, small_step(k))
    blocks.update(gh=(2 * SEQ // F, gh), gno=(half // F, gno), gnw=(half // F, gnw), t=(tiles, back))
    run_plan(B_PLAN, blocks, lambda chunk, k: big.event(chunk, k, o_gw))
    for chunk in range(CHUNKS):
        big.drain(chunk)
    if group == 1:
        small.drain(0)
    for cp in (row_copy, rnn_copy, gain_copy):
        cp.wait_send()
    block_copy.wait()


def finish_kernel(sizes, block_in, gtok_in, gw, gs,
                  o_block, o_gtok, o_mg, o_rnn, o_gel, o_cw, o_cb, o_rw, o_iw, o_rb, o_ib, o_dp, o_out, o_lg, o_gate, o_up,
                  o_down):
    ch = gw.shape[2]
    dp = sizes[0] * sizes[1]
    part, own = o_mg.shape[1], ch // dp
    dp_index = lax.axis_index("dp")
    o_block[...] = block_in[...]
    o_gtok[...] = gtok_in[...]
    o_rnn[...] = gw[RNN]
    o_gel[...] = gw[GEL]
    o_out[...] = gw[OUT].T
    for j in range(2):
        cols = slice(j * ch, (j + 1) * ch)
        o_gate[:, cols] = gw[GATE[j]]
        o_up[:, cols] = gw[UP[j]]
        o_down[cols, :] = gw[DOWN[j]].T
    for h in range(ch // 128):
        o_rw[h] = gs[0, 0:16, h * 128 : (h + 1) * 128]
        o_iw[h] = gs[0, 16:32, h * 128 : (h + 1) * 128]
    rows = pltpu.roll(gs[0, 32:40, :], ch - dp_index * own, 1)
    o_cw[...] = rows[0:4, 0:own]
    for k, ref in ((4, o_cb), (5, o_rb), (6, o_ib), (7, o_dp)):
        ref[...] = rows[k : k + 1, 0:own]
    for n, ref in ((0, o_mg), (1, o_lg)):
        row = jnp.concatenate([gs[0, 40 + 3 * n + k : 41 + 3 * n + k, :] for k in range(3)], axis=1)
        row = jnp.broadcast_to(row, (8, 3 * ch))
        ref[...] = pltpu.roll(row, 3 * ch - dp_index * part, 1)[0:1, 0:part]


def any_spec():
    return pl.BlockSpec(memory_space=pl.ANY)


def vmem_spec():
    return pl.BlockSpec(memory_space=pltpu.VMEM)


def body(sizes, tokens, mix_gain, rnn_weight, gelu_weight, conv_weight, conv_bias, recur_weight, input_weight,
         recur_bias, input_bias, decay_param, out_weight, mlp_gain, gate_weight, up_weight, down_weight, cotangent):
    z_size, x_size, y_size = sizes
    dp = z_size * x_size
    dp_index = lax.axis_index("dp")
    rows, depth = tokens.shape
    part, ch = rnn_weight.shape
    head_rows = recur_weight.shape[1]
    group = max(1, 16 // head_rows)
    wide = y_size * ch
    own = ch // dp
    small_in = jnp.concatenate([conv_weight, conv_bias[None], recur_bias[None], input_bias[None], decay_param[None]], axis=0)
    small_in = jnp.concatenate([jnp.pad(small_in, ((0, 0), (0, 128 - own))),
                                jnp.pad(jnp.stack([mix_gain, mlp_gain]), ((0, 6), (0, 128 - part)))], axis=0)
    heads = [recur_weight, input_weight]
    out_w, down_w = out_weight, down_weight
    if part % 128:
        out_w, down_w = out_weight.T, down_weight.T
    if group > 1:
        heads = [lax.dynamic_update_slice(jnp.zeros((w.shape[0], 16, 128), BF), w, (0, lax.rem(dp_index * head_rows, 16), 0))
                 for w in heads]
    shape = jax.ShapeDtypeStruct
    grid = (y_size, z_size, x_size)
    hops = z_size + x_size + y_size - 3
    f_out = [
        shape((UNITS, *grid, part, ch), BF), shape((SEQ, depth), BF), shape((depth, SEQ), BF),
        shape((depth, SEQ), BF), shape((depth, SEQ), BF), shape((6, SEQ, wide), BF), shape((6, SEQ, wide), BF),
        shape((SEQ, wide), F32), shape((SEQ + 8, wide), F32), shape((SEQ, wide), BF), shape((SEQ, wide), BF),
        shape((rows, depth), F32), shape((y_size, 16, ch), F32), shape((8, depth), F32), shape((2, 128, wide), BF),
    ]
    dma = pltpu.SemaphoreType.DMA
    kept = pl.pallas_call(
        functools.partial(forward_kernel, sizes, group),
        out_shape=f_out,
        in_specs=[vmem_spec(), any_spec(), any_spec(), any_spec(), vmem_spec(), any_spec(), any_spec(), vmem_spec(),
                  vmem_spec(), vmem_spec(), vmem_spec()],
        out_specs=[any_spec()] * 12 + [vmem_spec()] * 3,
        scratch_shapes=[
            pltpu.VMEM((UNITS, *grid, part, ch), BF), pltpu.VMEM((1, *grid, SMALL, ch), BF),
            pltpu.VMEM((SEQ, depth), BF), pltpu.VMEM((SEQ, depth), BF), pltpu.VMEM((depth, SEQ), BF),
            pltpu.VMEM((SEQ, depth), BF), pltpu.VMEM((SEQ + 8, wide), F32), pltpu.VMEM((SEQ, wide), F32),
            pltpu.VMEM((SEQ, wide), BF), pltpu.VMEM((6, SEQ, wide), BF), pltpu.VMEM((SEQ, wide), BF),
            pltpu.VMEM((rows, depth), F32), pltpu.VMEM((rows, depth), F32), pltpu.VMEM((rows, depth), F32),
            pltpu.VMEM((16, ch), F32),
            dma((CHUNKS, hops)), dma((CHUNKS, hops)), dma((1, hops)), dma((1, hops)), dma((4,)), dma((4,)), dma((9,)),
            dma((24,)),
        ],
        compiler_params=pltpu.CompilerParams(collective_id=0, has_side_effects=True, vmem_limit_bytes=VMEM_LIMIT),
        name="gather_forward",
    )(tokens, cotangent, rnn_weight, gelu_weight, out_w, gate_weight, up_weight, down_w, small_in, *heads)
    landed = list(big_landing(sizes, part, ch).values())
    gs_shape, small_grid = (y_size, 272, ch), (1, 1, 1)
    if group == 1:
        landed += list(small_landing(sizes, ch).values())
        gs_shape, small_grid = (1, SMALL, ch), grid
    block_out, grad_tokens, gw, gs = pl.pallas_call(
        functools.partial(backward_kernel, sizes, group),
        out_shape=[shape((rows, depth), BF), shape((rows, depth), F32), shape((UNITS, part, ch), F32), shape(gs_shape, F32)],
        in_specs=[any_spec()] * 13 + [vmem_spec()] * 3,
        out_specs=[any_spec()] + [vmem_spec()] * 3,
        scratch_shapes=[
            pltpu.VMEM((UNITS + 2, *grid, part, ch), BF), pltpu.VMEM((6, SEQ, wide), BF), pltpu.VMEM((SEQ, depth), BF),
            pltpu.VMEM((depth, SEQ), BF), pltpu.VMEM((depth, SEQ), BF), pltpu.VMEM((rows, depth), F32),
            pltpu.VMEM((2, rows, depth), BF), pltpu.VMEM((2, rows, depth), BF), pltpu.VMEM((SEQ, wide), BF),
            pltpu.VMEM((2, 128, wide), F32), pltpu.VMEM((2, 136, wide), F32), pltpu.VMEM((y_size, 16, ch), F32),
            pltpu.VMEM((1, *small_grid, SMALL, ch), BF), pltpu.VMEM((16, depth), F32),
            dma((CHUNKS, hops)), dma((CHUNKS, hops)), dma((1, hops)), dma((1, hops)),
            dma((5,)), dma((5,)), dma((16,)), dma((2,)), dma((2,)),
            *[pltpu.VMEM(s, BF) for s in landed],
        ],
        compiler_params=pltpu.CompilerParams(collective_id=1, has_side_effects=True, vmem_limit_bytes=VMEM_LIMIT),
        name="backward_scatter",
    )(*kept[:12], tokens, *kept[12:])
    if group > 1:
        t = lax.axis_index("tensor")
        every = jnp.zeros((2 * y_size, 272, ch), F32)
        for yy in range(y_size):
            every = lax.dynamic_update_slice(every, gs[yy : yy + 1], (2 * yy + lax.rem(t, 2), 0, 0))
        gs = lax.dynamic_slice(lax.psum(every, ("dp", "tensor")), (t, 0, 0), (1, 272, ch))
        first = dp_index * head_rows
        rec = lax.dynamic_slice(gs[0], (first, 0), (head_rows, ch))
        inp = lax.dynamic_slice(gs[0], (128 + first, 0), (head_rows, ch))
        fill = jnp.zeros((16 - head_rows, ch), F32)
        gs = jnp.concatenate([rec, fill, inp, fill, gs[0, 256:]], axis=0)[None]
    f_shapes = [
        shape((rows, depth), BF), shape((rows, depth), F32), shape((1, part), F32), shape((part, ch), F32),
        shape((part, ch), F32), shape((4, own), F32), shape((1, own), F32), shape((ch // 128, 16, 128), F32),
        shape((ch // 128, 16, 128), F32), shape((1, own), F32), shape((1, own), F32), shape((1, own), F32),
        shape((ch, part), F32), shape((1, part), F32), shape((part, 2 * ch), F32), shape((part, 2 * ch), F32),
        shape((2 * ch, part), F32),
    ]
    res = list(pl.pallas_call(
        functools.partial(finish_kernel, sizes),
        out_shape=f_shapes,
        in_specs=[vmem_spec()] * 4,
        out_specs=[vmem_spec()] * 17,
        compiler_params=pltpu.CompilerParams(vmem_limit_bytes=VMEM_LIMIT),
        name="unpack",
    )(block_out, grad_tokens, gw, gs))
    for k in (2, 6, 9, 10, 11, 13):
        res[k] = res[k][0]
    for k in (7, 8):
        res[k] = res[k][:, :head_rows]
    return tuple(res)


def solution(mesh):
    dp, tensor = mesh.shape["dp"], mesh.shape["tensor"]
    x_size = 2
    sizes = (dp // x_size, x_size, tensor // 2)
    rows, split, vec = P(("dp", "tensor"), None), P("dp", "tensor"), P(("tensor", "dp"))
    head, flip, taps = P("tensor", "dp", None), P("tensor", "dp"), P(None, ("tensor", "dp"))
    return jax.shard_map(
        functools.partial(body, sizes),
        mesh=mesh,
        in_specs=(rows, P("dp"), split, split, taps, vec, head, head, vec, vec, vec, flip, P("dp"), split, split, flip,
                  rows),
        out_specs=(rows, rows, P("dp"), split, split, taps, vec, head, head, vec, vec, vec, flip, P("dp"), split, split,
                   flip),
        check_vma=False,
    )
```

time: 377 us -> 276 us (0.73)
  Pallas kernels: 348 us -> 273 us
  local copies, waits for them, and re-layouts: 22.7 us -> 0.74 us
    pallas_call x1, Pallas kernels: 185 us -> 135 us  [body(): pl.pallas_call(functools.partial(backward_kernel, sizes, group), out_shap...]
    pallas_call x1, Pallas kernels: 163 us -> 133 us  [body(): pl.pallas_call(functools.partial(forward_kernel, sizes, group), out_shape...]
    unnamed x31 -> x0, local copies, waits for them, and re-layouts: 11.2 us -> none
    pallas_call x0 -> x1, Pallas kernels: none -> 5 us  [body(): pl.pallas_call(functools.partial(finish_kernel, sizes), out_shape=f_shape...]
where the time goes in v2:
time: 276 us
  Pallas kernels  273 us (99%)
    pallas_call x1, Pallas kernels, body(): pl.pallas_call(functools.partial(backward_kernel, sizes, group), out_shap...  135 us
    pallas_call x1, Pallas kernels, body(): pl.pallas_call(functools.partial(forward_kernel, sizes, group), out_shape...  133 us

profile of v2, /device:TPU:0, one launch (start us, length us, event | category | flops | bytes accessed | tf_op | source)
XLA Modules:
  0.0 276.1 jit_solution(17214260833286682449)
XLA Ops:
  0.7 0.7 fusion.4
  1.3 0.7 concatenate.6
  2.1 0.6 fusion.1.small_in
  2.7 132.9 %gather_forward.1 = (bf16[9,2,4,2,128,384]{5,4,3,2,1,0:T(8,128)(2,1)}, bf16[1024,1024]{1,0:T(8,128)(2,1)}, bf16[1024,1024]{1,0:T(8,128)(2,1)}, bf16[1024,1024]{1...) custom-call(bf16[512,1024]{1,0:T(8,128)(2,1)} %tok_h.1, ...), custom_call_target="tpu_custom_call" | custom-call | tf_op jit(solution)/shard_map/gather_forward/pallas_call | solution.py:974
  135.6 135.4 %backward_scatter.1 = (bf16[512,1024]{1,0:T(8,128)(2,1)}, f32[512,1024]{1,0:T(8,128)}, f32[9,128,384]{2,1,0:T(8,128)}, f32[1,48,384]{2,1,0:T(8,128)}) custom-call(bf16[9,2,4,2,128,384]{5,4,3,2,1,0:T(8,128)(2,1)} %get-tuple-element.53.w_h, bf16[1024,1024]{1,0:T(8,128)(2,1)} %get-tuple-element.54.cot_h, bf16[1024,1024]{1,0:T(8,128)(2,1)} %get-tuple-element.55.cott_h, ...), custom_call_target="tpu_custom_call" | custom-call | tf_op jit(solution)/shard_map/backward_scatter/pallas_call | solution.py:998
  271.0 5.0 %unpack.1 = (bf16[512,1024]{1,0:T(8,128)(2,1)}, f32[512,1024]{1,0:T(8,128)}, f32[1,128]{1,0:T(1,128)}, f32[128,384]{1,0:T(8,128)}, f32[128,384]{1,0:T(8,128)}, /...) custom-call(bf16[512,1024]{1,0:T(8,128)(2,1)} %get-tuple-element.68., ...), custom_call_target="tpu_custom_call" | custom-call | tf_op jit(solution)/shard_map/unpack/pallas_call | solution.py:1034

commit v3 on v2

v3 whole, which is shorter than its diff:
```python
import functools

import jax
import jax.numpy as jnp
from jax import lax
from jax.experimental import pallas as pl
from jax.experimental.pallas import tpu as pltpu
from jax.sharding import PartitionSpec as P

SEQ = 1024
EPS = 1e-06
GUARD = 0.01
DECAY_SCALE = 8.0
GELU_K = 0.7978845608028654
GELU_C = 0.044715
BF = jnp.bfloat16
F32 = jnp.float32
MESH = pl.DeviceIdType.MESH
VMEM_LIMIT = 63 * 1024 * 1024

RNN, GEL, OUT, GA0, UP0, GA1, UP1, DN0, DN1 = range(9)
UNITS = 9
GATE, UP, DOWN = (GA0, GA1), (UP0, UP1), (DN0, DN1)
CHUNKS = 2 * UNITS
SMALL = 48
FLOW = (
    "zxy", "zyx", "zxy", "zyx", "zxy", "yxz", "zxy", "xzy", "yzx", "zyx", "zyx", "zxy", "zyx", "xyz", "zyx", "xzy",
    "zyx", "xyz",
)
BACK = (
    "xyz", "xzy", "yxz", "yxz", "yxz", "yzx", "xzy", "yxz", "xzy", "yxz", "yxz", "xzy", "zyx", "xyz", "zxy", "xzy",
    "yzx", "zyx",
)
PLAN = (
    15, 75, 85, 40, 0, 65, 25, 66, 19, 86, 5, "pre1", "pre2", 26, "pre25", 4, 10, 9, "pre3", 30, 16, 1, 6, 35, 14,
    41, 11, 2, 7, 34, 20, 60, 17, 44, 12, 50, 64, 24, 45, 21, 61, 54, 55, 49, 80, 46, 31, 8, 3, 18, 13, 70, "br", 51,
    42, 59, 36, "br", 22, 47, 27, "br", "br", 84, 56, 32, "br", 39, 74, "br", 76, "br", 52, 37, 71, "br", 48, 62, 33,
    23, 29, 79, 67, 28, "out", "mix", 38, "n2", 43, 57, "ffa", "ffa", 69, 81, 87, 53, 72, 77, "ffa", "ffa", "d0",
    160, 63, 68, 58, "ffb", 82, "ffb", "ffb", "ffb", 89, "d1", 170, 165, 164, 73, 78, 175, 88, 83, "gh", "gh", "gh",
    "gh", "gh", "gh", "gh", "gh", "bo", "bw", "ga0", 120, 166, 171, 125, 179, "ga1", 145, 140, "gno", "gno", 169,
    "gnw", "gnw", 121, 174, "norm", "up0", 130, 135, "up1", 146, "outg", 124, 110, 126, 150, "t", 155, "t", "t", 115,
    "t", 141, 154, 149, "t", "t", 111, 131, "t", 156, 136, "t", 142, "gel", 134, 100, 127, 112, "rnn", 105, 95, 137,
    90, 144, "gn1o", 122, 129, 167, 157, 114, "gn1w", 116, "heads", 113, 101, 159, 143, 139, 161, 96, 176, "fin", 91,
    "s0", 106, 119, 99, 132, 123, 128, "s1", 102, 151, 168, 177, 92, 162, 172, "s2", 117, 104, 97, 147, 107, 94, 138,
    "sr", 152, 178, 173, 158, 133, 163, 109, "s3", 103, 98, 153, 148, 93, 118, 108,
)


def run_plan(plan, blocks, event):
    i = 0
    while i < len(plan):
        name = plan[i]
        i += 1
        if isinstance(name, int):
            event(name // 5, name % 5)
            continue
        turns, fn = blocks[name]
        if turns == 1:
            fn()
            continue
        hooks = {}
        for turn in range(1, turns):
            hooks[turn] = []
            while isinstance(plan[i], int):
                hooks[turn].append(plan[i])
                i += 1
            i += 1

        def hook(n, hooks=hooks):
            for turn, steps in hooks.items():
                if steps:
                    @pl.when(n == turn)
                    def _(steps=steps):
                        for step in steps:
                            event(step // 5, step % 5)

        fn(hook)


def nn(a, b):
    return jnp.dot(a, b, preferred_element_type=F32)


def nt(a, b):
    return lax.dot_general(a, b, (((1,), (1,)), ((), ())), preferred_element_type=F32)


def gelu_parts(v):
    v2 = v * v
    th = jnp.tanh(GELU_K * v * (1.0 + GELU_C * v2))
    half = 0.5 * (1.0 + th)
    return v * half, half + (0.5 * GELU_K) * v * (1.0 - th * th) * (1.0 + (3.0 * GELU_C) * v2)


class Net:
    def __init__(self, z_size, x_size, y_size):
        self.size = {"z": z_size, "x": x_size, "y": y_size, "c": 2}
        dp, t = lax.axis_index("dp"), lax.axis_index("tensor")
        self.at = {"z": dp // x_size, "x": lax.rem(dp, x_size), "y": t // 2, "c": lax.rem(t, 2)}
        self.off = {"z": 0, "x": z_size - 1, "y": z_size + x_size - 2}
        self.relay = z_size + x_size + y_size - 3 if z_size == 4 else None

    def shifted(self, d, j):
        n = self.size[d]
        return lax.rem(self.at[d] + (j % n), n)

    def device(self, d, j):
        at = dict(self.at)
        at[d] = self.shifted(d, j)
        return (at["z"] * self.size["x"] + at["x"], at["y"] * 2 + at["c"])

    def barrier(self):
        sem = pltpu.get_barrier_semaphore()
        count = 0
        for d in "zxyc":
            for j in range(1, self.size[d]):
                pl.semaphore_signal(sem, inc=1, device_id=self.device(d, j), device_id_type=MESH)
                count += 1
        pl.semaphore_wait(sem, count)


def chunk_rows(c, part):
    if part % 32:
        return slice(None) if c % 2 == 0 else None
    return slice(c % 2 * (part // 2), (c % 2 + 1) * (part // 2))


class Gather:
    def __init__(self, net, ref, flows, ss, rs, halves):
        self.net, self.ref, self.flows, self.ss, self.rs, self.halves = net, ref, flows, ss, rs, halves

    def region(self, c, s, at):
        order = self.flows[c]
        idx = [slice(None) if d in order[:s] else at[d] for d in "yzx"]
        if not self.halves:
            return self.ref.at[(c, *idx)]
        return self.ref.at[(c // 2, *idx, chunk_rows(c, self.ref.shape[4]))]

    def copy(self, c, s, j, sender, origin=None, send=None, recv=None):
        d = self.flows[c][s]
        at = dict(self.net.at)
        if sender:
            at[d] = self.net.shifted(d, -j)
        if origin is not None:
            at[d] = origin
        region = self.region(c, s, at)
        k = self.net.off[d] + j - 1
        return pltpu.make_async_remote_copy(
            src_ref=region, dst_ref=region, send_sem=self.ss.at[c, k if send is None else send],
            recv_sem=self.rs.at[c, k if recv is None else recv], device_id=self.net.device(d, j), device_id_type=MESH)

    def relayed(self, c, s):
        return self.net.relay is not None and self.flows[c][s] == "z"

    def sends(self, c, s, act):
        if not self.relayed(c, s):
            for j in range(1, self.net.size[self.flows[c][s]]):
                act(self.copy(c, s, j, False))
            return
        z = self.net.at["z"]
        act(self.copy(c, s, 2, False))
        pl.when(z != 3)(lambda: act(self.copy(c, s, 1, False)))
        pl.when(z != 0)(lambda: act(self.copy(c, s, 3, False)))

    def passes_on(self, c, s, act):
        z = self.net.at["z"]
        k = self.net.relay
        pl.when(z == 2)(lambda: act(self.copy(c, s, 1, False, 0, k, 2)))
        pl.when(z == 1)(lambda: act(self.copy(c, s, 3, False, 3, k, 0)))

    def event(self, c, k):
        if self.halves and chunk_rows(c, self.ref.shape[4]) is None:
            return
        if k == 4:
            s = self.flows[c].index("z")
            if self.relayed(c, s):
                self.copy(c, s, 2, True).wait_recv()
                self.passes_on(c, s, lambda cp: cp.start())
            return
        if k:
            for j in range(1, self.net.size[self.flows[c][k - 1]]):
                if not (self.relayed(c, k - 1) and j == 2):
                    self.copy(c, k - 1, j, True).wait_recv()
        if k < 3:
            self.sends(c, k, lambda cp: cp.start())

    def drain(self, c):
        if self.halves and chunk_rows(c, self.ref.shape[4]) is None:
            return
        for s in range(3):
            self.sends(c, s, lambda cp: cp.wait_send())
            if self.relayed(c, s):
                self.passes_on(c, s, lambda cp: cp.wait_send())


def pair_copy(net, src, dst, ss, rs, k):
    return pltpu.make_async_remote_copy(
        src_ref=src, dst_ref=dst, send_sem=ss.at[k], recv_sem=rs.at[k],
        device_id=net.device("c", 1), device_id_type=MESH)


def scan_forward(a, b, carry):
    rows, cols = a.shape
    a = a.reshape(rows // 8, 8, cols)
    b = b.reshape(rows // 8, 8, cols)
    place = lax.broadcasted_iota(jnp.int32, (rows // 8, 8, cols), 1)
    for k in (1, 2, 4):
        keep = place >= k
        b = b + a * jnp.where(keep, pltpu.roll(b, k, 1), 0.0)
        a = a * jnp.where(keep, pltpu.roll(a, k, 1), 1.0)
    out = []
    for g in range(rows // 8):
        s = b[g] + a[g] * carry
        out.append(s)
        carry = s[7:8]
    return jnp.concatenate(out, axis=0), carry


def scan_backward(a, b, carry):
    rows, cols = a.shape
    a = a.reshape(rows // 8, 8, cols)
    b = b.reshape(rows // 8, 8, cols)
    place = lax.broadcasted_iota(jnp.int32, (rows // 8, 8, cols), 1)
    for k in (1, 2, 4):
        keep = place < 8 - k
        b = b + a * jnp.where(keep, pltpu.roll(b, 8 - k, 1), 0.0)
        a = a * jnp.where(keep, pltpu.roll(a, 8 - k, 1), 1.0)
    out = []
    for g in reversed(range(rows // 8)):
        s = b[g] + a[g] * carry
        out.append(s)
        carry = s[0:1]
    return jnp.concatenate(out[::-1], axis=0), carry


def rows_of(i, n):
    return pl.ds(pl.multiple_of(i * n, n), n)


def join_params(gs, prm, gains, sizes):
    y_size = sizes[2]
    for yy in range(y_size):
        prm[yy] = jnp.sum(gs[0, yy, :, :, 32:48, :].astype(F32), axis=(0, 1))
    d = gains.shape[1]
    for n in range(2):
        row = jnp.concatenate([prm[0, 8 + 3 * n + k : 9 + 3 * n + k, :] for k in range(3)], axis=1)
        gains[n : n + 1, :] = row[:, :d]


def head_weight(gs, yy, first):
    blocks = gs[0, yy, :, :, first : first + 16, :]
    return blocks.reshape(-1, blocks.shape[-1])


def transpose_into(dst, src, n, step=256):
    @pl.loop(0, n // step)
    def _(i):
        dst[:, rows_of(i, step)] = src[rows_of(i, step), :].T


class Scatter:
    def __init__(self, net, ref, flows, bufs, ss, rs, halves):
        self.net, self.ref, self.flows, self.bufs, self.ss, self.rs, self.halves = net, ref, flows, bufs, ss, rs, halves

    def rows(self, c):
        return chunk_rows(c, self.ref.shape[4]) if self.halves else slice(None)

    def slot(self, c):
        return SLOT[c // 2] if self.halves else c

    def copy(self, c, s, j, owner=None, slot=None, k=None):
        order = self.flows[c]
        d = order[s]
        at = dict(self.net.at)
        at[d] = self.net.shifted(d, j) if owner is None else owner
        idx = [at[e] if e in order[: s + 1] else slice(None) for e in "yzx"]
        k = self.net.off[d] + j - 1 if k is None else k
        return pltpu.make_async_remote_copy(
            src_ref=self.ref.at[(self.slot(c), *idx, self.rows(c))], dst_ref=self.bufs[c, s].at[j - 1 if slot is None else slot],
            send_sem=self.ss.at[c, k], recv_sem=self.rs.at[c, k],
            device_id=self.net.device(d, j), device_id_type=MESH)

    def relayed(self, c, s):
        return self.net.relay is not None and self.flows[c][s] == "z"

    def hops(self, c, s):
        return range(1, self.net.size[self.flows[c][s]])

    def far(self, c, s, act):
        z = self.net.at["z"]
        pl.when(z == 3)(lambda: act(self.copy(c, s, 3, 0, 3, self.net.relay)))
        pl.when(z == 0)(lambda: act(self.copy(c, s, 1, 3, 3, self.net.relay)))

    def sends(self, c, s, act):
        if not self.relayed(c, s):
            for j in self.hops(c, s):
                act(self.copy(c, s, j))
            return
        z = self.net.at["z"]
        self.far(c, s, act)
        pl.when(jnp.logical_or(z == 0, z == 3))(lambda: act(self.copy(c, s, 2)))
        pl.when(z != 3)(lambda: act(self.copy(c, s, 1)))
        pl.when(z != 0)(lambda: act(self.copy(c, s, 3)))

    def over(self, names, fn, place):
        if not names:
            fn(place)
        elif names[0] == "z":
            @pl.loop(0, self.net.size["z"])
            def _(z):
                self.over(names[1:], fn, {**place, "z": z})
        else:
            for n in range(self.net.size[names[0]]):
                self.over(names[1:], fn, {**place, names[0]: n})

    def pass_on(self, c, s):
        order = self.flows[c]
        rest = [e for e in "zyx" if e not in order[: s + 1]]
        buf = self.bufs[c, s]
        rows = self.rows(c)
        z = self.net.at["z"]

        def middle(owner):
            def fn():
                self.copy(c, s, 1, None, 3, self.net.relay).wait_recv()

                def block(place):
                    place = {**place, "z": owner}
                    idx = (self.slot(c), *[place[e] if e in place else self.net.at[e] for e in "yzx"], rows)
                    got = buf[(3, *[place[e] for e in "yzx" if e in rest])]
                    self.ref[idx] = (self.ref[idx].astype(F32) + got.astype(F32)).astype(BF)

                self.over(rest, block, {})
                self.copy(c, s, 2).start()
            return fn

        def end(unused):
            def fn():
                def block(place):
                    buf[(unused, *[place[e] for e in "yzx" if e in rest])] = jnp.zeros(buf.shape[-2:], BF)

                self.over(rest, block, {})
            return fn

        pl.when(z == 0)(end(0))
        pl.when(z == 1)(middle(3))
        pl.when(z == 2)(middle(0))
        pl.when(z == 3)(end(2))

    def add(self, c, s, out):
        order = self.flows[c]
        z = self.net.at["z"]
        for j in self.hops(c, s):
            take = self.copy(c, s, j).wait_recv
            if self.relayed(c, s) and j != 2:
                pl.when(z != (0 if j == 1 else 3))(take)
            else:
                take()
        rest = [e for e in "zyx" if e not in order[: s + 1]]
        buf = self.bufs[c, s]
        rows = self.rows(c)

        def block(place):
            idx = (self.slot(c), *[place[e] if e in place else self.net.at[e] for e in "yzx"], rows)
            total = self.ref[idx].astype(F32)
            for j in self.hops(c, s):
                total = total + buf[(j - 1, *[place[e] for e in "yzx" if e in place])].astype(F32)
            if s < 2:
                self.ref[idx] = total.astype(BF)
            elif self.halves:
                out.put(c // 2, rows, total)
            else:
                out[c] = total

        self.over(rest, block, {})

    def event(self, c, k, out):
        if self.rows(c) is None:
            return
        if k == 4:
            s = self.flows[c].index("z")
            if self.relayed(c, s):
                self.pass_on(c, s)
            return
        if k:
            self.add(c, k - 1, out)
        if k < 3:
            self.sends(c, k, lambda cp: cp.start())

    def drain(self, c):
        if self.rows(c) is None:
            return
        z = self.net.at["z"]
        for s in range(3):
            self.sends(c, s, lambda cp: cp.wait_send())
            if self.relayed(c, s):
                pl.when(jnp.logical_or(z == 1, z == 2))(lambda: self.copy(c, s, 2).wait_send())


def landing(flows, sizes, rows, ch):
    size = dict(zip("zxy", sizes))
    shapes = {}
    for c, order in enumerate(flows):
        n = rows(c)
        for s in range(3):
            if n:
                rest = [size[e] for e in "yzx" if e not in order[: s + 1]]
                places = 4 if order[s] == "z" and size["z"] == 4 else size[order[s]] - 1
                shapes[c, s] = (places, *rest, n, ch)
    return shapes


SLOT = {DN0: 9, DN1: 10, GA0: DN0, GA1: DN1, UP0: GA0, UP1: GA1, OUT: UP0, GEL: UP1, RNN: OUT}


def big_landing(sizes, part, ch):
    def rows(c):
        cut = chunk_rows(c, part)
        return 0 if cut is None else len(range(part)[cut])

    return landing(BACK, sizes, rows, ch)


def small_landing(sizes, ch):
    return landing(("yxz",), sizes, lambda c: SMALL, ch)


class Finals:
    def __init__(self, ref, out, sem):
        self.ref, self.out, self.sem, self.copies = ref, out, sem, []

    def copy(self, n):
        u, rows = self.copies[n]
        return pltpu.make_async_copy(self.ref.at[n % 2], self.out.at[u, rows], self.sem.at[n % 2])

    def put(self, u, rows, total):
        n = len(self.copies)
        self.copies.append((u, rows))
        if n >= 2:
            self.copy(n - 2).wait()
        self.ref[n % 2] = total
        self.copy(n).start()

    def drain(self):
        for n in range(max(0, len(self.copies) - 2), len(self.copies)):
            self.copy(n).wait()


def block_kernel(sizes, group,
                 tok, cot, w_rnn, w_gel, w_out, w_gate, w_up, w_down, small_in, rec_in, inp_in, prm_in, gains_in, hw_in,
                 o_block, o_gtok, o_gw, o_gs, h_cf, h_a, h_ri, h_cv,
                 W, gs, C6, LRU, T1, SA, N1, TT, MIX, PS, PR, AS, RS, FB, acc, pgain, pack, prm, gains, hw,
                 ss, rs, bss, brs, sss, srs, bsss, bsrs, ps, pr, ls, ts, fs, *landed):
    net = Net(*sizes)
    z_size, x_size, y_size = sizes
    c = net.at["c"]
    half = SEQ // 2
    ch = W.shape[-1]
    part = W.shape[4]
    depth = T1.shape[1]
    own, other = pl.ds(pl.multiple_of(c * half, half), half), pl.ds(pl.multiple_of((1 - c) * half, half), half)
    base_own, base_other = c * half, (1 - c) * half
    mine = (net.at["y"], net.at["z"], net.at["x"])
    dp_index = lax.axis_index("dp")

    sources = {RNN: w_rnn, GEL: w_gel, GA0: w_gate.at[:, 0:ch], GA1: w_gate.at[:, ch : 2 * ch], UP0: w_up.at[:, 0:ch],
               UP1: w_up.at[:, ch : 2 * ch]}
    place = {u: pltpu.make_async_copy(src, W.at[(u, *mine)], ls.at[u]) for u, src in sources.items()}
    place["tok"] = pltpu.make_async_copy(tok, T1.at[own], ls.at[OUT])
    place["cot"] = pltpu.make_async_copy(cot, SA.at[own], ls.at[DN0])
    for cp in place.values():
        cp.start()
    if group == 1:
        lanes = small_in[...].astype(F32)
        lanes = jnp.concatenate([lanes, jnp.zeros((16, 3 * ch - 128), F32)], axis=1)
        pack[...] = jnp.zeros_like(pack)
        pack[0:8, :] = pltpu.roll(lanes, dp_index * (ch // (z_size * x_size)), 1)[0:8, 0:ch]
        spread = pltpu.roll(lanes, dp_index * part, 1)
        for n in range(2):
            for k in range(3):
                pack[8 + 3 * n + k : 9 + 3 * n + k, :] = spread[8 + n : 9 + n, k * ch : (k + 1) * ch]
        gs[(0, *mine, slice(32, 48))] = pack[...].astype(BF)
        for n, src in enumerate((rec_in, inp_in)):
            for h in range(ch // 128):
                gs[(0, *mine, slice(16 * n, 16 * n + 16), slice(h * 128, (h + 1) * 128))] = src[h]
    if part % 128:
        W[(OUT, *mine)] = w_out[...]
        W[(DN0, *mine)] = w_down[:, :ch]
        W[(DN1, *mine)] = w_down[:, ch:]
    else:
        W[(OUT, *mine)] = w_out[...].T
        W[(DN0, *mine)] = w_down[:ch, :].T
        W[(DN1, *mine)] = w_down[ch:, :].T
    net.barrier()

    ag = Gather(net, W, FLOW, ss, rs, True)
    shapes = big_landing(sizes, part, ch)
    back = Scatter(net, W, BACK, dict(zip(shapes, landed)), bss, brs, True)
    small = back_small = None
    if group == 1:
        small = Gather(net, gs, ("zxy",), sss, srs, False)
        tail = landed[len(shapes):]
        back_small = Scatter(net, gs, ("yxz",), dict(zip(small_landing(sizes, ch), tail)), bsss, bsrs, False)

    tok_copy = pair_copy(net, tok, T1.at[own], ps, pr, 0)
    cot_copy = pair_copy(net, cot, SA.at[own], ps, pr, 1)
    tok_in = pair_copy(net, tok, T1.at[other], ps, pr, 0)
    cot_in = pair_copy(net, cot, SA.at[other], ps, pr, 1)
    mix_copy = pair_copy(net, PS, PR.at[0], ps, pr, 2)
    n2_copy = pair_copy(net, T1.at[own], T1.at[own], ps, pr, 3)
    n2_in = pair_copy(net, T1.at[other], T1.at[other], ps, pr, 3)
    back_copy = pair_copy(net, PS, PR.at[0], ps, pr, 4)
    row_copy = pair_copy(net, SA.at[own], SA.at[own], ps, pr, 5)
    row_in = pair_copy(net, SA.at[other], SA.at[other], ps, pr, 5)
    out_copy = pair_copy(net, PS, PR.at[1], ps, pr, 6)
    rnn_copy = pair_copy(net, PS, PR.at[0], ps, pr, 7)
    gain_copy = pair_copy(net, pgain.at[0:8], pgain.at[8:16], ps, pr, 8)
    cf_out = pltpu.make_async_copy(C6, h_cf, ls.at[9])
    cf_in = pltpu.make_async_copy(h_cf, C6, ls.at[10])
    cv_in = pltpu.make_async_copy(h_cv, LRU, ls.at[11])
    tok_again = pltpu.make_async_copy(tok, PR.at[1], ls.at[12])
    block_copy = pltpu.make_async_copy(PR.at[1], o_block, ls.at[13])

    if group == 1:
        small.event(0, 0)
    tok_copy.start()
    cot_copy.start()
    for u in sources:
        place[u].wait()

    def full(u):
        return jnp.concatenate([W[u, yy].reshape(depth, ch) for yy in range(y_size)], axis=1)

    finals = Finals(FB, o_gw, fs)


    def pre1():
        place["tok"].wait()
        place["cot"].wait()
        if group == 1:
            small.event(0, 4)
        cot_in.wait_recv()
        transpose_into(TT, SA, SEQ)

    def pre2():
        tok_in.wait_recv()
        if group == 1:
            small.event(0, 1)

    def pre25():
        if group == 1:
            small.event(0, 2)

    def pre3():
        if group == 1:
            small.event(0, 3)
            join_params(gs, prm, gains, sizes)
            for yy in range(y_size):
                for n in range(2):
                    hw[n, :, yy * ch : (yy + 1) * ch] = head_weight(gs, yy, 16 * n)
        else:
            prm[...] = prm_in[...]
            gains[...] = gains_in[...]
            hw[...] = hw_in[...]
        RS[1, 128:136, :] = jnp.zeros((8, y_size * ch), F32)

        @pl.loop(0, SEQ // 128)
        def _(i):
            v = T1[rows_of(i, 128), :].astype(F32)
            s = lax.rsqrt(jnp.mean(v * v, axis=1, keepdims=True) + EPS)
            N1[rows_of(i, 128), :] = (v * s * gains[0:1, :]).astype(BF)

    T = 128
    tiles = SEQ // T

    def kept(i, slot):
        return (pltpu.make_async_copy(AS.at[slot], h_a.at[i], ts.at[0, slot]),
                pltpu.make_async_copy(RS.at[slot], h_ri.at[i], ts.at[1, slot]),
                pltpu.make_async_copy(PS.at[rows_of(slot, T), 0 : y_size * ch], h_cv.at[rows_of(i, T)], ts.at[2, slot]))

    def branch(hook):
        def branch_tile(i, carries):
            hook(i)
            slot = lax.rem(i, 2)

            @pl.when(i >= 2)
            def _():
                for cp in kept(i - 2, slot):
                    cp.wait()

            RS[slot, 0:8, :] = RS[1 - slot, 128:136, :]
            RS[slot, 8:136, :] = nn(N1[rows_of(i, T), :], full(RNN))
            rows = rows_of(i, T)
            br = nn(N1[rows, :], full(GEL))
            new = []
            for yy in range(y_size):
                cols = slice(yy * ch, (yy + 1) * ch)
                p = prm[yy]
                x = RS[slot, :, cols]
                cv = p[4:5] + p[0:1] * x[8:]
                for k in range(1, 4):
                    cv = cv + p[k : k + 1] * pltpu.roll(x, k, 0)[8:]
                cv_low = cv.astype(BF)
                PS[pl.ds(pl.multiple_of(slot * T, T), T), cols] = cv_low
                cv = cv_low.astype(F32)
                rec, inp = [], []
                for h in range(ch // 128):
                    hc = slice(yy * ch + h * 128, yy * ch + (h + 1) * 128)
                    both = nn(cv_low[:, h * 128 : (h + 1) * 128], jnp.concatenate([hw[0, :, hc], hw[1, :, hc]], axis=1))
                    rec.append(both[:, :128])
                    inp.append(both[:, 128:])
                r = jax.nn.sigmoid(jnp.concatenate(rec, axis=1) + p[5:6])
                w = jax.nn.sigmoid(jnp.concatenate(inp, axis=1) + p[6:7])
                soft = jnp.log1p(jnp.exp(-jnp.abs(p[7:8]))) + jnp.maximum(p[7:8], 0.0)
                a = jnp.exp((-DECAY_SCALE * soft) * r)
                u = 1.0 - a * a + GUARD
                inv = lax.rsqrt(u)
                root = u * inv
                wc = w * cv
                state, last = scan_forward(a, root * wc, carries[yy])
                first = lax.broadcasted_iota(jnp.int32, (T, ch), 0) == 0
                prev = jnp.where(first, carries[yy], pltpu.roll(state, 1, 0))
                new.append(last)
                g, gp = gelu_parts(br[:, cols])
                LRU[rows, cols] = (state * g).astype(BF)
                cp = (prev - a * wc * inv) * a * r * (-DECAY_SCALE)
                AS[slot, :, cols] = a
                C6[0, rows, cols] = g.astype(BF)
                C6[1, rows, cols] = (state * gp).astype(BF)
                C6[2, rows, cols] = cp.astype(BF)
                C6[3, rows, cols] = (cp * soft * (1.0 - r)).astype(BF)
                C6[4, rows, cols] = (root * wc * (1.0 - w)).astype(BF)
                C6[5, rows, cols] = (root * w).astype(BF)
            for cp in kept(i, slot):
                cp.start()
            return tuple(new)

        lax.fori_loop(0, tiles, branch_tile, tuple(jnp.zeros((1, ch), F32) for _ in range(y_size)))
        cf_out.start()
        for i in (tiles - 2, tiles - 1):
            for cp in kept(i, i % 2):
                cp.wait()

    def out_rows(rows):
        return nt(LRU[rows, :], full(OUT))

    def out():
        PS[...] = out_rows(other).astype(BF)
        mix_copy.start()
        MIX[...] = out_rows(own)

    def mix():
        mix_copy.wait_recv()

        @pl.loop(0, half // T)
        def _(i):
            rows = rows_of(i, T)
            at = pl.ds(pl.multiple_of(base_own + i * T, T), T)
            v = T1[at, :].astype(F32) + MIX[rows, :] + PR[0, rows, :].astype(F32)
            MIX[rows, :] = v
            s = lax.rsqrt(jnp.mean(v * v, axis=1, keepdims=True) + EPS)
            T1[at, :] = (v * s * gains[1:2, :]).astype(BF)

        n2_copy.start()

    def n2():
        n2_in.wait_recv()
        cf_out.wait()

    F = 256

    def ff(j):
        def loop(hook):
            @pl.loop(0, SEQ // F)
            def _(i):
                hook(i)
                rows = rows_of(i, F)
                up = nn(T1[rows, :], full(UP[j]))
                g, gp = gelu_parts(nn(T1[rows, :], full(GATE[j])))
                C6[j, rows, :] = (g * up).astype(BF)
                C6[2 + j, rows, :] = (gp * up).astype(BF)
                C6[4 + j, rows, :] = g.astype(BF)
        return loop


    zh = z_size // 2

    def weight_grad(u, left, right):
        if SLOT[u] < UNITS:
            for chunk in (2 * SLOT[u], 2 * SLOT[u] + 1):
                ag.drain(chunk)

        @pl.loop(0, 2)
        def _(i):
            val = nn(left[rows_of(i, depth // 2), :], right[...]).astype(BF)
            for yy in range(y_size):
                W[SLOT[u], yy, pl.ds(i * zh, zh)] = val[:, yy * ch : (yy + 1) * ch].reshape(
                    zh, x_size, depth // (z_size * x_size), ch)

    def d0():
        weight_grad(DN0, TT, C6.at[0])

    def d1():
        weight_grad(DN1, TT, C6.at[1])

    def gh(hook):
        @pl.loop(0, 2 * (SEQ // F))
        def _(n):
            hook(n)
            j, i = n // (SEQ // F), lax.rem(n, SEQ // F)
            rows = rows_of(i, F)
            g = nn(SA[rows, :], full(DN0 + j))
            C6[2 + j, rows, :] = (g * C6[2 + j, rows, :].astype(F32)).astype(BF)
            C6[4 + j, rows, :] = (g * C6[4 + j, rows, :].astype(F32)).astype(BF)

    def span(base, i):
        return pl.ds(pl.multiple_of(base + i * F, F), F)

    def mlp_back(rows):
        return (nt(C6[2, rows, :], full(GA0)) + nt(C6[3, rows, :], full(GA1))
                + nt(C6[4, rows, :], full(UP0)) + nt(C6[5, rows, :], full(UP1)))

    def mlp_out(rows):
        return nt(C6[0, rows, :], full(DN0)) + nt(C6[1, rows, :], full(DN1))

    def rnn_back(rows):
        return nt(C6[5, rows, :], full(RNN)) + nt(C6[1, rows, :], full(GEL))

    def partial_rows(fn, base, dst, hook=None):
        @pl.loop(0, half // F)
        def _(i):
            if hook is not None:
                hook(i)
            dst[rows_of(i, F), :] = fn(span(base, i)).astype(dst.dtype)

    def bo():
        mix_copy.wait_send()
        partial_rows(mlp_out, base_other, PS)
        out_copy.start()

    def bw():
        partial_rows(mlp_out, base_own, o_gtok)

    def gno(hook):
        out_copy.wait_recv()

        @pl.loop(0, half // F)
        def _(i):
            rows = rows_of(i, F)
            PR[1, rows, :] = (MIX[rows, :] + o_gtok[rows, :] + PR[1, rows, :].astype(F32)).astype(BF)

        block_copy.start()
        out_copy.wait_send()
        partial_rows(mlp_back, base_other, PS, hook)
        back_copy.start()

    def gnw(hook):
        partial_rows(mlp_back, base_own, o_gtok, hook)

    def norm():
        acc[...] = jnp.zeros_like(acc)
        pgain[...] = jnp.zeros_like(pgain)
        n2_copy.wait_send()
        back_copy.wait_recv()

        @pl.loop(0, half // T)
        def _(i):
            rows = rows_of(i, T)
            at = pl.ds(pl.multiple_of(base_own + i * T, T), T)
            v = MIX[rows, :]
            gn = o_gtok[rows, :] + PR[0, rows, :].astype(F32)
            s = lax.rsqrt(jnp.mean(v * v, axis=1, keepdims=True) + EPS)
            q = gn * gains[1:2, :]
            pgain[1:2, :] += jnp.sum(gn * v * s, axis=0, keepdims=True)
            gm = SA[at, :].astype(F32) + s * q - (s * s * s) * v * jnp.mean(q * v, axis=1, keepdims=True)
            o_gtok[rows, :] = gm
            SA[at, :] = gm.astype(BF)

        row_copy.start()

    def ga0():
        transpose_into(TT, T1, SEQ)
        weight_grad(GA0, TT, C6.at[2])

    def ga1():
        weight_grad(GA1, TT, C6.at[3])

    def up0():
        weight_grad(UP0, TT, C6.at[4])

    def up1():
        weight_grad(UP1, TT, C6.at[5])
        cf_in.start()
        block_copy.wait()
        tok_again.start()

    def fetch(n, slot):
        i = tiles - 1 - n
        return (pltpu.make_async_copy(h_a.at[i], AS.at[slot], ts.at[0, slot]),
                pltpu.make_async_copy(h_ri.at[i], RS.at[slot], ts.at[1, slot]))

    def outg():
        for cp in fetch(0, 0):
            cp.start()
        row_in.wait_recv()
        transpose_into(TT, SA, SEQ)
        weight_grad(OUT, TT, LRU)
        cv_in.start()
        cf_in.wait()

    def back_rows(hook):
        def back_tile(n, carries):
            hook(n)
            slot = lax.rem(n, 2)
            for cp in fetch(n, slot):
                cp.wait()

            @pl.when(n + 1 < tiles)
            def _():
                for cp in fetch(n + 1, 1 - slot):
                    cp.start()

            i = tiles - 1 - n
            rows = rows_of(i, T)
            gl_all = nn(SA[rows, :], full(OUT))
            new = []
            for yy in range(y_size):
                adj_next, a_next, gco_next = carries[yy]
                cols = slice(yy * ch, (yy + 1) * ch)
                p = prm[yy]
                gl = gl_all[:, cols]
                at = AS[slot, :, cols]
                last = lax.broadcasted_iota(jnp.int32, (T, ch), 0) == T - 1
                shifted = jnp.where(last, a_next, pltpu.roll(at, T - 1, 0))
                adj, adj_first = scan_backward(shifted, gl * C6[0, rows, cols].astype(F32), adj_next)
                C6[1, rows, cols] = (gl * C6[1, rows, cols].astype(F32)).astype(BF)
                grp = adj * C6[3, rows, cols].astype(F32)
                gip = adj * C6[4, rows, cols].astype(F32)
                gr_low, gi_low = grp.astype(BF), gip.astype(BF)
                gcd = adj * C6[5, rows, cols].astype(F32)
                acc[yy, 5:6] += jnp.sum(grp, axis=0, keepdims=True)
                acc[yy, 6:7] += jnp.sum(gip, axis=0, keepdims=True)
                acc[yy, 7:8] += jnp.sum(adj * C6[2, rows, cols].astype(F32), axis=0, keepdims=True)
                C6[3, rows, cols] = gr_low
                C6[4, rows, cols] = gi_low
                parts = []
                for h in range(ch // 128):
                    hs = slice(h * 128, (h + 1) * 128)
                    hc = slice(yy * ch + h * 128, yy * ch + (h + 1) * 128)
                    parts.append(nt(jnp.concatenate([gr_low[:, hs], gi_low[:, hs]], axis=1),
                                    jnp.concatenate([hw[0, :, hc], hw[1, :, hc]], axis=1)))
                gco = gcd + jnp.concatenate(parts, axis=1)
                ext = jnp.concatenate([gco, gco_next], axis=0)
                x = RS[slot, :, cols]
                grn = p[0:1] * gco
                acc[yy, 0:1] += jnp.sum(gco * x[8:], axis=0, keepdims=True)
                acc[yy, 4:5] += jnp.sum(gco, axis=0, keepdims=True)
                for k in range(1, 4):
                    grn = grn + p[k : k + 1] * pltpu.roll(ext, T + 8 - k, 0)[:T]
                    acc[yy, k : k + 1] += jnp.sum(gco * pltpu.roll(x, k, 0)[8:], axis=0, keepdims=True)
                C6[5, rows, cols] = grn.astype(BF)
                new.append((adj_first, at[0:1], gco[0:8]))
            return tuple(new)

        zero = (jnp.zeros((1, ch), F32), jnp.zeros((1, ch), F32), jnp.zeros((8, ch), F32))
        lax.fori_loop(0, tiles, back_tile, (zero,) * y_size)

    def gel():
        transpose_into(TT, N1, SEQ)
        weight_grad(GEL, TT, C6.at[1])

    def rnn():
        weight_grad(RNN, TT, C6.at[5])

    def gn1o():
        back_copy.wait_send()
        partial_rows(rnn_back, base_other, PS)
        rnn_copy.start()

    def gn1w():
        partial_rows(rnn_back, base_own, MIX)

    def heads():
        cv_in.wait()
        if group == 1:
            small.drain(0)
        for yy in range(y_size):
            acc[yy, 7:8] = acc[yy, 7:8] * jax.nn.sigmoid(prm[yy, 7:8])
            for h in range(ch // 128):
                hs = slice(h * 128, (h + 1) * 128)
                hc = slice(yy * ch + h * 128, yy * ch + (h + 1) * 128)
                both = lax.dot_general(LRU[:, hc], jnp.concatenate([C6[3, :, hc], C6[4, :, hc]], axis=1),
                                       (((0,), (0,)), ((), ())), preferred_element_type=F32)
                for n in range(2):
                    val = both[:, n * 128 : (n + 1) * 128]
                    if group > 1:
                        o_gs[yy, 128 * n : 128 * n + 128, hs] = val
                    else:
                        gs[0, yy, :, :, 16 * n : 16 * n + 16, hs] = val.astype(BF).reshape(z_size, x_size, 16, 128)

    def fin():
        tok_again.wait()
        rnn_copy.wait_recv()

        @pl.loop(0, half // T)
        def _(i):
            rows = rows_of(i, T)
            v = PR[1, rows, :].astype(F32)
            gn = MIX[rows, :] + PR[0, rows, :].astype(F32)
            s = lax.rsqrt(jnp.mean(v * v, axis=1, keepdims=True) + EPS)
            q = gn * gains[0:1, :]
            pgain[0:1, :] += jnp.sum(gn * v * s, axis=0, keepdims=True)
            o_gtok[rows, :] += s * q - (s * s * s) * v * jnp.mean(q * v, axis=1, keepdims=True)

        gain_copy.start()

    def small_step(k):
        def fn():
            if k == 0:
                gain_copy.wait_recv()
                for n in range(2):
                    row = pgain[n : n + 1, :] + pgain[8 + n : 9 + n, :]
                    row = jnp.concatenate([row, jnp.zeros((1, 3 * ch - depth), F32)], axis=1)
                    for m in range(3):
                        for yy in range(y_size):
                            acc[yy, 8 + 3 * n + m : 9 + 3 * n + m, :] = row[:, m * ch : (m + 1) * ch]
                if group > 1:
                    for yy in range(y_size):
                        o_gs[yy, 256:272, :] = acc[yy]
                    return

                @pl.loop(0, z_size)
                def _(z):
                    for yy in range(y_size):
                        for xx in range(x_size):
                            gs[0, yy, z, xx, 32:48, :] = acc[yy].astype(BF)

            if group == 1:
                back_small.event(0, k, o_gs)
        return fn

    blocks = dict(pre1=pre1, pre2=pre2, pre25=pre25, pre3=pre3, out=out, mix=mix, n2=n2, d0=d0, d1=d1, bo=bo, bw=bw, ga0=ga0,
                  ga1=ga1, norm=norm, up0=up0, up1=up1, outg=outg, gel=gel, rnn=rnn, gn1o=gn1o, gn1w=gn1w, heads=heads,
                  fin=fin, s0=small_step(0), s1=small_step(1), s2=small_step(2), sr=small_step(4), s3=small_step(3))
    blocks = {name: (1, fn) for name, fn in blocks.items()}
    blocks.update(br=(tiles, branch), ffa=(SEQ // F, ff(0)), ffb=(SEQ // F, ff(1)), gh=(2 * SEQ // F, gh),
                  gno=(half // F, gno), gnw=(half // F, gnw), t=(tiles, back_rows))

    def event(chunk, k):
        if chunk < CHUNKS:
            ag.event(chunk, k)
        else:
            back.event(chunk - CHUNKS, k, finals)

    run_plan(PLAN, blocks, event)
    for u in (RNN, GEL):
        for chunk in (2 * u, 2 * u + 1):
            ag.drain(chunk)
    for chunk in range(CHUNKS):
        back.drain(chunk)
    if group == 1:
        back_small.drain(0)
    finals.drain()
    for cp in (tok_copy, cot_copy, row_copy, rnn_copy, gain_copy):
        cp.wait_send()


def finish_kernel(sizes, block_in, gtok_in, gw, gs,
                  o_block, o_gtok, o_mg, o_rnn, o_gel, o_cw, o_cb, o_rw, o_iw, o_rb, o_ib, o_dp, o_out, o_lg, o_gate, o_up,
                  o_down):
    ch = gw.shape[2]
    dp = sizes[0] * sizes[1]
    part, own = o_mg.shape[1], ch // dp
    dp_index = lax.axis_index("dp")
    o_block[...] = block_in[...]
    o_gtok[...] = gtok_in[...]
    o_rnn[...] = gw[RNN]
    o_gel[...] = gw[GEL]
    o_out[...] = gw[OUT].T
    for j in range(2):
        cols = slice(j * ch, (j + 1) * ch)
        o_gate[:, cols] = gw[GATE[j]]
        o_up[:, cols] = gw[UP[j]]
        o_down[cols, :] = gw[DOWN[j]].T
    for h in range(ch // 128):
        o_rw[h] = gs[0, 0:16, h * 128 : (h + 1) * 128]
        o_iw[h] = gs[0, 16:32, h * 128 : (h + 1) * 128]
    rows = pltpu.roll(gs[0, 32:40, :], ch - dp_index * own, 1)
    o_cw[...] = rows[0:4, 0:own]
    for k, ref in ((4, o_cb), (5, o_rb), (6, o_ib), (7, o_dp)):
        ref[...] = rows[k : k + 1, 0:own]
    for n, ref in ((0, o_mg), (1, o_lg)):
        row = jnp.concatenate([gs[0, 40 + 3 * n + k : 41 + 3 * n + k, :] for k in range(3)], axis=1)
        row = jnp.broadcast_to(row, (8, 3 * ch))
        ref[...] = pltpu.roll(row, 3 * ch - dp_index * part, 1)[0:1, 0:part]


def any_spec():
    return pl.BlockSpec(memory_space=pl.ANY)


def vmem_spec():
    return pl.BlockSpec(memory_space=pltpu.VMEM)


def body(sizes, tokens, mix_gain, rnn_weight, gelu_weight, conv_weight, conv_bias, recur_weight, input_weight,
         recur_bias, input_bias, decay_param, out_weight, mlp_gain, gate_weight, up_weight, down_weight, cotangent):
    z_size, x_size, y_size = sizes
    dp = z_size * x_size
    dp_index = lax.axis_index("dp")
    rows, depth = tokens.shape
    part, ch = rnn_weight.shape
    head_rows = recur_weight.shape[1]
    group = max(1, 16 // head_rows)
    wide = y_size * ch
    own = ch // dp
    small_in = jnp.concatenate([conv_weight, conv_bias[None], recur_bias[None], input_bias[None], decay_param[None]], axis=0)
    small_in = jnp.concatenate([jnp.pad(small_in, ((0, 0), (0, 128 - own))),
                                jnp.pad(jnp.stack([mix_gain, mlp_gain]), ((0, 6), (0, 128 - part)))], axis=0)
    heads = [recur_weight, input_weight]
    out_w, down_w = out_weight, down_weight
    if part % 128:
        out_w, down_w = out_weight.T, down_weight.T
    shape = jax.ShapeDtypeStruct
    grid = (y_size, z_size, x_size)
    hops = z_size + x_size + y_size - 2
    t = lax.axis_index("tensor")
    joined = [small_in] * 3
    if group > 1:
        lanes = jnp.pad(small_in[0:8, :own].astype(F32), ((0, 8), (0, ch - own)))
        lanes = jnp.roll(lanes, dp_index * own, axis=1)
        gain = jnp.pad(jnp.stack([mix_gain, mlp_gain]).astype(F32), ((0, 6), (0, depth - part)))
        gain = lax.psum(jnp.roll(gain, dp_index * part, axis=1), "dp")
        every = jnp.zeros((2 * y_size, 272, ch), F32)
        for n, w in enumerate(heads):
            w = jnp.transpose(w, (1, 0, 2)).reshape(1, head_rows, ch).astype(F32)
            every = lax.dynamic_update_slice(every, w, (t, 128 * n + dp_index * head_rows, 0))
        every = lax.psum(lax.dynamic_update_slice(every, lanes[None], (t, 256, 0)), ("dp", "tensor"))
        mine = [every[2 * yy] * (1 - lax.rem(t, 2)) + every[2 * yy + 1] * lax.rem(t, 2) for yy in range(y_size)]
        joined = [jnp.stack([m[256:] for m in mine]), gain,
                  jnp.concatenate([m[0:256].reshape(2, 128, ch) for m in mine], axis=2).astype(BF)]
        heads = [jnp.zeros((ch // 128, 16, 128), BF)] * 2
    dma = pltpu.SemaphoreType.DMA
    landed = list(big_landing(sizes, part, ch).values())
    gs_out, small_grid = (y_size, 272, ch), (1, 1, 1)
    if group == 1:
        landed += list(small_landing(sizes, ch).values())
        gs_out, small_grid = (1, SMALL, ch), grid
    block_out, grad_tokens, gw, gs = pl.pallas_call(
        functools.partial(block_kernel, sizes, group),
        out_shape=[shape((rows, depth), BF), shape((rows, depth), F32), shape((UNITS, part, ch), F32), shape(gs_out, F32),
                   shape((6, SEQ, wide), BF), shape((SEQ // 128, 128, wide), F32), shape((SEQ // 128, 136, wide), F32),
                   shape((SEQ, wide), BF)],
        in_specs=[any_spec(), any_spec(), any_spec(), any_spec(), vmem_spec(), any_spec(), any_spec(), vmem_spec(),
                  vmem_spec(), vmem_spec(), vmem_spec(), *([vmem_spec()] * 3 if group > 1 else [any_spec()] * 3)],
        out_specs=[any_spec(), vmem_spec(), any_spec(), vmem_spec()] + [any_spec()] * 4,
        scratch_shapes=[
            pltpu.VMEM((UNITS + 2, *grid, part, ch), BF), pltpu.VMEM((1, *small_grid, SMALL, ch), BF),
            pltpu.VMEM((6, SEQ, wide), BF), pltpu.VMEM((SEQ, wide), BF),
            *[pltpu.VMEM((SEQ, depth), BF)] * 4, pltpu.VMEM((rows, depth), F32),
            pltpu.VMEM((rows, depth), BF), pltpu.VMEM((2, rows, depth), BF),
            pltpu.VMEM((2, 128, wide), F32), pltpu.VMEM((2, 136, wide), F32),
            pltpu.VMEM((2, max(part // 2, 16), ch), F32),
            pltpu.VMEM((y_size, 16, ch), F32), pltpu.VMEM((16, depth), F32), pltpu.VMEM((16, ch), F32),
            pltpu.VMEM((y_size, 16, ch), F32), pltpu.VMEM((8, depth), F32), pltpu.VMEM((2, 128, wide), BF),
            dma((CHUNKS, hops)), dma((CHUNKS, hops)), dma((CHUNKS, hops)), dma((CHUNKS, hops)),
            dma((1, hops)), dma((1, hops)), dma((1, hops)), dma((1, hops)), dma((9,)), dma((9,)), dma((14,)), dma((3, 2)), dma((2,)),
            *[pltpu.VMEM(s, BF) for s in landed],
        ],
        compiler_params=pltpu.CompilerParams(collective_id=0, has_side_effects=True, vmem_limit_bytes=VMEM_LIMIT),
        name="residual_block",
    )(tokens, cotangent, rnn_weight, gelu_weight, out_w, gate_weight, up_weight, down_w, small_in, *heads, *joined)[:4]
    if group > 1:
        every = jnp.zeros((2 * y_size, 272, ch), F32)
        for yy in range(y_size):
            every = lax.dynamic_update_slice(every, gs[yy : yy + 1], (2 * yy + lax.rem(t, 2), 0, 0))
        gs = lax.dynamic_slice(lax.psum(every, ("dp", "tensor")), (t, 0, 0), (1, 272, ch))
        first = dp_index * head_rows
        rec = lax.dynamic_slice(gs[0], (first, 0), (head_rows, ch))
        inp = lax.dynamic_slice(gs[0], (128 + first, 0), (head_rows, ch))
        fill = jnp.zeros((16 - head_rows, ch), F32)
        gs = jnp.concatenate([rec, fill, inp, fill, gs[0, 256:]], axis=0)[None]
    f_shapes = [
        shape((rows, depth), BF), shape((rows, depth), F32), shape((1, part), F32), shape((part, ch), F32),
        shape((part, ch), F32), shape((4, own), F32), shape((1, own), F32), shape((ch // 128, 16, 128), F32),
        shape((ch // 128, 16, 128), F32), shape((1, own), F32), shape((1, own), F32), shape((1, own), F32),
        shape((ch, part), F32), shape((1, part), F32), shape((part, 2 * ch), F32), shape((part, 2 * ch), F32),
        shape((2 * ch, part), F32),
    ]
    res = list(pl.pallas_call(
        functools.partial(finish_kernel, sizes),
        out_shape=f_shapes,
        in_specs=[vmem_spec()] * 4,
        out_specs=[vmem_spec()] * 17,
        compiler_params=pltpu.CompilerParams(vmem_limit_bytes=VMEM_LIMIT),
        name="unpack",
    )(block_out, grad_tokens, gw, gs))
    for k in (2, 6, 9, 10, 11, 13):
        res[k] = res[k][0]
    for k in (7, 8):
        res[k] = res[k][:, :head_rows]
    return tuple(res)


def solution(mesh):
    dp, tensor = mesh.shape["dp"], mesh.shape["tensor"]
    x_size = 2
    sizes = (dp // x_size, x_size, tensor // 2)
    rows, split, vec = P(("dp", "tensor"), None), P("dp", "tensor"), P(("tensor", "dp"))
    head, flip, taps = P("tensor", "dp", None), P("tensor", "dp"), P(None, ("tensor", "dp"))
    return jax.shard_map(
        functools.partial(body, sizes),
        mesh=mesh,
        in_specs=(rows, P("dp"), split, split, taps, vec, head, head, vec, vec, vec, flip, P("dp"), split, split, flip,
                  rows),
        out_specs=(rows, rows, P("dp"), split, split, taps, vec, head, head, vec, vec, vec, flip, P("dp"), split, split,
                   flip),
        check_vma=False,
    )
```

time: 276 us -> 239 us (0.87)
  Pallas kernels: 273 us -> 236 us
    pallas_call x2 -> x1, Pallas kernels: 268 us -> 231 us  [body(): pl.pallas_call(functools.partial(block_kernel, sizes, group), out_shape=[...]
where the time goes in v3:
time: 239 us; the launch traced here: 238 us
  Pallas kernels  236 us (99%)
    pallas_call x1, Pallas kernels, body(): pl.pallas_call(functools.partial(block_kernel, sizes, group), out_shape=[...  231 us
    pallas_call x1, Pallas kernels, body(): pl.pallas_call(functools.partial(finish_kernel, sizes), out_shape=f_shape...  5 us

profile of v3, /device:TPU:0, one launch (start us, length us, event | category | flops | bytes accessed | tf_op | source)
XLA Modules:
  0.0 238.4 jit_solution(427891647706220323)
XLA Ops:
  0.7 0.7 fusion.4
  1.3 0.7 concatenate.6
  2.1 0.6 fusion.1.small_in.prm_in.gains_in.hw_in
  2.7 230.6 %residual_block.1 = (bf16[512,1024]{1,0:T(8,128)(2,1)}, f32[512,1024]{1,0:T(8,128)}, f32[9,128,384]{2,1,0:T(8,128)}, f32[1,48,384]{2,1,0:T(8,128)}, bf16[6,1024,...) custom-call(bf16[512,1024]{1,0:T(8,128)(2,1)} %tok.1, ...), custom_call_target="tpu_custom_call" | custom-call | tf_op jit(solution)/shard_map/residual_block/pallas_call | solution.py:1049
  233.3 5.0 %unpack.1 = (bf16[512,1024]{1,0:T(8,128)(2,1)}, f32[512,1024]{1,0:T(8,128)}, f32[1,128]{1,0:T(1,128)}, f32[128,384]{1,0:T(8,128)}, f32[128,384]{1,0:T(8,128)}, /...) custom-call(bf16[512,1024]{1,0:T(8,128)(2,1)} %get-tuple-element.38., ...), custom_call_target="tpu_custom_call" | custom-call | tf_op jit(solution)/shard_map/unpack/pallas_call | solution.py:1090

commit v4 on v3

--- a/solution.py
+++ b/solution.py
@@ -24,25 +24,26 @@
 CHUNKS = 2 * UNITS
 SMALL = 48
 FLOW = (
-    "zxy", "zyx", "zxy", "zyx", "zxy", "yxz", "zxy", "xzy", "yzx", "zyx", "zyx", "zxy", "zyx", "xyz", "zyx", "xzy",
-    "zyx", "xyz",
+    "zxy", "zxy", "zyx", "zyx", "zxy", "yzx", "xzy", "yzx", "zyx", "zyx", "xzy", "xzy", "yxz", "zyx", "zyx", "zyx",
+    "xyz", "xzy",
 )
 BACK = (
-    "xyz", "xzy", "yxz", "yxz", "yxz", "yzx", "xzy", "yxz", "xzy", "yxz", "yxz", "xzy", "zyx", "xyz", "zxy", "xzy",
-    "yzx", "zyx",
+    "xyz", "yxz", "xyz", "yzx", "xyz", "yzx", "xzy", "zyx", "yzx", "xyz", "yxz", "xzy", "xzy", "yxz", "zyx", "xyz",
+    "zxy", "yzx",
 )
+SMALL_FLOW, SMALL_BACK = ("zxy",), ("xyz",)
 PLAN = (
-    15, 75, 85, 40, 0, 65, 25, 66, 19, 86, 5, "pre1", "pre2", 26, "pre25", 4, 10, 9, "pre3", 30, 16, 1, 6, 35, 14,
-    41, 11, 2, 7, 34, 20, 60, 17, 44, 12, 50, 64, 24, 45, 21, 61, 54, 55, 49, 80, 46, 31, 8, 3, 18, 13, 70, "br", 51,
-    42, 59, 36, "br", 22, 47, 27, "br", "br", 84, 56, 32, "br", 39, 74, "br", 76, "br", 52, 37, 71, "br", 48, 62, 33,
-    23, 29, 79, 67, 28, "out", "mix", 38, "n2", 43, 57, "ffa", "ffa", 69, 81, 87, 53, 72, 77, "ffa", "ffa", "d0",
-    160, 63, 68, 58, "ffb", 82, "ffb", "ffb", "ffb", 89, "d1", 170, 165, 164, 73, 78, 175, 88, 83, "gh", "gh", "gh",
-    "gh", "gh", "gh", "gh", "gh", "bo", "bw", "ga0", 120, 166, 171, 125, 179, "ga1", 145, 140, "gno", "gno", 169,
-    "gnw", "gnw", 121, 174, "norm", "up0", 130, 135, "up1", 146, "outg", 124, 110, 126, 150, "t", 155, "t", "t", 115,
-    "t", 141, 154, 149, "t", "t", 111, 131, "t", 156, 136, "t", 142, "gel", 134, 100, 127, 112, "rnn", 105, 95, 137,
-    90, 144, "gn1o", 122, 129, 167, 157, 114, "gn1w", 116, "heads", 113, 101, 159, 143, 139, 161, 96, 176, "fin", 91,
-    "s0", 106, 119, 99, 132, 123, 128, "s1", 102, 151, 168, 177, 92, 162, 172, "s2", 117, 104, 97, 147, 107, 94, 138,
-    "sr", 152, 178, 173, 158, 133, 163, 109, "s3", 103, 98, 153, 148, 93, 118, 108,
+    0, 45, 60, "pre0", 25, 50, 80, 35, 30, 4, "pre1", 180, 81, 1, 49, 46, 10, 184, 15, 61, 20, 2, 181, 47, 5, 24, 85,
+    55, 14, 65, 40, 19, 182, 9, 44, 11, 70, 36, 21, 41, 75, 16, 6, 12, 69, 48, 31, 39, 7, 183, 26, 66, 17, "pre3",
+    13, 79, 34, 74, 42, 8, 22, 76, 56, 29, 3, 18, 32, 86, 51, "br", "br", 27, "br", "br", 37, "br", 59, 62, "br",
+    "br", 57, "br", 43, 54, 33, 23, 28, 89, "out", 67, "mix", 77, 71, "n2", 82, 38, "ffa", 52, "ffa", 87, 64, "ffa",
+    58, "ffa", 68, "d0", 160, 72, 165, 63, 53, "ffb", 84, 78, "ffb", "ffb", "ffb", 164, "d1", 170, 175, 88, 73, 83,
+    "gh", "gh", "gh", "gh", "gh", "gh", "gh", "gh", "bo", "bw", "ga0", 120, 166, 174, 125, "ga1", "gno", 140, 145,
+    161, "gno", "gnw", "gnw", "norm", 129, "up0", 167, 130, 176, 135, "up1", 169, 141, 155, 146, "outg", "t", 150,
+    "t", "t", "t", 149, 121, 179, 110, 131, 115, "t", "t", "t", 168, 124, "t", 136, 151, "gel", 134, 105, "rnn", 100,
+    95, "gn1o", "gn1w", 142, 154, "heads", 90, 144, 111, 156, 177, 137, 106, "fin", "s0", 116, 139, 91, 185, 119,
+    109, 101, 147, 96, 126, 112, 171, 157, 143, 92, 132, 102, 148, 159, 162, 186, 152, 117, 94, 114, 97, 122, 187,
+    127, 172, 133, 104, 113, 138, 163, 158, 178, 107, 99, 128, 93, 103, 153, 173, 189, 123, 108, 118, 98, 188,
 )
 
 
@@ -422,7 +423,7 @@
 
 
 def small_landing(sizes, ch):
-    return landing(("yxz",), sizes, lambda c: SMALL, ch)
+    return landing(SMALL_BACK, sizes, lambda c: SMALL, ch)
 
 
 class Finals:
@@ -449,7 +450,7 @@
 def block_kernel(sizes, group,
                  tok, cot, w_rnn, w_gel, w_out, w_gate, w_up, w_down, small_in, rec_in, inp_in, prm_in, gains_in, hw_in,
                  o_block, o_gtok, o_gw, o_gs, h_cf, h_a, h_ri, h_cv,
-                 W, gs, C6, LRU, T1, SA, N1, TT, MIX, PS, PR, AS, RS, FB, acc, pgain, pack, prm, gains, hw,
+                 W, gs, C6, LRU, T1, SA, N1, TT, MIX, PS, PR, gtok, AS, RS, FB, acc, pgain, pack, prm, gains, hw,
                  ss, rs, bss, brs, sss, srs, bsss, bsrs, ps, pr, ls, ts, fs, *landed):
     net = Net(*sizes)
     z_size, x_size, y_size = sizes
@@ -470,27 +471,6 @@
     place["cot"] = pltpu.make_async_copy(cot, SA.at[own], ls.at[DN0])
     for cp in place.values():
         cp.start()
-    if group == 1:
-        lanes = small_in[...].astype(F32)
-        lanes = jnp.concatenate([lanes, jnp.zeros((16, 3 * ch - 128), F32)], axis=1)
-        pack[...] = jnp.zeros_like(pack)
-        pack[0:8, :] = pltpu.roll(lanes, dp_index * (ch // (z_size * x_size)), 1)[0:8, 0:ch]
-        spread = pltpu.roll(lanes, dp_index * part, 1)
-        for n in range(2):
-            for k in range(3):
-                pack[8 + 3 * n + k : 9 + 3 * n + k, :] = spread[8 + n : 9 + n, k * ch : (k + 1) * ch]
-        gs[(0, *mine, slice(32, 48))] = pack[...].astype(BF)
-        for n, src in enumerate((rec_in, inp_in)):
-            for h in range(ch // 128):
-                gs[(0, *mine, slice(16 * n, 16 * n + 16), slice(h * 128, (h + 1) * 128))] = src[h]
-    if part % 128:
-        W[(OUT, *mine)] = w_out[...]
-        W[(DN0, *mine)] = w_down[:, :ch]
-        W[(DN1, *mine)] = w_down[:, ch:]
-    else:
-        W[(OUT, *mine)] = w_out[...].T
-        W[(DN0, *mine)] = w_down[:ch, :].T
-        W[(DN1, *mine)] = w_down[ch:, :].T
     net.barrier()
 
     ag = Gather(net, W, FLOW, ss, rs, True)
@@ -498,9 +478,9 @@
     back = Scatter(net, W, BACK, dict(zip(shapes, landed)), bss, brs, True)
     small = back_small = None
     if group == 1:
-        small = Gather(net, gs, ("zxy",), sss, srs, False)
+        small = Gather(net, gs, SMALL_FLOW, sss, srs, False)
         tail = landed[len(shapes):]
-        back_small = Scatter(net, gs, ("yxz",), dict(zip(small_landing(sizes, ch), tail)), bsss, bsrs, False)
+        back_small = Scatter(net, gs, SMALL_BACK, dict(zip(small_landing(sizes, ch), tail)), bsss, bsrs, False)
 
     tok_copy = pair_copy(net, tok, T1.at[own], ps, pr, 0)
     cot_copy = pair_copy(net, cot, SA.at[own], ps, pr, 1)
@@ -520,13 +500,10 @@
     cv_in = pltpu.make_async_copy(h_cv, LRU, ls.at[11])
     tok_again = pltpu.make_async_copy(tok, PR.at[1], ls.at[12])
     block_copy = pltpu.make_async_copy(PR.at[1], o_block, ls.at[13])
-
-    if group == 1:
-        small.event(0, 0)
+    gtok_copy = pltpu.make_async_copy(gtok, o_gtok, ls.at[14])
+
     tok_copy.start()
     cot_copy.start()
-    for u in sources:
-        place[u].wait()
 
     def full(u):
         return jnp.concatenate([W[u, yy].reshape(depth, ch) for yy in range(y_size)], axis=1)
@@ -534,26 +511,37 @@
     finals = Finals(FB, o_gw, fs)
 
 
+    def pre0():
+        if group == 1:
+            lanes = small_in[...].astype(F32)
+            lanes = jnp.concatenate([lanes, jnp.zeros((16, 3 * ch - 128), F32)], axis=1)
+            pack[...] = jnp.zeros_like(pack)
+            pack[0:8, :] = pltpu.roll(lanes, dp_index * (ch // (z_size * x_size)), 1)[0:8, 0:ch]
+            spread = pltpu.roll(lanes, dp_index * part, 1)
+            for n in range(2):
+                for k in range(3):
+                    pack[8 + 3 * n + k : 9 + 3 * n + k, :] = spread[8 + n : 9 + n, k * ch : (k + 1) * ch]
+            gs[(0, *mine, slice(32, 48))] = pack[...].astype(BF)
+            for n, src in enumerate((rec_in, inp_in)):
+                for h in range(ch // 128):
+                    gs[(0, *mine, slice(16 * n, 16 * n + 16), slice(h * 128, (h + 1) * 128))] = src[h]
+        if part % 128:
+            W[(OUT, *mine)] = w_out[...]
+            W[(DN0, *mine)] = w_down[:, :ch]
+            W[(DN1, *mine)] = w_down[:, ch:]
+        else:
+            W[(OUT, *mine)] = w_out[...].T
+            W[(DN0, *mine)] = w_down[:ch, :].T
+            W[(DN1, *mine)] = w_down[ch:, :].T
     def pre1():
         place["tok"].wait()
         place["cot"].wait()
-        if group == 1:
-            small.event(0, 4)
         cot_in.wait_recv()
         transpose_into(TT, SA, SEQ)
-
-    def pre2():
         tok_in.wait_recv()
-        if group == 1:
-            small.event(0, 1)
-
-    def pre25():
-        if group == 1:
-            small.event(0, 2)
 
     def pre3():
         if group == 1:
-            small.event(0, 3)
             join_params(gs, prm, gains, sizes)
             for yy in range(y_size):
                 for n in range(2):
@@ -739,7 +727,7 @@
         out_copy.start()
 
     def bw():
-        partial_rows(mlp_out, base_own, o_gtok)
+        partial_rows(mlp_out, base_own, gtok)
 
     def gno(hook):
         out_copy.wait_recv()
@@ -747,7 +735,7 @@
         @pl.loop(0, half // F)
         def _(i):
             rows = rows_of(i, F)
-            PR[1, rows, :] = (MIX[rows, :] + o_gtok[rows, :] + PR[1, rows, :].astype(F32)).astype(BF)
+            PR[1, rows, :] = (MIX[rows, :] + gtok[rows, :] + PR[1, rows, :].astype(F32)).astype(BF)
 
         block_copy.start()
         out_copy.wait_send()
@@ -755,7 +743,7 @@
         back_copy.start()
 
     def gnw(hook):
-        partial_rows(mlp_back, base_own, o_gtok, hook)
+        partial_rows(mlp_back, base_own, gtok, hook)
 
     def norm():
         acc[...] = jnp.zeros_like(acc)
@@ -768,12 +756,12 @@
             rows = rows_of(i, T)
             at = pl.ds(pl.multiple_of(base_own + i * T, T), T)
             v = MIX[rows, :]
-            gn = o_gtok[rows, :] + PR[0, rows, :].astype(F32)
+            gn = gtok[rows, :] + PR[0, rows, :].astype(F32)
             s = lax.rsqrt(jnp.mean(v * v, axis=1, keepdims=True) + EPS)
             q = gn * gains[1:2, :]
             pgain[1:2, :] += jnp.sum(gn * v * s, axis=0, keepdims=True)
             gm = SA[at, :].astype(F32) + s * q - (s * s * s) * v * jnp.mean(q * v, axis=1, keepdims=True)
-            o_gtok[rows, :] = gm
+            gtok[rows, :] = gm
             SA[at, :] = gm.astype(BF)
 
         row_copy.start()
@@ -910,47 +898,53 @@
             s = lax.rsqrt(jnp.mean(v * v, axis=1, keepdims=True) + EPS)
             q = gn * gains[0:1, :]
             pgain[0:1, :] += jnp.sum(gn * v * s, axis=0, keepdims=True)
-            o_gtok[rows, :] += s * q - (s * s * s) * v * jnp.mean(q * v, axis=1, keepdims=True)
+            gtok[rows, :] += s * q - (s * s * s) * v * jnp.mean(q * v, axis=1, keepdims=True)
 
         gain_copy.start()
-
-    def small_step(k):
-        def fn():
-            if k == 0:
-                gain_copy.wait_recv()
-                for n in range(2):
-                    row = pgain[n : n + 1, :] + pgain[8 + n : 9 + n, :]
-                    row = jnp.concatenate([row, jnp.zeros((1, 3 * ch - depth), F32)], axis=1)
-                    for m in range(3):
-                        for yy in range(y_size):
-                            acc[yy, 8 + 3 * n + m : 9 + 3 * n + m, :] = row[:, m * ch : (m + 1) * ch]
-                if group > 1:
-                    for yy in range(y_size):
-                        o_gs[yy, 256:272, :] = acc[yy]
-                    return
-
-                @pl.loop(0, z_size)
-                def _(z):
-                    for yy in range(y_size):
-                        for xx in range(x_size):
-                            gs[0, yy, z, xx, 32:48, :] = acc[yy].astype(BF)
-
-            if group == 1:
-                back_small.event(0, k, o_gs)
-        return fn
-
-    blocks = dict(pre1=pre1, pre2=pre2, pre25=pre25, pre3=pre3, out=out, mix=mix, n2=n2, d0=d0, d1=d1, bo=bo, bw=bw, ga0=ga0,
+        gtok_copy.start()
+
+    def s0():
+        gain_copy.wait_recv()
+        for n in range(2):
+            row = pgain[n : n + 1, :] + pgain[8 + n : 9 + n, :]
+            row = jnp.concatenate([row, jnp.zeros((1, 3 * ch - depth), F32)], axis=1)
+            for m in range(3):
+                for yy in range(y_size):
+                    acc[yy, 8 + 3 * n + m : 9 + 3 * n + m, :] = row[:, m * ch : (m + 1) * ch]
+        if group > 1:
+            for yy in range(y_size):
+                o_gs[yy, 256:272, :] = acc[yy]
+            return
+
+        @pl.loop(0, z_size)
+        def _(z):
+            for yy in range(y_size):
+                for xx in range(x_size):
+                    gs[0, yy, z, xx, 32:48, :] = acc[yy].astype(BF)
+
+    blocks = dict(pre0=pre0, pre1=pre1, pre3=pre3, out=out, mix=mix, n2=n2, d0=d0, d1=d1, bo=bo, bw=bw, ga0=ga0,
                   ga1=ga1, norm=norm, up0=up0, up1=up1, outg=outg, gel=gel, rnn=rnn, gn1o=gn1o, gn1w=gn1w, heads=heads,
-                  fin=fin, s0=small_step(0), s1=small_step(1), s2=small_step(2), sr=small_step(4), s3=small_step(3))
+                  fin=fin, s0=s0)
     blocks = {name: (1, fn) for name, fn in blocks.items()}
     blocks.update(br=(tiles, branch), ffa=(SEQ // F, ff(0)), ffb=(SEQ // F, ff(1)), gh=(2 * SEQ // F, gh),
                   gno=(half // F, gno), gnw=(half // F, gnw), t=(tiles, back_rows))
 
+    placed = set()
+
     def event(chunk, k):
         if chunk < CHUNKS:
+            u = chunk // 2
+            if k == 0 and u in sources and u not in placed:
+                placed.add(u)
+                place[u].wait()
             ag.event(chunk, k)
-        else:
+        elif chunk < 2 * CHUNKS:
             back.event(chunk - CHUNKS, k, finals)
+        elif group == 1:
+            if chunk == 2 * CHUNKS:
+                small.event(0, k)
+            else:
+                back_small.event(0, k, o_gs)
 
     run_plan(PLAN, blocks, event)
     for u in (RNN, GEL):
@@ -961,6 +955,7 @@
     if group == 1:
         back_small.drain(0)
     finals.drain()
+    gtok_copy.wait()
     for cp in (tok_copy, cot_copy, row_copy, rnn_copy, gain_copy):
         cp.wait_send()
 
@@ -1053,18 +1048,18 @@
                    shape((SEQ, wide), BF)],
         in_specs=[any_spec(), any_spec(), any_spec(), any_spec(), vmem_spec(), any_spec(), any_spec(), vmem_spec(),
                   vmem_spec(), vmem_spec(), vmem_spec(), *([vmem_spec()] * 3 if group > 1 else [any_spec()] * 3)],
-        out_specs=[any_spec(), vmem_spec(), any_spec(), vmem_spec()] + [any_spec()] * 4,
+        out_specs=[any_spec(), any_spec(), any_spec(), vmem_spec()] + [any_spec()] * 4,
         scratch_shapes=[
             pltpu.VMEM((UNITS + 2, *grid, part, ch), BF), pltpu.VMEM((1, *small_grid, SMALL, ch), BF),
             pltpu.VMEM((6, SEQ, wide), BF), pltpu.VMEM((SEQ, wide), BF),
             *[pltpu.VMEM((SEQ, depth), BF)] * 4, pltpu.VMEM((rows, depth), F32),
             pltpu.VMEM((rows, depth), BF), pltpu.VMEM((2, rows, depth), BF),
-            pltpu.VMEM((2, 128, wide), F32), pltpu.VMEM((2, 136, wide), F32),
+            pltpu.VMEM((rows, depth), F32), pltpu.VMEM((2, 128, wide), F32), pltpu.VMEM((2, 136, wide), F32),
             pltpu.VMEM((2, max(part // 2, 16), ch), F32),
             pltpu.VMEM((y_size, 16, ch), F32), pltpu.VMEM((16, depth), F32), pltpu.VMEM((16, ch), F32),
             pltpu.VMEM((y_size, 16, ch), F32), pltpu.VMEM((8, depth), F32), pltpu.VMEM((2, 128, wide), BF),
             dma((CHUNKS, hops)), dma((CHUNKS, hops)), dma((CHUNKS, hops)), dma((CHUNKS, hops)),
-            dma((1, hops)), dma((1, hops)), dma((1, hops)), dma((1, hops)), dma((9,)), dma((9,)), dma((14,)), dma((3, 2)), dma((2,)),
+            dma((1, hops)), dma((1, hops)), dma((1, hops)), dma((1, hops)), dma((9,)), dma((9,)), dma((15,)), dma((3, 2)), dma((2,)),
             *[pltpu.VMEM(s, BF) for s in landed],
         ],
         compiler_params=pltpu.CompilerParams(collective_id=0, has_side_effects=True, vmem_limit_bytes=VMEM_LIMIT),

time: 239 us -> 230 us (0.962)
  Pallas kernels: 236 us -> 227 us
    pallas_call x1, Pallas kernels: 231 us -> 222 us  [body(): pl.pallas_call(functools.partial(block_kernel, sizes, group), out_shape=[...]
where the time goes in v4:
time: 230 us
  Pallas kernels  227 us (99%)
    pallas_call x1, Pallas kernels, body(): pl.pallas_call(functools.partial(block_kernel, sizes, group), out_shape=[...  222 us
    pallas_call x1, Pallas kernels, body(): pl.pallas_call(functools.partial(finish_kernel, sizes), out_shape=f_shape...  5 us

profile of v4, /device:TPU:0, one launch (start us, length us, event | category | flops | bytes accessed | tf_op | source)
XLA Modules:
  0.0 230.2 jit_solution(16659512614892916382)
XLA Ops:
  0.7 0.7 fusion.4
  1.3 0.7 concatenate.6
  2.1 0.6 fusion.1.small_in.prm_in.gains_in.hw_in
  2.7 222.4 %residual_block.1 = (bf16[512,1024]{1,0:T(8,128)(2,1)}, f32[512,1024]{1,0:T(8,128)}, f32[9,128,384]{2,1,0:T(8,128)}, f32[1,48,384]{2,1,0:T(8,128)}, bf16[6,1024,...) custom-call(bf16[512,1024]{1,0:T(8,128)(2,1)} %tok.1, ...), custom_call_target="tpu_custom_call" | custom-call | tf_op jit(solution)/shard_map/residual_block/pallas_call | solution.py:1044
  225.1 5.0 %unpack.1 = (bf16[512,1024]{1,0:T(8,128)(2,1)}, f32[512,1024]{1,0:T(8,128)}, f32[1,128]{1,0:T(1,128)}, f32[128,384]{1,0:T(8,128)}, f32[128,384]{1,0:T(8,128)}, /...) custom-call(bf16[512,1024]{1,0:T(8,128)(2,1)} %get-tuple-element.38., ...), custom_call_target="tpu_custom_call" | custom-call | tf_op jit(solution)/shard_map/unpack/pallas_call | solution.py:1085

commit v5 on v4

--- a/solution.py
+++ b/solution.py
@@ -24,26 +24,26 @@
 CHUNKS = 2 * UNITS
 SMALL = 48
 FLOW = (
-    "zxy", "zxy", "zyx", "zyx", "zxy", "yzx", "xzy", "yzx", "zyx", "zyx", "xzy", "xzy", "yxz", "zyx", "zyx", "zyx",
-    "xyz", "xzy",
+    "zxy", "zxy", "zyx", "zxy", "yzx", "zyx", "zxy", "zyx", "xyz", "xzy", "yxz", "zyx", "zxy", "yzx", "zxy", "xyz",
+    "zyx", "zxy",
 )
 BACK = (
-    "xyz", "yxz", "xyz", "yzx", "xyz", "yzx", "xzy", "zyx", "yzx", "xyz", "yxz", "xzy", "xzy", "yxz", "zyx", "xyz",
-    "zxy", "yzx",
+    "yxz", "yxz", "yxz", "xzy", "xzy", "xzy", "xzy", "yzx", "xyz", "yxz", "zyx", "xzy", "yxz", "yxz", "yxz", "zyx",
+    "xyz", "zxy",
 )
-SMALL_FLOW, SMALL_BACK = ("zxy",), ("xyz",)
+SMALL_FLOW, SMALL_BACK = ("zyx",), ("yxz",)
 PLAN = (
-    0, 45, 60, "pre0", 25, 50, 80, 35, 30, 4, "pre1", 180, 81, 1, 49, 46, 10, 184, 15, 61, 20, 2, 181, 47, 5, 24, 85,
-    55, 14, 65, 40, 19, 182, 9, 44, 11, 70, 36, 21, 41, 75, 16, 6, 12, 69, 48, 31, 39, 7, 183, 26, 66, 17, "pre3",
-    13, 79, 34, 74, 42, 8, 22, 76, 56, 29, 3, 18, 32, 86, 51, "br", "br", 27, "br", "br", 37, "br", 59, 62, "br",
-    "br", 57, "br", 43, 54, 33, 23, 28, 89, "out", 67, "mix", 77, 71, "n2", 82, 38, "ffa", 52, "ffa", 87, 64, "ffa",
-    58, "ffa", 68, "d0", 160, 72, 165, 63, 53, "ffb", 84, 78, "ffb", "ffb", "ffb", 164, "d1", 170, 175, 88, 73, 83,
-    "gh", "gh", "gh", "gh", "gh", "gh", "gh", "gh", "bo", "bw", "ga0", 120, 166, 174, 125, "ga1", "gno", 140, 145,
-    161, "gno", "gnw", "gnw", "norm", 129, "up0", 167, 130, 176, 135, "up1", 169, 141, 155, 146, "outg", "t", 150,
-    "t", "t", "t", 149, 121, 179, 110, 131, 115, "t", "t", "t", 168, 124, "t", 136, 151, "gel", 134, 105, "rnn", 100,
-    95, "gn1o", "gn1w", 142, 154, "heads", 90, 144, 111, 156, 177, 137, 106, "fin", "s0", 116, 139, 91, 185, 119,
-    109, 101, 147, 96, 126, 112, 171, 157, 143, 92, 132, 102, 148, 159, 162, 186, 152, 117, 94, 114, 97, 122, 187,
-    127, 172, 133, 104, 113, 138, 163, 158, 178, 107, 99, 128, 93, 103, 153, 173, 189, 123, 108, 118, 98, 188,
+    10, 50, 15, 40, "pre0", 51, 41, 14, 20, "pre1", 180, 75, 45, 11, 19, 16, 55, 184, 5, 76, 12, 35, 181, 65, 9, 6,
+    17, 0, 39, 30, 36, 21, 182, 59, 4, 25, 7, 1, 37, 34, 29, 80, 24, 60, 26, 13, 46, 2, 56, 64, 31, 84, 183, 18, 85,
+    38, 70, 27, "pre3", 66, 3, 74, 81, 8, 22, "br", 89, 49, 32, 42, "br", 47, 71, "br", 61, 57, 86, "br", 69, "br",
+    52, 28, "br", "br", "br", 62, 44, 23, 67, "out", 48, 77, "mix", 72, 82, "n2", 43, 33, "ffa", "ffa", "ffa", 54,
+    58, 63, 87, "ffa", "d0", 165, 160, 73, 53, 68, "ffb", "ffb", 79, "ffb", "ffb", "d1", 170, 88, 175, 169, 78, 83,
+    "gh", "gh", "gh", "gh", "gh", "gh", "gh", "gh", "bo", 161, "bw", "ga0", 120, 125, 179, "ga1", 140, "gno", "gno",
+    145, "gnw", 171, "gnw", "norm", "up0", 135, 130, 162, 144, "up1", "outg", 110, 126, "t", 150, "t", 164, "t", 121,
+    "t", 115, "t", 155, 129, 131, 136, 124, 146, 172, "t", "t", 149, 111, "t", "gel", "rnn", 90, 116, 114, 156, 105,
+    "gn1o", "gn1w", "heads", 100, 132, 119, 95, 174, "fin", "s0", 137, 157, 151, 101, 106, 134, 185, 133, 159, 147,
+    141, 139, 91, 109, 152, 112, 117, 102, 96, 154, 166, 92, 186, 148, 176, 97, 122, 142, 94, 163, 104, 113, 158,
+    173, 138, 127, 187, 107, 167, 93, 177, 99, 118, 103, 153, 123, 143, 189, 128, 108, 98, 178, 168, 188,
 )
 
 
@@ -448,9 +448,10 @@
 
 
 def block_kernel(sizes, group,
-                 tok, cot, w_rnn, w_gel, w_out, w_gate, w_up, w_down, small_in, rec_in, inp_in, prm_in, gains_in, hw_in,
-                 o_block, o_gtok, o_gw, o_gs, h_cf, h_a, h_ri, h_cv,
+                 tok, cot, w_rnn, w_gel, out_h, w_gate, w_up, down_h, taps_in, cb_in, rb_in, ib_in, dp_in, mg_in, lg_in, rec_h, inp_h, prm_in, gains_in, hw_in,
+                 o_block, o_gtok, o_gw, gs_h, h_cf, h_a, h_ri, h_cv,
                  W, gs, C6, LRU, T1, SA, N1, TT, MIX, PS, PR, gtok, AS, RS, FB, acc, pgain, pack, prm, gains, hw,
+                 w_out, w_down, rec_in, inp_in, o_gs, taps,
                  ss, rs, bss, brs, sss, srs, bsss, bsrs, ps, pr, ls, ts, fs, *landed):
     net = Net(*sizes)
     z_size, x_size, y_size = sizes
@@ -469,6 +470,9 @@
     place = {u: pltpu.make_async_copy(src, W.at[(u, *mine)], ls.at[u]) for u, src in sources.items()}
     place["tok"] = pltpu.make_async_copy(tok, T1.at[own], ls.at[OUT])
     place["cot"] = pltpu.make_async_copy(cot, SA.at[own], ls.at[DN0])
+    for n, (name, src, dst) in enumerate((("out", out_h, w_out), ("down", down_h, w_down), ("rec", rec_h, rec_in),
+                                          ("inp", inp_h, inp_in))):
+        place[name] = pltpu.make_async_copy(src, dst, ls.at[15 + n])
     for cp in place.values():
         cp.start()
     net.barrier()
@@ -501,6 +505,7 @@
     tok_again = pltpu.make_async_copy(tok, PR.at[1], ls.at[12])
     block_copy = pltpu.make_async_copy(PR.at[1], o_block, ls.at[13])
     gtok_copy = pltpu.make_async_copy(gtok, o_gtok, ls.at[14])
+    gs_copy = pltpu.make_async_copy(o_gs, gs_h, ls.at[8])
 
     tok_copy.start()
     cot_copy.start()
@@ -512,15 +517,23 @@
 
 
     def pre0():
+        for name in ("out", "down", "rec", "inp"):
+            place[name].wait()
         if group == 1:
-            lanes = small_in[...].astype(F32)
-            lanes = jnp.concatenate([lanes, jnp.zeros((16, 3 * ch - 128), F32)], axis=1)
+            width = taps_in.shape[1]
+            taps[...] = jnp.zeros_like(taps)
+            taps[0:4, 0:width] = taps_in[...].astype(F32)
+            for n, ref in enumerate((cb_in, rb_in, ib_in, dp_in)):
+                taps[4 + n : 5 + n, 0:width] = ref[...].astype(F32)
             pack[...] = jnp.zeros_like(pack)
-            pack[0:8, :] = pltpu.roll(lanes, dp_index * (ch // (z_size * x_size)), 1)[0:8, 0:ch]
-            spread = pltpu.roll(lanes, dp_index * part, 1)
+            pack[0:8, :] = pltpu.roll(taps[...], dp_index * (ch // (z_size * x_size)), 1)[0:8, 0:ch]
+            taps[...] = jnp.zeros_like(taps)
+            for n, ref in enumerate((mg_in, lg_in)):
+                taps[n : n + 1, 0:part] = ref[...].astype(F32)
+            spread = pltpu.roll(taps[...], dp_index * part, 1)
             for n in range(2):
                 for k in range(3):
-                    pack[8 + 3 * n + k : 9 + 3 * n + k, :] = spread[8 + n : 9 + n, k * ch : (k + 1) * ch]
+                    pack[8 + 3 * n + k : 9 + 3 * n + k, :] = spread[n : n + 1, k * ch : (k + 1) * ch]
             gs[(0, *mine, slice(32, 48))] = pack[...].astype(BF)
             for n, src in enumerate((rec_in, inp_in)):
                 for h in range(ch // 128):
@@ -533,6 +546,7 @@
             W[(OUT, *mine)] = w_out[...].T
             W[(DN0, *mine)] = w_down[:ch, :].T
             W[(DN1, *mine)] = w_down[ch:, :].T
+
     def pre1():
         place["tok"].wait()
         place["cot"].wait()
@@ -945,6 +959,8 @@
                 small.event(0, k)
             else:
                 back_small.event(0, k, o_gs)
+                if k == 3:
+                    gs_copy.start()
 
     run_plan(PLAN, blocks, event)
     for u in (RNN, GEL):
@@ -954,8 +970,11 @@
         back.drain(chunk)
     if group == 1:
         back_small.drain(0)
+    else:
+        gs_copy.start()
     finals.drain()
     gtok_copy.wait()
+    gs_copy.wait()
     for cp in (tok_copy, cot_copy, row_copy, rnn_copy, gain_copy):
         cp.wait_send()
 
@@ -1009,9 +1028,7 @@
     group = max(1, 16 // head_rows)
     wide = y_size * ch
     own = ch // dp
-    small_in = jnp.concatenate([conv_weight, conv_bias[None], recur_bias[None], input_bias[None], decay_param[None]], axis=0)
-    small_in = jnp.concatenate([jnp.pad(small_in, ((0, 0), (0, 128 - own))),
-                                jnp.pad(jnp.stack([mix_gain, mlp_gain]), ((0, 6), (0, 128 - part)))], axis=0)
+    vectors = [v[None] for v in (conv_bias, recur_bias, input_bias, decay_param, mix_gain, mlp_gain)]
     heads = [recur_weight, input_weight]
     out_w, down_w = out_weight, down_weight
     if part % 128:
@@ -1020,11 +1037,12 @@
     grid = (y_size, z_size, x_size)
     hops = z_size + x_size + y_size - 2
     t = lax.axis_index("tensor")
-    joined = [small_in] * 3
+    joined = [conv_weight] * 3
     if group > 1:
-        lanes = jnp.pad(small_in[0:8, :own].astype(F32), ((0, 8), (0, ch - own)))
+        lanes = jnp.concatenate([conv_weight, *vectors[0:4]], axis=0).astype(F32)
+        lanes = jnp.pad(lanes, ((0, 8), (0, ch - own)))
         lanes = jnp.roll(lanes, dp_index * own, axis=1)
-        gain = jnp.pad(jnp.stack([mix_gain, mlp_gain]).astype(F32), ((0, 6), (0, depth - part)))
+        gain = jnp.pad(jnp.concatenate(vectors[4:6], axis=0).astype(F32), ((0, 6), (0, depth - part)))
         gain = lax.psum(jnp.roll(gain, dp_index * part, axis=1), "dp")
         every = jnp.zeros((2 * y_size, 272, ch), F32)
         for n, w in enumerate(heads):
@@ -1046,9 +1064,8 @@
         out_shape=[shape((rows, depth), BF), shape((rows, depth), F32), shape((UNITS, part, ch), F32), shape(gs_out, F32),
                    shape((6, SEQ, wide), BF), shape((SEQ // 128, 128, wide), F32), shape((SEQ // 128, 136, wide), F32),
                    shape((SEQ, wide), BF)],
-        in_specs=[any_spec(), any_spec(), any_spec(), any_spec(), vmem_spec(), any_spec(), any_spec(), vmem_spec(),
-                  vmem_spec(), vmem_spec(), vmem_spec(), *([vmem_spec()] * 3 if group > 1 else [any_spec()] * 3)],
-        out_specs=[any_spec(), any_spec(), any_spec(), vmem_spec()] + [any_spec()] * 4,
+        in_specs=[*[any_spec()] * 8, *[vmem_spec()] * 7, any_spec(), any_spec(), *([vmem_spec()] * 3 if group > 1 else [any_spec()] * 3)],
+        out_specs=[any_spec()] * 8,
         scratch_shapes=[
             pltpu.VMEM((UNITS + 2, *grid, part, ch), BF), pltpu.VMEM((1, *small_grid, SMALL, ch), BF),
             pltpu.VMEM((6, SEQ, wide), BF), pltpu.VMEM((SEQ, wide), BF),
@@ -1058,13 +1075,16 @@
             pltpu.VMEM((2, max(part // 2, 16), ch), F32),
             pltpu.VMEM((y_size, 16, ch), F32), pltpu.VMEM((16, depth), F32), pltpu.VMEM((16, ch), F32),
             pltpu.VMEM((y_size, 16, ch), F32), pltpu.VMEM((8, depth), F32), pltpu.VMEM((2, 128, wide), BF),
+            pltpu.VMEM(out_w.shape, BF), pltpu.VMEM(down_w.shape, BF), pltpu.VMEM(heads[0].shape, BF),
+            pltpu.VMEM(heads[1].shape, BF), pltpu.VMEM(gs_out, F32), pltpu.VMEM((8, 3 * ch), F32),
             dma((CHUNKS, hops)), dma((CHUNKS, hops)), dma((CHUNKS, hops)), dma((CHUNKS, hops)),
-            dma((1, hops)), dma((1, hops)), dma((1, hops)), dma((1, hops)), dma((9,)), dma((9,)), dma((15,)), dma((3, 2)), dma((2,)),
+            dma((1, hops)), dma((1, hops)), dma((1, hops)), dma((1, hops)), dma((9,)), dma((9,)), dma((19,)), dma((3, 2)), dma((2,)),
             *[pltpu.VMEM(s, BF) for s in landed],
         ],
         compiler_params=pltpu.CompilerParams(collective_id=0, has_side_effects=True, vmem_limit_bytes=VMEM_LIMIT),
         name="residual_block",
-    )(tokens, cotangent, rnn_weight, gelu_weight, out_w, gate_weight, up_weight, down_w, small_in, *heads, *joined)[:4]
+    )(tokens, cotangent, rnn_weight, gelu_weight, out_w, gate_weight, up_weight, down_w, conv_weight, *vectors, *heads,
+      *joined)[:4]
     if group > 1:
         every = jnp.zeros((2 * y_size, 272, ch), F32)
         for yy in range(y_size):

time: 230 us -> 225 us (0.978)
  Pallas kernels: 227 us -> 224 us
    pallas_call x1, Pallas kernels: 222 us -> 219 us  [body(): pl.pallas_call(functools.partial(block_kernel, sizes, group), out_shape=[...]
where the time goes in v5:
time: 225 us
  Pallas kernels  224 us (100%)
    pallas_call x1, Pallas kernels, body(): pl.pallas_call(functools.partial(block_kernel, sizes, group), out_shape=[...  219 us
    pallas_call x1, Pallas kernels, body(): pl.pallas_call(functools.partial(finish_kernel, sizes), out_shape=f_shape...  5 us

profile of v5, /device:TPU:0, one launch (start us, length us, event | category | flops | bytes accessed | tf_op | source)
XLA Modules:
  0.0 225.1 jit_solution(8744664198456957594)
XLA Ops:
  0.7 219.3 %residual_block.1 = (bf16[512,1024]{1,0:T(8,128)(2,1)}, f32[512,1024]{1,0:T(8,128)}, f32[9,128,384]{2,1,0:T(8,128)}, f32[1,48,384]{2,1,0:T(8,128)}, bf16[6,1024,...) custom-call(bf16[512,1024]{1,0:T(8,128)(2,1)} %tok.1, ...), custom_call_target="tpu_custom_call" | custom-call | tf_op jit(solution)/shard_map/residual_block/pallas_call | solution.py:1062
  220.0 5.0 %unpack.1 = (bf16[512,1024]{1,0:T(8,128)(2,1)}, f32[512,1024]{1,0:T(8,128)}, f32[1,128]{1,0:T(1,128)}, f32[128,384]{1,0:T(8,128)}, f32[128,384]{1,0:T(8,128)}, /...) custom-call(bf16[512,1024]{1,0:T(8,128)(2,1)} %get-tuple-element.38., ...), custom_call_target="tpu_custom_call" | custom-call | tf_op jit(solution)/shard_map/unpack/pallas_call | solution.py:1105

commit v6 on v5

--- a/solution.py
+++ b/solution.py
@@ -22,7 +22,7 @@
 UNITS = 9
 GATE, UP, DOWN = (GA0, GA1), (UP0, UP1), (DN0, DN1)
 CHUNKS = 2 * UNITS
-SMALL = 48
+SMALL = 32
 FLOW = (
     "zxy", "zxy", "zyx", "zxy", "yzx", "zyx", "zxy", "zyx", "xyz", "xzy", "yxz", "zyx", "zxy", "yzx", "zxy", "xyz",
     "zyx", "zxy",
@@ -238,14 +238,30 @@
     return pl.ds(pl.multiple_of(i * n, n), n)
 
 
-def join_params(gs, prm, gains, sizes):
-    y_size = sizes[2]
+def join_params(gp, prm, gains, sizes):
+    z_size, x_size, y_size = sizes
+    ch = prm.shape[2]
+    own = ch // (z_size * x_size)
+    lane = lax.broadcasted_iota(jnp.int32, (8, 128), 1)
     for yy in range(y_size):
-        prm[yy] = jnp.sum(gs[0, yy, :, :, 32:48, :].astype(F32), axis=(0, 1))
-    d = gains.shape[1]
-    for n in range(2):
-        row = jnp.concatenate([prm[0, 8 + 3 * n + k : 9 + 3 * n + k, :] for k in range(3)], axis=1)
-        gains[n : n + 1, :] = row[:, :d]
+        total = jnp.zeros((8, ch), F32)
+        for i in range(z_size * x_size):
+            block = gp[0, yy, i // x_size, i % x_size]
+            row = jnp.concatenate([jnp.where(lane < own, block, 0.0), jnp.zeros((8, ch - 128), F32)], axis=1)
+            total = total + (pltpu.roll(row, i * own, 1) if i else row)
+        prm[yy] = jnp.concatenate([total, jnp.zeros((8, ch), F32)], axis=0)
+    for i in range(z_size * x_size):
+        block = gp[0, 0, i // x_size, i % x_size]
+        turned = pltpu.roll(block, 64, 1)
+        for n in range(2):
+            gains[n : n + 1, i * 128 : (i + 1) * 128] = jnp.where(
+                lane[0:1] < 64, turned[2 * n : 2 * n + 1], block[2 * n + 1 : 2 * n + 2])
+
+
+def put_gain(block, n, row):
+    turned = pltpu.roll(jnp.broadcast_to(row, (8, 128)), 64, 1)
+    block[2 * n : 2 * n + 1, 64:128] = turned[0:1, 64:128]
+    block[2 * n + 1 : 2 * n + 2, 64:128] = row[:, 64:128]
 
 
 def head_weight(gs, yy, first):
@@ -329,7 +345,7 @@
                     place = {**place, "z": owner}
                     idx = (self.slot(c), *[place[e] if e in place else self.net.at[e] for e in "yzx"], rows)
                     got = buf[(3, *[place[e] for e in "yzx" if e in rest])]
-                    self.ref[idx] = (self.ref[idx].astype(F32) + got.astype(F32)).astype(BF)
+                    self.ref[idx] = (self.ref[idx].astype(F32) + got.astype(F32)).astype(self.ref.dtype)
 
                 self.over(rest, block, {})
                 self.copy(c, s, 2).start()
@@ -338,7 +354,7 @@
         def end(unused):
             def fn():
                 def block(place):
-                    buf[(unused, *[place[e] for e in "yzx" if e in rest])] = jnp.zeros(buf.shape[-2:], BF)
+                    buf[(unused, *[place[e] for e in "yzx" if e in rest])] = jnp.zeros(buf.shape[-2:], buf.dtype)
 
                 self.over(rest, block, {})
             return fn
@@ -367,7 +383,7 @@
             for j in self.hops(c, s):
                 total = total + buf[(j - 1, *[place[e] for e in "yzx" if e in place])].astype(F32)
             if s < 2:
-                self.ref[idx] = total.astype(BF)
+                self.ref[idx] = total.astype(self.ref.dtype)
             elif self.halves:
                 out.put(c // 2, rows, total)
             else:
@@ -426,6 +442,10 @@
     return landing(SMALL_BACK, sizes, lambda c: SMALL, ch)
 
 
+def params_landing(sizes):
+    return landing(SMALL_BACK, sizes, lambda c: 8, 128)
+
+
 class Finals:
     def __init__(self, ref, out, sem):
         self.ref, self.out, self.sem, self.copies = ref, out, sem, []
@@ -449,10 +469,10 @@
 
 def block_kernel(sizes, group,
                  tok, cot, w_rnn, w_gel, out_h, w_gate, w_up, down_h, taps_in, cb_in, rb_in, ib_in, dp_in, mg_in, lg_in, rec_h, inp_h, prm_in, gains_in, hw_in,
-                 o_block, o_gtok, o_gw, gs_h, h_cf, h_a, h_ri, h_cv,
-                 W, gs, C6, LRU, T1, SA, N1, TT, MIX, PS, PR, gtok, AS, RS, FB, acc, pgain, pack, prm, gains, hw,
-                 w_out, w_down, rec_in, inp_in, o_gs, taps,
-                 ss, rs, bss, brs, sss, srs, bsss, bsrs, ps, pr, ls, ts, fs, *landed):
+                 o_block, o_gtok, o_gw, gs_h, gp_h, h_cf, h_a, h_ri, h_cv,
+                 W, gs, C6, LRU, T1, SA, N1, TT, MIX, PS, PR, gtok, AS, RS, FB, acc, pgain, prm, gains, hw,
+                 w_out, w_down, rec_in, inp_in, o_gs, o_gp, taps, gp,
+                 ss, rs, bss, brs, sss, srs, bsss, bsrs, pss, prs, bpss, bprs, ps, pr, ls, ts, fs, *landed):
     net = Net(*sizes)
     z_size, x_size, y_size = sizes
     c = net.at["c"]
@@ -480,10 +500,12 @@
     ag = Gather(net, W, FLOW, ss, rs, True)
     shapes = big_landing(sizes, part, ch)
     back = Scatter(net, W, BACK, dict(zip(shapes, landed)), bss, brs, True)
-    small = back_small = None
+    small = back_small = params = back_params = None
     if group == 1:
         small = Gather(net, gs, SMALL_FLOW, sss, srs, False)
         tail = landed[len(shapes):]
+        params = Gather(net, gp, SMALL_FLOW, pss, prs, False)
+        back_params = Scatter(net, gp, SMALL_BACK, dict(zip(params_landing(sizes), tail[3:])), bpss, bprs, False)
         back_small = Scatter(net, gs, SMALL_BACK, dict(zip(small_landing(sizes, ch), tail)), bsss, bsrs, False)
 
     tok_copy = pair_copy(net, tok, T1.at[own], ps, pr, 0)
@@ -506,6 +528,7 @@
     block_copy = pltpu.make_async_copy(PR.at[1], o_block, ls.at[13])
     gtok_copy = pltpu.make_async_copy(gtok, o_gtok, ls.at[14])
     gs_copy = pltpu.make_async_copy(o_gs, gs_h, ls.at[8])
+    gp_copy = pltpu.make_async_copy(o_gp, gp_h, ls.at[19])
 
     tok_copy.start()
     cot_copy.start()
@@ -525,16 +548,9 @@
             taps[0:4, 0:width] = taps_in[...].astype(F32)
             for n, ref in enumerate((cb_in, rb_in, ib_in, dp_in)):
                 taps[4 + n : 5 + n, 0:width] = ref[...].astype(F32)
-            pack[...] = jnp.zeros_like(pack)
-            pack[0:8, :] = pltpu.roll(taps[...], dp_index * (ch // (z_size * x_size)), 1)[0:8, 0:ch]
-            taps[...] = jnp.zeros_like(taps)
             for n, ref in enumerate((mg_in, lg_in)):
-                taps[n : n + 1, 0:part] = ref[...].astype(F32)
-            spread = pltpu.roll(taps[...], dp_index * part, 1)
-            for n in range(2):
-                for k in range(3):
-                    pack[8 + 3 * n + k : 9 + 3 * n + k, :] = spread[n : n + 1, k * ch : (k + 1) * ch]
-            gs[(0, *mine, slice(32, 48))] = pack[...].astype(BF)
+                put_gain(taps, n, ref[...].astype(F32))
+            gp[(0, *mine)] = taps[...]
             for n, src in enumerate((rec_in, inp_in)):
                 for h in range(ch // 128):
                     gs[(0, *mine, slice(16 * n, 16 * n + 16), slice(h * 128, (h + 1) * 128))] = src[h]
@@ -556,7 +572,7 @@
 
     def pre3():
         if group == 1:
-            join_params(gs, prm, gains, sizes)
+            join_params(gp, prm, gains, sizes)
             for yy in range(y_size):
                 for n in range(2):
                     hw[n, :, yy * ch : (yy + 1) * ch] = head_weight(gs, yy, 16 * n)
@@ -886,6 +902,7 @@
         cv_in.wait()
         if group == 1:
             small.drain(0)
+            params.drain(0)
         for yy in range(y_size):
             acc[yy, 7:8] = acc[yy, 7:8] * jax.nn.sigmoid(prm[yy, 7:8])
             for h in range(ch // 128):
@@ -919,22 +936,25 @@
 
     def s0():
         gain_copy.wait_recv()
-        for n in range(2):
-            row = pgain[n : n + 1, :] + pgain[8 + n : 9 + n, :]
-            row = jnp.concatenate([row, jnp.zeros((1, 3 * ch - depth), F32)], axis=1)
-            for m in range(3):
-                for yy in range(y_size):
-                    acc[yy, 8 + 3 * n + m : 9 + 3 * n + m, :] = row[:, m * ch : (m + 1) * ch]
+        rows = [pgain[n : n + 1, :] + pgain[8 + n : 9 + n, :] for n in range(2)]
         if group > 1:
+            for n in range(2):
+                row = jnp.concatenate([rows[n], jnp.zeros((1, 3 * ch - depth), F32)], axis=1)
+                for m in range(3):
+                    for yy in range(y_size):
+                        acc[yy, 8 + 3 * n + m : 9 + 3 * n + m, :] = row[:, m * ch : (m + 1) * ch]
             for yy in range(y_size):
                 o_gs[yy, 256:272, :] = acc[yy]
             return
-
-        @pl.loop(0, z_size)
-        def _(z):
+        own_lanes = ch // (z_size * x_size)
+        lane = lax.broadcasted_iota(jnp.int32, (8, 128), 1)
+        for i in range(z_size * x_size):
             for yy in range(y_size):
-                for xx in range(x_size):
-                    gs[0, yy, z, xx, 32:48, :] = acc[yy].astype(BF)
+                turned = pltpu.roll(acc[yy, 0:8, :], (ch - i * own_lanes) % ch, 1)[:, 0:128] if i else acc[yy, 0:8, 0:128]
+                taps[...] = jnp.where(lane < own_lanes, turned, 0.0)
+                for n in range(2):
+                    put_gain(taps, n, rows[n][:, i * 128 : (i + 1) * 128])
+                gp[0, yy, i // x_size, i % x_size] = taps[...]
 
     blocks = dict(pre0=pre0, pre1=pre1, pre3=pre3, out=out, mix=mix, n2=n2, d0=d0, d1=d1, bo=bo, bw=bw, ga0=ga0,
                   ga1=ga1, norm=norm, up0=up0, up1=up1, outg=outg, gel=gel, rnn=rnn, gn1o=gn1o, gn1w=gn1w, heads=heads,
@@ -957,10 +977,13 @@
         elif group == 1:
             if chunk == 2 * CHUNKS:
                 small.event(0, k)
+                params.event(0, k)
             else:
                 back_small.event(0, k, o_gs)
+                back_params.event(0, k, o_gp)
                 if k == 3:
                     gs_copy.start()
+                    gp_copy.start()
 
     run_plan(PLAN, blocks, event)
     for u in (RNN, GEL):
@@ -970,6 +993,8 @@
         back.drain(chunk)
     if group == 1:
         back_small.drain(0)
+        back_params.drain(0)
+        gp_copy.wait()
     else:
         gs_copy.start()
     finals.drain()
@@ -979,13 +1004,11 @@
         cp.wait_send()
 
 
-def finish_kernel(sizes, block_in, gtok_in, gw, gs,
+def finish_kernel(block_in, gtok_in, gw, gs, gp,
                   o_block, o_gtok, o_mg, o_rnn, o_gel, o_cw, o_cb, o_rw, o_iw, o_rb, o_ib, o_dp, o_out, o_lg, o_gate, o_up,
                   o_down):
     ch = gw.shape[2]
-    dp = sizes[0] * sizes[1]
-    part, own = o_mg.shape[1], ch // dp
-    dp_index = lax.axis_index("dp")
+    part, own = o_mg.shape[1], o_cb.shape[1]
     o_block[...] = block_in[...]
     o_gtok[...] = gtok_in[...]
     o_rnn[...] = gw[RNN]
@@ -999,14 +1022,14 @@
     for h in range(ch // 128):
         o_rw[h] = gs[0, 0:16, h * 128 : (h + 1) * 128]
         o_iw[h] = gs[0, 16:32, h * 128 : (h + 1) * 128]
-    rows = pltpu.roll(gs[0, 32:40, :], ch - dp_index * own, 1)
-    o_cw[...] = rows[0:4, 0:own]
+    block = gp[0]
+    o_cw[...] = block[0:4, 0:own]
     for k, ref in ((4, o_cb), (5, o_rb), (6, o_ib), (7, o_dp)):
-        ref[...] = rows[k : k + 1, 0:own]
+        ref[...] = block[k : k + 1, 0:own]
+    turned = pltpu.roll(block, 64, 1)
+    lane = lax.broadcasted_iota(jnp.int32, (1, 128), 1)
     for n, ref in ((0, o_mg), (1, o_lg)):
-        row = jnp.concatenate([gs[0, 40 + 3 * n + k : 41 + 3 * n + k, :] for k in range(3)], axis=1)
-        row = jnp.broadcast_to(row, (8, 3 * ch))
-        ref[...] = pltpu.roll(row, 3 * ch - dp_index * part, 1)[0:1, 0:part]
+        ref[...] = jnp.where(lane < 64, turned[2 * n : 2 * n + 1], block[2 * n + 1 : 2 * n + 2])[:, 0:part]
 
 
 def any_spec():
@@ -1055,17 +1078,20 @@
         heads = [jnp.zeros((ch // 128, 16, 128), BF)] * 2
     dma = pltpu.SemaphoreType.DMA
     landed = list(big_landing(sizes, part, ch).values())
+    landed_params = []
     gs_out, small_grid = (y_size, 272, ch), (1, 1, 1)
     if group == 1:
         landed += list(small_landing(sizes, ch).values())
+        landed_params = list(params_landing(sizes).values())
         gs_out, small_grid = (1, SMALL, ch), grid
-    block_out, grad_tokens, gw, gs = pl.pallas_call(
+    block_out, grad_tokens, gw, gs, gp = pl.pallas_call(
         functools.partial(block_kernel, sizes, group),
         out_shape=[shape((rows, depth), BF), shape((rows, depth), F32), shape((UNITS, part, ch), F32), shape(gs_out, F32),
+                   shape((1, 8, 128), F32),
                    shape((6, SEQ, wide), BF), shape((SEQ // 128, 128, wide), F32), shape((SEQ // 128, 136, wide), F32),
                    shape((SEQ, wide), BF)],
         in_specs=[*[any_spec()] * 8, *[vmem_spec()] * 7, any_spec(), any_spec(), *([vmem_spec()] * 3 if group > 1 else [any_spec()] * 3)],
-        out_specs=[any_spec()] * 8,
+        out_specs=[any_spec()] * 9,
         scratch_shapes=[
             pltpu.VMEM((UNITS + 2, *grid, part, ch), BF), pltpu.VMEM((1, *small_grid, SMALL, ch), BF),
             pltpu.VMEM((6, SEQ, wide), BF), pltpu.VMEM((SEQ, wide), BF),
@@ -1073,18 +1099,19 @@
             pltpu.VMEM((rows, depth), BF), pltpu.VMEM((2, rows, depth), BF),
             pltpu.VMEM((rows, depth), F32), pltpu.VMEM((2, 128, wide), F32), pltpu.VMEM((2, 136, wide), F32),
             pltpu.VMEM((2, max(part // 2, 16), ch), F32),
-            pltpu.VMEM((y_size, 16, ch), F32), pltpu.VMEM((16, depth), F32), pltpu.VMEM((16, ch), F32),
+            pltpu.VMEM((y_size, 16, ch), F32), pltpu.VMEM((16, depth), F32),
             pltpu.VMEM((y_size, 16, ch), F32), pltpu.VMEM((8, depth), F32), pltpu.VMEM((2, 128, wide), BF),
             pltpu.VMEM(out_w.shape, BF), pltpu.VMEM(down_w.shape, BF), pltpu.VMEM(heads[0].shape, BF),
-            pltpu.VMEM(heads[1].shape, BF), pltpu.VMEM(gs_out, F32), pltpu.VMEM((8, 3 * ch), F32),
+            pltpu.VMEM(heads[1].shape, BF), pltpu.VMEM(gs_out, F32), pltpu.VMEM((1, 8, 128), F32),
+            pltpu.VMEM((8, 128), F32), pltpu.VMEM((1, *small_grid, 8, 128), F32),
             dma((CHUNKS, hops)), dma((CHUNKS, hops)), dma((CHUNKS, hops)), dma((CHUNKS, hops)),
-            dma((1, hops)), dma((1, hops)), dma((1, hops)), dma((1, hops)), dma((9,)), dma((9,)), dma((19,)), dma((3, 2)), dma((2,)),
-            *[pltpu.VMEM(s, BF) for s in landed],
+            *[dma((1, hops))] * 8, dma((9,)), dma((9,)), dma((20,)), dma((3, 2)), dma((2,)),
+            *[pltpu.VMEM(s, BF) for s in landed], *[pltpu.VMEM(s, F32) for s in landed_params],
         ],
         compiler_params=pltpu.CompilerParams(collective_id=0, has_side_effects=True, vmem_limit_bytes=VMEM_LIMIT),
         name="residual_block",
     )(tokens, cotangent, rnn_weight, gelu_weight, out_w, gate_weight, up_weight, down_w, conv_weight, *vectors, *heads,
-      *joined)[:4]
+      *joined)[:5]
     if group > 1:
         every = jnp.zeros((2 * y_size, 272, ch), F32)
         for yy in range(y_size):
@@ -1094,7 +1121,10 @@
         rec = lax.dynamic_slice(gs[0], (first, 0), (head_rows, ch))
         inp = lax.dynamic_slice(gs[0], (128 + first, 0), (head_rows, ch))
         fill = jnp.zeros((16 - head_rows, ch), F32)
-        gs = jnp.concatenate([rec, fill, inp, fill, gs[0, 256:]], axis=0)[None]
+        par = lax.dynamic_slice(gs[0, 256:264], (0, dp_index * own), (8, own))
+        gain = lax.dynamic_slice(gs[0, 264:270].reshape(2, 3 * ch), (0, dp_index * part), (2, part))
+        gp = jnp.zeros((1, 8, 128), F32).at[0, :, :own].set(par).at[0, 0:4:2, 64 : 64 + part].set(gain)
+        gs = jnp.concatenate([rec, fill, inp, fill], axis=0)[None]
     f_shapes = [
         shape((rows, depth), BF), shape((rows, depth), F32), shape((1, part), F32), shape((part, ch), F32),
         shape((part, ch), F32), shape((4, own), F32), shape((1, own), F32), shape((ch // 128, 16, 128), F32),
@@ -1103,13 +1133,13 @@
         shape((2 * ch, part), F32),
     ]
     res = list(pl.pallas_call(
-        functools.partial(finish_kernel, sizes),
+        finish_kernel,
         out_shape=f_shapes,
-        in_specs=[vmem_spec()] * 4,
+        in_specs=[vmem_spec()] * 5,
         out_specs=[vmem_spec()] * 17,
         compiler_params=pltpu.CompilerParams(vmem_limit_bytes=VMEM_LIMIT),
         name="unpack",
-    )(block_out, grad_tokens, gw, gs))
+    )(block_out, grad_tokens, gw, gs, gp))
     for k in (2, 6, 9, 10, 11, 13):
         res[k] = res[k][0]
     for k in (7, 8):

time: 225 us -> 223 us (level)
    pallas_call x1, Pallas kernels: 219 us -> 217 us  [body(): pl.pallas_call(functools.partial(block_kernel, sizes, group), out_shape=[...]
where the time goes in v6:
time: 223 us
  Pallas kernels  222 us (100%)
    pallas_call x1, Pallas kernels, body(): pl.pallas_call(functools.partial(block_kernel, sizes, group), out_shape=[...  217 us
    pallas_call x1, Pallas kernels, body(): pl.pallas_call(finish_kernel, out_shape=f_shapes, in_specs=[vmem_spec()]...  5 us

profile of v6, /device:TPU:0, one launch (start us, length us, event | category | flops | bytes accessed | tf_op | source)
XLA Modules:
  0.0 222.8 jit_solution(4961777411983028717)
XLA Ops:
  0.7 217.0 %residual_block.1 = (bf16[512,1024]{1,0:T(8,128)(2,1)}, f32[512,1024]{1,0:T(8,128)}, f32[9,128,384]{2,1,0:T(8,128)}, f32[1,32,384]{2,1,0:T(8,128)}, f32[1,8,128]...) custom-call(bf16[512,1024]{1,0:T(8,128)(2,1)} %tok.1, ...), custom_call_target="tpu_custom_call" | custom-call | tf_op jit(solution)/shard_map/residual_block/pallas_call | solution.py:1087
  217.7 5.0 %unpack.1 = (bf16[512,1024]{1,0:T(8,128)(2,1)}, f32[512,1024]{1,0:T(8,128)}, f32[1,128]{1,0:T(1,128)}, f32[128,384]{1,0:T(8,128)}, f32[128,384]{1,0:T(8,128)}, /...) custom-call(bf16[512,1024]{1,0:T(8,128)(2,1)} %get-tuple-element.39., ...), custom_call_target="tpu_custom_call" | custom-call | tf_op jit(solution)/shard_map/unpack/pallas_call | solution.py:1135

commit v7 on v6

--- a/solution.py
+++ b/solution.py
@@ -403,6 +403,8 @@
             self.add(c, k - 1, out)
         if k < 3:
             self.sends(c, k, lambda cp: cp.start())
+        else:
+            self.drain(c)
 
     def drain(self, c):
         if self.rows(c) is None:
@@ -989,11 +991,7 @@
     for u in (RNN, GEL):
         for chunk in (2 * u, 2 * u + 1):
             ag.drain(chunk)
-    for chunk in range(CHUNKS):
-        back.drain(chunk)
     if group == 1:
-        back_small.drain(0)
-        back_params.drain(0)
         gp_copy.wait()
     else:
         gs_copy.start()

time: 223 us -> 223 us (level)
  no operation moved by 1% of the time
where the time goes in v7:
time: 223 us
  Pallas kernels  222 us (100%)
    pallas_call x1, Pallas kernels, body(): pl.pallas_call(functools.partial(block_kernel, sizes, group), out_shape=[...  217 us
    pallas_call x1, Pallas kernels, body(): pl.pallas_call(finish_kernel, out_shape=f_shapes, in_specs=[vmem_spec()]...  5 us

profile of v7, /device:TPU:0, one launch (start us, length us, event | category | flops | bytes accessed | tf_op | source)
XLA Modules:
  0.0 222.8 jit_solution(6689759459597390030)
XLA Ops:
  0.7 217.0 %residual_block.1 = (bf16[512,1024]{1,0:T(8,128)(2,1)}, f32[512,1024]{1,0:T(8,128)}, f32[9,128,384]{2,1,0:T(8,128)}, f32[1,32,384]{2,1,0:T(8,128)}, f32[1,8,128]...) custom-call(bf16[512,1024]{1,0:T(8,128)(2,1)} %tok.1, ...), custom_call_target="tpu_custom_call" | custom-call | tf_op jit(solution)/shard_map/residual_block/pallas_call | solution.py:1085
  217.7 5.0 %unpack.1 = (bf16[512,1024]{1,0:T(8,128)(2,1)}, f32[512,1024]{1,0:T(8,128)}, f32[1,128]{1,0:T(1,128)}, f32[128,384]{1,0:T(8,128)}, f32[128,384]{1,0:T(8,128)}, /...) custom-call(bf16[512,1024]{1,0:T(8,128)(2,1)} %get-tuple-element.39., ...), custom_call_target="tpu_custom_call" | custom-call | tf_op jit(solution)/shard_map/unpack/pallas_call | solution.py:1133
